TPU v7x, 32 devices: a whole 2x2x4 slice. The times are simulated.
32 devices in a mesh: grp: 4 (over y, x), seq: 8 (over z, core).
Axes of the slice: x: 2, y: 2, z: 4, core: 2. Of those that a mesh axis runs over, the one named last changes fastest.
Arguments:
- tokens: bfloat16 [12288, 1024], P(('grp', 'seq')), may hold values from -6 to 6
- cotangent: bfloat16 [12288, 1024], P(('grp', 'seq')), may hold values from -6 to 6
- master: float32 [24, 1024, 1024], P('grp', 'seq')
- first_moment: float32 [24, 1024, 1024], P('grp', 'seq')
- second_moment: float32 [24, 1024, 1024], P('grp', 'seq')
- norm_params: float32 [4, 1024], replicated
- norm_first: float32 [4, 1024], replicated
- norm_second: float32 [4, 1024], replicated
- seg_valid: int32 [4, 6], replicated, may hold values from 0 to 512, as said below
- book_of_group: int32 [4], replicated, may hold values from 0 to 3, each once
- panel_slot: int32 [15], replicated, may hold values from 0 to 23, as said below
Outputs:
- mixed: bfloat16 [12288, 1024], P(('grp', 'seq'))
- input_grad: float32 [12288, 1024], P(('grp', 'seq'))
- slot_grad: float32 [24, 1024, 1024], P('grp', 'seq')
- slot_first: float32 [24, 1024, 1024], P('grp', 'seq')
- slot_second: float32 [24, 1024, 1024], P('grp', 'seq')
- slot_weight: float32 [24, 1024, 1024], P('grp', 'seq')
- norm_grad: float32 [4, 1024], replicated
- norm_first_new: float32 [4, 1024], replicated
- norm_second_new: float32 [2, 1024], replicated
- norm_second_after: float32 [2, 1024], replicated
- norm_weight: float32 [4, 1024], replicated
Inputs may be any that keep to these rules, and one draw needn't show every extreme that they name: `seg_valid`: each book has 512 valid positions in every segment but its last, which holds more than 512 - min(512, 384) valid positions; one book fills all 6 segments. `panel_slot`: all values differ; at most 6 panels fall in the slots of one group, and one group holds exactly 6.
All inputs are finite; a program needn't handle non-finite values.
Results may differ from a plain program's by a relative error of at most 0.024.
Values may be sent and summed in bfloat16 or wider, within the bound.
A program may use at most 512 MiB of HBM per device.

v0:
```python
import jax
import jax.numpy as jnp
from jax import lax
from jax.sharding import PartitionSpec as P

D = 1024
HEADS = 8
HEAD_DIM = 128
FF = 4096
S = 512
CM = 512
STEP = 10


NEG_SCORE = -1e30
FAR_INDEX = 1 << 30
NORM_EPS = 1e-05
BETA_ONE = 0.9
BETA_TWO = 0.999
WEIGHT_DECAY = 0.1
ADAM_EPS = 1e-08
NORM_RATE = 1.0
SLOT_RATE = 2.0


def layer_norm(values, gain, shift):
    row_mean = jnp.mean(values, axis=-1, keepdims=True)
    centered = values - row_mean
    variance = jnp.mean(centered * centered, axis=-1, keepdims=True)
    return centered * lax.rsqrt(variance + NORM_EPS) * gain + shift


def panel_deviations():
    inner_dev = D ** (-0.5)
    hidden_ratio = FF // D
    deviations = [inner_dev] * 3 + [(D // (2 * S)) ** (-0.5)] + [inner_dev] * hidden_ratio
    deviations = deviations + [FF ** (-0.5)] * hidden_ratio + [(3 * D) ** (-0.5)] * 3
    return jnp.array(deviations, jnp.float32)


def adam_update(gradient, first_old, second_old, weight_old, step_rate):
    first_new = BETA_ONE * first_old + (1.0 - BETA_ONE) * gradient
    second_new = BETA_TWO * second_old + (1.0 - BETA_TWO) * gradient * gradient
    fix_one = 1.0 - BETA_ONE**STEP
    fix_two = 1.0 - BETA_TWO**STEP
    movement = first_new / fix_one / (jnp.sqrt(second_new / fix_two) + ADAM_EPS)
    return (first_new, second_new, weight_old - step_rate * (movement + WEIGHT_DECAY * weight_old))


def matmul(left, right):
    return jnp.dot(left, right, preferred_element_type=jnp.float32)


def times_transposed(left, right):
    return lax.dot_general(
        left, right, (((1,), (1,)), ((), ())), preferred_element_type=jnp.float32
    )


def contract_rows(left, right):
    return lax.dot_general(
        left, right, (((0,), (0,)), ((), ())), preferred_element_type=jnp.float32
    )


def key_marks(source, tok_dev, comp_slots):
    anchor = source * tok_dev
    raw_mark = jnp.where(source >= 0, anchor + jnp.arange(tok_dev, dtype=jnp.int32), -FAR_INDEX)
    comp_index = anchor // 3 + jnp.arange(comp_slots, dtype=jnp.int32)
    return (raw_mark, jnp.where(source >= 0, comp_index, -FAR_INDEX))


def allowed_keys(positions, raw_mark, comp_mark):
    memory_start = (positions // S - 1) * S
    comp_end = jnp.floor_divide(memory_start, 3)
    comp_start = jnp.maximum(comp_end - CM, 0)
    raw_ok = (
        (raw_mark[None, :] >= memory_start[:, None])
        & (raw_mark[None, :] <= positions[:, None])
        & (raw_mark[None, :] >= 0)
    )
    comp_ok = (comp_mark[None, :] >= comp_start[:, None]) & (comp_mark[None, :] < comp_end[:, None])
    return jnp.concatenate([raw_ok, comp_ok], 1)


def local(
    tokens,
    cotangent,
    master,
    first_moment,
    second_moment,
    norm_params,
    norm_first,
    norm_second,
    seg_valid,
    book_of_group,
    panel_slot,
):
    seq_count = lax.axis_size("seq")
    group_count = lax.axis_size("grp")
    seq_index = lax.axis_index("seq")
    group_index = lax.axis_index("grp")
    tok_dev = tokens.shape[0]
    model_width = tokens.shape[1]
    slot_count = master.shape[0]
    comp_slots = tok_dev // 3
    key_rows = tok_dev + comp_slots
    hidden_ratio = FF // D
    score_scale = HEAD_DIM ** (-0.5)
    key_devs = min((2 * S + 3 * CM + tok_dev) // tok_dev + 1, seq_count)
    all_slots = slot_count * group_count
    owner_onehot = (panel_slot[None, :] == jnp.arange(all_slots, dtype=jnp.int32)[:, None]).astype(
        jnp.float32
    )
    owner_scaled = owner_onehot * panel_deviations()[None, :]
    slot_scale = lax.dynamic_slice_in_dim(
        jnp.sum(owner_scaled, 1), group_index * slot_count, slot_count, 0
    )

    def fetch_weights():
        scaled = (master * slot_scale[:, None, None]).astype(jnp.bfloat16)
        local_rows = lax.all_gather(scaled, "seq", axis=1, tiled=True)
        gathered = lax.all_gather(local_rows, "grp", axis=0, tiled=True)

        def select_panel(panel_index):
            return lax.dynamic_index_in_dim(gathered, panel_slot[panel_index], 0, keepdims=False)

        return (
            select_panel(0),
            select_panel(1),
            select_panel(2),
            select_panel(3),
            jnp.concatenate(
                [select_panel(4 + piece_index) for piece_index in range(hidden_ratio)], 0
            ),
            jnp.concatenate(
                [
                    select_panel(4 + hidden_ratio + piece_index)
                    for piece_index in range(hidden_ratio)
                ],
                0,
            ),
            jnp.stack(
                [select_panel(4 + 2 * hidden_ratio + tap_index) for tap_index in range(3)], 0
            ),
        )

    positions = seq_index * tok_dev + jnp.arange(tok_dev, dtype=jnp.int32)
    book_id = jnp.sum(jnp.where(jnp.arange(group_count) == group_index, book_of_group, 0))
    book_counts = jnp.sum(jnp.where((jnp.arange(group_count) == book_id)[:, None], seg_valid, 0), 0)
    segments = seg_valid.shape[1]
    row_counts = jnp.sum(
        jnp.where(
            (positions // S)[:, None] == jnp.arange(segments)[None, :], book_counts[None, :], 0
        ),
        1,
    )
    row_valid = (positions % S < row_counts).astype(jnp.float32)
    query_weight, key_weight, value_weight, out_weight, up_weight, down_weight, conv_weight = (
        fetch_weights()
    )
    inputs = tokens.astype(jnp.float32)
    normed = layer_norm(inputs, norm_params[0], norm_params[1]).astype(jnp.bfloat16)
    queries = matmul(normed, query_weight).astype(jnp.bfloat16)
    keys_raw = matmul(normed, key_weight).astype(jnp.bfloat16)
    values_raw = matmul(normed, value_weight).astype(jnp.bfloat16)
    windows = normed.reshape(comp_slots, 3, model_width)
    compressed = jnp.einsum(
        "jtd,tde->je", windows, conv_weight, preferred_element_type=jnp.float32
    ).astype(jnp.bfloat16)
    key_block = jnp.concatenate([keys_raw, matmul(compressed, key_weight).astype(jnp.bfloat16)], 0)
    value_block = jnp.concatenate(
        [values_raw, matmul(compressed, value_weight).astype(jnp.bfloat16)], 0
    )
    key_source = jnp.concatenate([normed, compressed], 0)
    sources = seq_index - jnp.arange(key_devs, dtype=jnp.int32)
    all_keys, all_values = (
        lax.all_gather(key_block, "seq", axis=0, tiled=True),
        lax.all_gather(value_block, "seq", axis=0, tiled=True),
    )
    clipped = jnp.maximum(sources, 0)
    key_pieces = jax.vmap(
        lambda source: lax.dynamic_slice_in_dim(all_keys, source * key_rows, key_rows, 0)
    )(clipped)
    value_pieces = jax.vmap(
        lambda source: lax.dynamic_slice_in_dim(all_values, source * key_rows, key_rows, 0)
    )(clipped)
    raw_marks, comp_marks = jax.vmap(lambda source: key_marks(source, tok_dev, comp_slots))(sources)
    pieces = (key_pieces, value_pieces, raw_marks, comp_marks)
    heads_query = queries.reshape(tok_dev, HEADS, HEAD_DIM)

    def piece_scores(piece):
        allowed = allowed_keys(positions, piece[2], piece[3])
        scores = (
            jnp.einsum(
                "qhd,khd->hqk",
                heads_query,
                piece[0].reshape(key_rows, HEADS, HEAD_DIM),
                preferred_element_type=jnp.float32,
            )
            * score_scale
        )
        return (jnp.where(allowed[None], scores, NEG_SCORE), allowed)

    def max_step(carry, piece):
        running_max, running_total = carry
        scores, allowed = piece_scores(piece)
        new_max = jnp.maximum(running_max, jnp.max(scores, axis=-1))
        exp_terms = jnp.where(allowed[None], jnp.exp(scores - new_max[..., None]), 0.0)
        return (
            (new_max, running_total * jnp.exp(running_max - new_max) + jnp.sum(exp_terms, -1)),
            None,
        )

    start_max = jnp.full((HEADS, tok_dev), NEG_SCORE, jnp.float32)
    (final_max, final_total), unused = lax.scan(
        max_step, (start_max, jnp.zeros((HEADS, tok_dev), jnp.float32)), pieces
    )
    log_total = final_max + jnp.log(final_total)

    def probabilities(piece):
        scores, allowed = piece_scores(piece)
        return jnp.where(allowed[None], jnp.exp(scores - log_total[..., None]), 0.0)

    def value_step(accum, piece):
        probs = probabilities(piece).astype(jnp.bfloat16)
        values_heads = piece[1].reshape(key_rows, HEADS, HEAD_DIM)
        return (
            accum
            + jnp.einsum("hqk,khd->qhd", probs, values_heads, preferred_element_type=jnp.float32),
            None,
        )

    attended_sum, unused = lax.scan(
        value_step, jnp.zeros((tok_dev, HEADS, HEAD_DIM), jnp.float32), pieces
    )
    attended = attended_sum.reshape(tok_dev, model_width).astype(jnp.bfloat16)
    hidden = inputs + matmul(attended, out_weight)
    normed_two = layer_norm(hidden, norm_params[2], norm_params[3]).astype(jnp.bfloat16)
    pre_act = times_transposed(normed_two, up_weight)
    active = jax.nn.gelu(pre_act).astype(jnp.bfloat16)
    output = hidden + matmul(active, down_weight)
    mixed = (output * row_valid[:, None]).astype(jnp.bfloat16)
    grad_out = cotangent.astype(jnp.float32) * row_valid[:, None]
    grad_out_low = grad_out.astype(jnp.bfloat16)
    grad_active = times_transposed(grad_out_low, down_weight)
    gelu_value, gelu_back = jax.vjp(jax.nn.gelu, pre_act)
    grad_pre = gelu_back(grad_active)[0].astype(jnp.bfloat16)
    grad_normed_two = matmul(grad_pre, up_weight)
    norm_value, norm_two_back = jax.vjp(layer_norm, hidden, norm_params[2], norm_params[3])
    grad_hidden_norm, grad_gain_two, grad_shift_two = norm_two_back(grad_normed_two)
    grad_hidden = grad_out + grad_hidden_norm
    grad_branch = grad_hidden.astype(jnp.bfloat16)
    grad_attended = times_transposed(grad_branch, out_weight).astype(jnp.bfloat16)
    heads_grad = grad_attended.reshape(tok_dev, HEADS, HEAD_DIM)
    delta = jnp.sum(heads_grad.astype(jnp.float32) * attended_sum, -1).T

    def grad_step(accum, piece):
        probs = probabilities(piece)
        keys_heads = piece[0].reshape(key_rows, HEADS, HEAD_DIM)
        grad_probs = jnp.einsum(
            "qhd,khd->hqk",
            heads_grad,
            piece[1].reshape(key_rows, HEADS, HEAD_DIM),
            preferred_element_type=jnp.float32,
        )
        grad_scores = (probs * (grad_probs - delta[..., None])).astype(jnp.bfloat16)
        accum = accum + jnp.einsum(
            "hqk,khd->qhd", grad_scores, keys_heads, preferred_element_type=jnp.float32
        )
        piece_key_grad = (
            jnp.einsum("hqk,qhd->khd", grad_scores, heads_query, preferred_element_type=jnp.float32)
            * score_scale
        )
        piece_value_grad = jnp.einsum(
            "hqk,qhd->khd",
            probs.astype(jnp.bfloat16),
            heads_grad,
            preferred_element_type=jnp.float32,
        )
        return (
            accum,
            (
                piece_key_grad.reshape(key_rows, model_width),
                piece_value_grad.reshape(key_rows, model_width),
            ),
        )

    query_accum, (key_grads, value_grads) = lax.scan(
        grad_step, jnp.zeros((tok_dev, HEADS, HEAD_DIM), jnp.float32), pieces
    )
    grad_queries = (query_accum * score_scale).reshape(tok_dev, model_width).astype(jnp.bfloat16)
    block_total = lax.axis_size("seq") * key_rows // key_rows
    block_sources = jnp.arange(block_total, dtype=jnp.int32)
    slot_offsets = seq_index - block_sources
    inside = ((slot_offsets >= 0) & (slot_offsets < key_devs)).astype(jnp.float32)
    picked = jnp.clip(slot_offsets, 0, key_devs - 1)
    joined = jnp.concatenate([key_grads[picked], value_grads[picked]], 2)
    summed = lax.psum_scatter(
        (joined * inside[:, None, None])
        .reshape(lax.axis_size("seq") * key_rows, 2 * model_width)
        .astype(jnp.bfloat16),
        "seq",
        scatter_dimension=0,
        tiled=True,
    ).astype(jnp.float32)
    key_total = summed[:, :model_width]
    value_total = summed[:, model_width:]
    grad_keys = key_total.astype(jnp.bfloat16)
    grad_values = value_total.astype(jnp.bfloat16)
    grad_normed = (
        times_transposed(grad_queries, query_weight)
        + times_transposed(grad_keys[:tok_dev], key_weight)
        + times_transposed(grad_values[:tok_dev], value_weight)
    )
    grad_compressed = (
        times_transposed(grad_keys[tok_dev:], key_weight)
        + times_transposed(grad_values[tok_dev:], value_weight)
    ).astype(jnp.bfloat16)
    grad_windows = jnp.einsum(
        "je,tde->jtd", grad_compressed, conv_weight, preferred_element_type=jnp.float32
    ).reshape(tok_dev, model_width)
    grad_normed = grad_normed + grad_windows
    norm_value_one, norm_one_back = jax.vjp(layer_norm, inputs, norm_params[0], norm_params[1])
    grad_inputs_norm, grad_gain_one, grad_shift_one = norm_one_back(grad_normed)
    input_grad = grad_hidden + grad_inputs_norm
    norm_local = jnp.stack([grad_gain_one, grad_shift_one, grad_gain_two, grad_shift_two], 0)
    norm_grad = lax.psum(norm_local, ("grp", "seq"))
    pairs = [
        (normed, grad_queries),
        (key_source, grad_keys),
        (key_source, grad_values),
        (attended, grad_branch),
    ]
    pairs = pairs + [
        (grad_pre[:, piece_index * model_width : (piece_index + 1) * model_width], normed_two)
        for piece_index in range(hidden_ratio)
    ]
    pairs = pairs + [
        (active[:, piece_index * model_width : (piece_index + 1) * model_width], grad_out_low)
        for piece_index in range(hidden_ratio)
    ]
    pairs = pairs + [(windows[:, tap_index], grad_compressed) for tap_index in range(3)]
    row_grads = lax.psum_scatter(
        jnp.stack(
            [contract_rows(left_part, right_part) for left_part, right_part in pairs], 1
        ).astype(jnp.bfloat16),
        "seq",
        scatter_dimension=0,
        tiled=True,
    ).astype(jnp.float32)
    slotted = jnp.einsum("sp,rpd->srd", owner_scaled, row_grads, precision=lax.Precision.HIGHEST)
    slot_grad = lax.psum_scatter(
        slotted.astype(jnp.bfloat16), "grp", scatter_dimension=0, tiled=True
    ).astype(jnp.float32)
    slot_first, slot_second, slot_weight = adam_update(
        slot_grad, first_moment, second_moment, master, SLOT_RATE
    )
    norm_first_new, norm_second_all, norm_weight = adam_update(
        norm_grad, norm_first, norm_second, norm_params, NORM_RATE
    )
    return (
        mixed,
        input_grad,
        slot_grad,
        slot_first,
        slot_second,
        slot_weight,
        norm_grad,
        norm_first_new,
        norm_second_all[:2],
        norm_second_all[2:],
        norm_weight,
    )


def solution(mesh):
    return jax.shard_map(
        local,
        mesh=mesh,
        in_specs=(
            P(("grp", "seq"), None),
            P(("grp", "seq"), None),
            P("grp", "seq", None),
            P("grp", "seq", None),
            P("grp", "seq", None),
            P(),
            P(),
            P(),
            P(),
            P(),
            P(),
        ),
        out_specs=(
            P(("grp", "seq"), None),
            P(("grp", "seq"), None),
            P("grp", "seq", None),
            P("grp", "seq", None),
            P("grp", "seq", None),
            P("grp", "seq", None),
            P(),
            P(),
            P(),
            P(),
            P(),
        ),
        check_vma=False,
    )
```

profile of v0, /device:TPU:0, one launch (start us, length us, event | category | flops | bytes accessed | tf_op | source)
XLA Modules:
  0.0 1895.7 jit_solution(11437562039423559559)
XLA Ops:
  11.6 119.5 %all-gather.5.cloned.1.call-done = bf16[6,1024,1024]{2,1,0:T(8,128)(2,1)} async-done(((bf16[6,128,1024]{2,1,0:T(8,128)(2,1)}), bf16[6,1024,1024]{2,1,0:T(8,128)(2,1)}) %all-gather.5.cloned.1.call-update) | async-done | bytes 12582928 | tf_op jit(solution)/shard_map/all_gather | solution.py:122
  158.4 409.8 %all-gather.7.cloned.1.call-done = bf16[24,1024,1024]{2,1,0:T(8,128)(2,1)} async-done(((bf16[6,1024,1024]{2,1,0:T(8,128)(2,1)}), bf16[24,1024,1024]{2,1,0:T(8,128)(2,1)}) %all-gather.7.cloned.1.call-update) | async-done | bytes 50331664 | tf_op jit(solution)/shard_map/all_gather | solution.py:123
  568.3 14.7 dynamic-slice_bitcast_fusion.5
  612.0 63.7 %all-gather.9.cloned.1.call-done = bf16[4096,1024]{1,0:T(8,128)(2,1)} async-done(((bf16[512,1024]{1,0:T(8,128)(2,1)}), bf16[4096,1024]{1,0:T(8,128)(2,1)}) %all-gather.9.cloned.1.call-update) | async-done | bytes 8388624 | tf_op jit(solution)/shard_map/all_gather | solution.py:179
  679.7 35.2 %while.56 = (s32[]{:T(128)}, bf16[4096,1024]{1,0:T(8,128)(2,1)}, s32[8,2]{0,1:T(2,128)S(1)}, bf16[8,512,1024]{1,2,0:T(8,128)(2,1)}, s32[]{:T(128)}) while((s32[]{:T(128)}, bf16[4096,1024]{1,0:T(8,128)(2,1)}, s32[8,2]{0,1:T(2,128)S(1)}, bf16[8,512,1024]{1,2,0:T(8,128)(2,1)}, s32[]{:T(128)}) %tuple.224), condition=%wide.while_cond, body=%wide.while_body.sunk | while | flops 2 | bytes 6291561 | solution.py:186
  714.8 43.4 %all-gather.11.cloned.1.call-done = bf16[4096,1024]{1,0:T(8,128)(2,1)} async-done(((bf16[512,1024]{1,0:T(8,128)(2,1)}), bf16[4096,1024]{1,0:T(8,128)(2,1)}) %all-gather.11.cloned.1.call-update) | async-done | bytes 8388624 | tf_op jit(solution)/shard_map/all_gather | solution.py:178
  762.3 34.9 %while.57 = (s32[]{:T(128)}, bf16[4096,1024]{1,0:T(8,128)(2,1)}, s32[8,2]{0,1:T(2,128)S(1)}, bf16[8,512,1024]{1,2,0:T(8,128)(2,1)}, s32[]{:T(128)}) while((s32[]{:T(128)}, bf16[4096,1024]{1,0:T(8,128)(2,1)}, s32[8,2]{0,1:T(2,128)S(1)}, bf16[8,512,1024]{1,2,0:T(8,128)(2,1)}, s32[]{:T(128)}) %tuple.260), condition=%wide.while_cond.1, body=%wide.while_body.1.sunk | while | flops 2 | bytes 6291561 | solution.py:183
  797.1 81.7 %while.58 = (s32[]{:T(128)}, f32[8,384]{1,0:T(8,128)S(1)}, f32[8,384]{1,0:T(8,128)S(1)}, s32[8,384]{1,0:T(8,128)S(1)}, s32[8,128]{1,0:T(8,128)S(1)}, /*index=5*/...) while((s32[]{:T(128)}, f32[8,384]{1,0:T(8,128)S(1)}, ...), condition=%wide.region_6.7_spmd.clone.clone.clone, body=%wide.region_3.6_spmd.clone.clone.clone.sunk | while | flops 416197248 | bytes 20828336 | solution.py:216
  878.9 74.5 %while.59 = (s32[]{:T(128)}, f32[384,8,128]{0,2,1:T(8,128)}, bf16[8,512,1024]{1,2,0:T(8,128)(2,1)}, s32[8,384]{1,0:T(8,128)S(1)}, s32[8,128]{1,0:T(8,128)S(1)}, ...) while((s32[]{:T(128)}, f32[384,8,128]{0,2,1:T(8,128)}, ...), condition=%wide.region_8.9_spmd.clone.clone.clone, body=%wide.region_7.8_spmd.clone.clone.clone.sunk | while | flops 814902912 | bytes 14192823 | solution.py:234
  960.4 15.2 multiply_convert_fusion
  975.6 15.5 fusion.70
  991.2 8.6 multiply_reduce_fusion
  1010.0 225.6 %while.60 = (s32[]{:T(128)}, f32[384,8,128]{0,2,1:T(8,128)}, f32[8,512,1024]{2,1,0:T(8,128)}, f32[8,512,1024]{2,1,0:T(8,128)}, bf16[8,512,1024]{1,2,0:T(8,128)(2...) while((s32[]{:T(128)}, f32[384,8,128]{0,2,1:T(8,128)}, ...), condition=%wide.region_18.19_spmd.clone.clone.clone, body=%wide.region_17.18_spmd.clone.clone.clone.sunk | while | flops 2034396800 | bytes 105902440 | solution.py:289
  1028.3 6.0 fusion.328
  1235.6 13.3 gather_fusion.1
  1249.0 13.5 gather_fusion
  1262.4 18.0 fusion.63
  1286.7 161.7 %reduce-scatter.4.cloned.1.call-done = bf16[512,2048]{1,0:T(8,128)(2,1)} async-done(((bf16[4096,2048]{1,0:T(8,128)(2,1)}), bf16[512,2048]{1,0:T(8,128)(2,1)}) %reduce-scatter.4.cloned.1.call-update) | async-done | bytes 2097168 | tf_op jit(solution)/shard_map/reduce_scatter | solution.py:299
  1490.8 304.8 %reduce-scatter.6.cloned.1.call-done = bf16[128,15,1024]{2,0,1:T(8,128)(2,1)} async-done(((bf16[1024,15,1024]{2,0,1:T(8,128)(2,1)}), bf16[128,15,1024]{2,0,1:T(8,128)(2,1)}) %reduce-scatter.6.cloned.1.call-update) | async-done | bytes 3932176 | tf_op jit(solution)/shard_map/reduce_scatter | solution.py:344
  1795.7 8.6 fusion.73
  1804.3 6.2 copy.187
  1815.6 7.7 multiply_convert_fusion.3
  1837.6 38.7 %psum.7 = f32[4,1024]{1,0:T(4,128)S(1)} all-reduce(f32[4,1024]{1,0:T(4,128)S(1)} %pad_maximum_fusion.22), channel_id=1, replica_groups=mesh['grp'=4,'seq'=8] {'grp','seq'}, use_global_device_ids=true, to_apply=%region_28.29 | all-reduce | flops 4096 | bytes 32768 | tf_op jit(solution)/shard_map/psum | solution.py:328
  1880.9 7.8 multiply_subtract_fusion
  (811 shorter events, 572.4 us)
Async XLA Ops:
  7.2 124.0 %all-gather.5.cloned.1.call-start = ((), (), s32[]{:S(2)}) async-start(), calls=%async_computation.3 | async-start | bytes 14155776 | tf_op jit(solution)/shard_map/all_gather | solution.py:122
  11.6 556.7 %all-gather.7.cloned.1.call-start = ((), (), s32[]{:S(2)}) async-start(), calls=%async_computation.4 | async-start | bytes 62914560 | tf_op jit(solution)/shard_map/all_gather | solution.py:123
  131.2 16.8 copy-start.7
  131.2 18.0 copy-start.56
  131.2 544.4 %all-gather.9.cloned.1.call-start = ((), (), s32[]{:S(2)}) async-start(), calls=%async_computation.5 | async-start | bytes 9437184 | tf_op jit(solution)/shard_map/all_gather | solution.py:179
  150.1 457.5 %copy-start.19 = (bf16[384,1024]{1,0:T(8,128)(2,1)}, bf16[384,1024]{1,0:T(8,128)(2,1)S(1)}, u32[]{:S(2)}) copy-start(bf16[384,1024]{1,0:T(8,128)(2,1)S(1)} %fusion.114) | copy-start | bytes 2359300
  150.7 432.3 %copy-start.15 = (bf16[128,3,1024]{2,1,0:T(4,128)(2,1)}, bf16[128,3,1024]{2,1,0:T(4,128)(2,1)S(1)}, u32[]{:S(2)}) copy-start(bf16[128,3,1024]{2,1,0:T(4,128)(2,1)S(1)} %reshape.627) | copy-start | bytes 2359300
  593.4 164.9 %all-gather.11.cloned.1.call-start = ((), (), s32[]{:S(2)}) async-start(), calls=%async_computation.6 | async-start | bytes 9437184 | tf_op jit(solution)/shard_map/all_gather | solution.py:178
  601.1 847.3 %reduce-scatter.4.cloned.1.call-start = ((), (), s32[]{:S(2)}) async-start(), calls=%async_computation.7 | async-start | bytes 18874368 | tf_op jit(solution)/shard_map/reduce_scatter | solution.py:299
  607.5 392.9 %copy-start.61 = (f32[384]{0:T(512)}, f32[384]{0:T(512)S(1)}, u32[]{:S(2)}) copy-start(f32[384]{0:T(512)S(1)} %fusion.203) | copy-start | bytes 4612
  878.9 76.0 %copy-start.8 = (bf16[384,1024]{1,0:T(8,128)(2,1)S(1)}, bf16[384,1024]{1,0:T(8,128)(2,1)}, u32[]{:S(2)}) copy-start(bf16[384,1024]{1,0:T(8,128)(2,1)} %param.18) | copy-start | bytes 2359300
  957.9 41.9 %copy-start.10 = (f32[384,1024]{1,0:T(8,128)}, f32[384,1024]{1,0:T(8,128)S(1)}, u32[]{:S(2)}) copy-start(f32[384,1024]{1,0:T(8,128)S(1)} %get-tuple-element.1263) | copy-start | bytes 4718596
  958.6 17.0 copy-start.43
  1280.4 515.2 %reduce-scatter.6.cloned.1.call-start = ((), (), s32[]{:S(2)}) async-start(), calls=%async_computation.8 | async-start | bytes 35389440 | tf_op jit(solution)/shard_map/reduce_scatter | solution.py:344
  1284.0 164.4 %copy-start.47 = (bf16[384,8,128]{0,2,1:T(8,128)(2,1)}, bf16[384,8,128]{0,2,1:T(8,128)(2,1)S(1)}, u32[]{:S(2)}) copy-start(bf16[384,8,128]{0,2,1:T(8,128)(2,1)S(1)} %multiply_convert_fusion.2) | copy-start | bytes 2359300
  1284.0 164.4 %copy-start.39 = (bf16[128,1024]{1,0:T(8,128)(2,1)S(1)}, bf16[128,1024]{1,0:T(8,128)(2,1)}, u32[]{:S(2)}) copy-start(bf16[128,1024]{1,0:T(8,128)(2,1)} %copy-done.38) | copy-start | bytes 786436
  1490.7 304.9 %copy-start.50 = (s32[15]{0:T(128)S(1)}, s32[15]{0:T(128)}, u32[]{:S(2)}) copy-start(s32[15]{0:T(128)} %param.28) | copy-start | bytes 184
  1490.7 304.9 %copy-start.72 = (f32[15]{0:T(128)S(1)}, f32[15]{0:T(128)}, u32[]{:S(2)}) copy-start(f32[15]{0:T(128)} %constant.430.clone) | copy-start | bytes 184
  1490.8 390.1 %reduce-scatter.8.cloned.1.call-start = ((), (), s32[]{:S(2)}) async-start(), calls=%async_computation.9 | async-start | bytes 7864320 | tf_op jit(solution)/shard_map/reduce_scatter | solution.py:353
  1832.2 44.2 %copy-start.57 = (f32[4,1024]{1,0:T(4,128)S(1)}, f32[4,1024]{1,0:T(4,128)}, u32[]{:S(2)}) copy-start(f32[4,1024]{1,0:T(4,128)} %param.23) | copy-start | bytes 49156
  1832.2 44.2 %copy-start.67 = (f32[4,1024]{1,0:T(4,128)S(1)}, f32[4,1024]{1,0:T(4,128)}, u32[]{:S(2)}) copy-start(f32[4,1024]{1,0:T(4,128)} %param.25) | copy-start | bytes 49156
  1832.2 44.2 %copy-start.68 = (f32[4,1024]{1,0:T(4,128)S(1)}, f32[4,1024]{1,0:T(4,128)}, u32[]{:S(2)}) copy-start(f32[4,1024]{1,0:T(4,128)} %param.24) | copy-start | bytes 49156
  1832.2 45.4 %copy-start.64 = (f32[384]{0:T(512)S(1)}, f32[384]{0:T(512)}, u32[]{:S(2)}) copy-start(f32[384]{0:T(512)} %copy-done.63) | copy-start | bytes 4612
  1835.6 42.0 %copy-start.13 = (f32[384,1024]{1,0:T(8,128)S(1)}, f32[384,1024]{1,0:T(8,128)}, u32[]{:S(2)}) copy-start(f32[384,1024]{1,0:T(8,128)} %copy-done.12) | copy-start | bytes 4718596
  (115 other events, 374.1 us)
Sparse Core Ops, SparseCore 0:
  11.7 119.4 all-gather.4
  133.0 435.1 all-gather.6
  593.5 82.0 all-gather.8
  677.7 80.5 all-gather.10
  1280.5 167.8 reduce-scatter.3
  1490.9 304.7 reduce-scatter.5
  1810.7 69.9 reduce-scatter.7
where the time goes:
time: 1910 us; the launch traced here: 1900 us
  waiting for transfers between devices  1100 us (58%)
  matrix products  348 us (18%)
  local copies, waits for them, and re-layouts  269 us (14%)
  other arithmetic  89.9 us (5%)
  between operations  43.8 us (2%)
  blocking collectives  38.7 us (2%)
    all_gather x1, waiting for transfers between devices, fetch_weights(): gathered = lax.all_gather(local_rows, 'grp', axis=0, tiled=True)  410 us
    reduce_scatter x1, waiting for transfers between devices, local(): lax.psum_scatter(jnp.stack([contract_rows(left_part, right_part) for left...  305 us
    reduce_scatter x1, waiting for transfers between devices, local(): lax.psum_scatter((joined * inside[:, None, None]).reshape(lax.axis_size('...  162 us
    all_gather x1, waiting for transfers between devices, fetch_weights(): local_rows = lax.all_gather(scaled, 'seq', axis=1, tiled=True)  120 us
    gather x80, local copies, waits for them, and re-layouts  69.6 us
    all_gather x1, waiting for transfers between devices, local(): lax.all_gather(value_block, 'seq', axis=0, tiled=True)  63.7 us
    dynamic_update_slice x32, local copies, waits for them, and re-layouts, local(): lax.scan(grad_step, jnp.zeros((tok_dev, HEADS, HEAD_DIM), jnp.float32), p...  54.7 us
    dynamic_slice x48, local copies, waits for them, and re-layouts, local(): lax.scan(max_step, (start_max, jnp.zeros((HEADS, tok_dev), jnp.float32)),...  51.3 us
  transfers between devices with their start and end apart: 7, of which 6 were waited for; matrix products, arithmetic and copies ran while one was open for 5% of the time, Pallas kernels for 0%

commit v1 on v0

v1 whole, which is shorter than its diff:
```python
import functools

import jax
import jax.numpy as jnp
from jax import lax
from jax.experimental import pallas as pl
from jax.experimental.pallas import tpu as pltpu
from jax.sharding import PartitionSpec as P

D = 1024
HEADS = 8
HEAD_DIM = 128
FF = 4096
S = 512
CM = 512
STEP = 10
PANELS = 15
RATIO = FF // D
QB = 128
RAW_KEYS = 2 * S
COMP_KEYS = CM + QB
MIB = 1 << 20

NEG_SCORE = -1e30
NORM_EPS = 1e-05
BETA_ONE = 0.9
BETA_TWO = 0.999
WEIGHT_DECAY = 0.1
ADAM_EPS = 1e-08
NORM_RATE = 1.0
SLOT_RATE = 2.0
BF16 = jnp.bfloat16
F32 = jnp.float32
MESH = pl.DeviceIdType.MESH


def layer_norm(values, gain, shift):
    row_mean = jnp.mean(values, axis=-1, keepdims=True)
    centered = values - row_mean
    variance = jnp.mean(centered * centered, axis=-1, keepdims=True)
    return centered * lax.rsqrt(variance + NORM_EPS) * gain + shift


def panel_deviations():
    inner_dev = D ** (-0.5)
    deviations = [inner_dev] * 3 + [(D // (2 * S)) ** (-0.5)] + [inner_dev] * RATIO
    deviations = deviations + [FF ** (-0.5)] * RATIO + [(3 * D) ** (-0.5)] * 3
    return jnp.array(deviations, F32)


def adam_update(gradient, first_old, second_old, weight_old, step_rate):
    first_new = BETA_ONE * first_old + (1.0 - BETA_ONE) * gradient
    second_new = BETA_TWO * second_old + (1.0 - BETA_TWO) * gradient * gradient
    fix_one = 1.0 - BETA_ONE**STEP
    fix_two = 1.0 - BETA_TWO**STEP
    movement = first_new / fix_one / (jnp.sqrt(second_new / fix_two) + ADAM_EPS)
    return (first_new, second_new, weight_old - step_rate * (movement + WEIGHT_DECAY * weight_old))


def matmul(left, right):
    return jnp.dot(left, right, preferred_element_type=F32)


def times_transposed(left, right):
    return lax.dot_general(left, right, (((1,), (1,)), ((), ())), preferred_element_type=F32)


def contract_rows(left, right):
    return lax.dot_general(left, right, (((0,), (0,)), ((), ())), preferred_element_type=F32)


class Place:
    def __init__(self, lines):
        self.lines = lines
        self.grp = lax.axis_index("grp")
        self.seq = lax.axis_index("seq")
        self.line = self.seq // 2
        self.core = self.seq % 2
        self.row = self.grp // 2
        self.col = self.grp % 2
        self.grp_x = self.row * 2 + 1 - self.col
        self.grp_y = (1 - self.row) * 2 + self.col
        self.x_dev = {"grp": self.grp_x, "seq": self.seq}
        self.y_dev = {"grp": self.grp_y, "seq": self.seq}
        self.core_dev = {"grp": self.grp, "seq": self.line * 2 + 1 - self.core}

    def other_line(self, k):
        return lax.rem(self.line + k, self.lines)

    def line_dev(self, k):
        return {"grp": self.grp, "seq": self.other_line(k) * 2 + self.core}

    def enter(self):
        barrier = pltpu.get_barrier_semaphore()
        partners = [self.line_dev(k) for k in range(1, self.lines)]
        partners = partners + [self.x_dev, self.y_dev, self.core_dev]
        for device in partners:
            pl.semaphore_signal(barrier, inc=1, device_id=device, device_id_type=MESH)
        pl.semaphore_wait(barrier, self.lines + 2)


def remote(src, dst, send, recv, device):
    return pltpu.make_async_remote_copy(
        src_ref=src,
        dst_ref=dst,
        send_sem=send,
        recv_sem=recv,
        device_id=device,
        device_id_type=MESH,
    )


def gather_kernel(panels, lines, ahead, block_ref, full_ref, own_sem, zs, zr, s1, r1, s2, r2, cs, cr):
    at = Place(lines)
    wide = block_ref.shape[-1]

    def cols(g):
        return pl.ds(pl.multiple_of(g * wide, wide), wide)

    def line_copy(p, k):
        dst = full_ref.at[p, at.line // 2, at.line % 2, at.core, :, cols(at.grp)]
        return remote(block_ref.at[p], dst, zs.at[p, k], zr.at[p, at.line], at.line_dev(k))

    def line_arrival(p, k):
        z = at.other_line(k)
        dst = full_ref.at[p, z // 2, z % 2, at.core, :, cols(at.grp)]
        return remote(block_ref.at[p], dst, zs.at[p, k], zr.at[p, z], at.line_dev(k))

    def part(p, h, g):
        return full_ref.at[p, :, h, at.core, :, cols(g)]

    def first(p, h, g):
        device = at.x_dev if h == 0 else at.y_dev
        return remote(part(p, h, g), part(p, h, g), s1.at[p, h], r1.at[p, h], device)

    def second(p, h, j, g):
        device = at.y_dev if h == 0 else at.x_dev
        return remote(part(p, h, g), part(p, h, g), s2.at[p, h, j], r2.at[p, h, j], device)

    def cross(p, h, core):
        ref = full_ref.at[p, :, h, core]
        return remote(ref, ref, cs.at[p, h], cr.at[p, h], at.core_dev)

    def start_lines(p):
        for k in range(1, lines):
            line_copy(p, k).start()

    def start_first(p):
        for k in range(1, lines):
            line_arrival(p, k).wait_recv()
        for h in (0, 1):
            first(p, h, at.grp).start()

    def start_second(p):
        for h in (0, 1):
            near = at.grp_x if h == 0 else at.grp_y
            first(p, h, near).wait_recv()
            second(p, h, 0, at.grp).start()
            second(p, h, 1, near).start()

    def start_cross(p):
        for h in (0, 1):
            second(p, h, 0, at.grp_y if h == 0 else at.grp_x).wait_recv()
            second(p, h, 1, 3 - at.grp).wait_recv()
            cross(p, h, at.core).start()

    def finish(p):
        for h in (0, 1):
            cross(p, h, 1 - at.core).wait_recv()
            first(p, h, at.grp).wait_send()
            second(p, h, 0, at.grp).wait_send()
            second(p, h, 1, at.grp_x if h == 0 else at.grp_y).wait_send()
            cross(p, h, at.core).wait_send()
        for k in range(1, lines):
            line_copy(p, k).wait_send()

    at.enter()
    own_place = full_ref.at[:, at.line // 2, at.line % 2, at.core, :, cols(at.grp)]
    own = pltpu.make_async_copy(block_ref, own_place, own_sem)
    own.start()
    for p in range(ahead):
        start_lines(p)
    own.wait()

    def step(t, carry):
        @pl.when(t + ahead < panels)
        def _():
            start_lines(t + ahead)

        @pl.when(t < panels)
        def _():
            start_first(t)

        @pl.when((t >= 1) & (t < panels + 1))
        def _():
            start_second(t - 1)

        @pl.when((t >= 2) & (t < panels + 2))
        def _():
            start_cross(t - 2)

        @pl.when(t >= 3)
        def _():
            finish(t - 3)

        return carry

    lax.fori_loop(0, panels + 3, step, 0)


def gather_panels(block, lines):
    panels, rows, wide = block.shape
    dma = pltpu.SemaphoreType.DMA
    full = pl.pallas_call(
        functools.partial(gather_kernel, panels, lines, 3),
        out_shape=jax.ShapeDtypeStruct((panels, lines // 2, 2, 2, rows, 4 * wide), BF16),
        in_specs=[pl.BlockSpec(memory_space=pl.ANY)],
        out_specs=pl.BlockSpec(memory_space=pl.ANY),
        scratch_shapes=[
            dma(()),
            dma((panels, lines)),
            dma((panels, lines)),
            dma((panels, 2)),
            dma((panels, 2)),
            dma((panels, 2, 2)),
            dma((panels, 2, 2)),
            dma((panels, 2)),
            dma((panels, 2)),
        ],
        compiler_params=pltpu.CompilerParams(collective_id=0, has_side_effects=True),
        name="gather_panels",
    )(block)
    return full.reshape(panels, D, D)


def reduce_kernel(
    panels, lines, grad_ref, out_ref, own, cross_in, first_in, second_in, line_in,
    own_sem, cs, cr, s1, r1, s2, r2, zs, zr,
):
    at = Place(lines)
    wide = out_ref.shape[-1]
    pairs = lines // 2

    def cols(g):
        return pl.ds(g * wide, wide)

    def load(p, g):
        src = grad_ref.at[p, :, :, at.core, :, cols(g)]
        return pltpu.make_async_copy(src, own.at[p, :, :, g // 2, g % 2], own_sem.at[p, g])

    def cross(p, g):
        src = grad_ref.at[p, :, :, 1 - at.core, :, cols(g)]
        dst = cross_in.at[p, :, :, g // 2, g % 2]
        return remote(src, dst, cs.at[p, g], cr.at[p, g], at.core_dev)

    def first(p, h):
        if h == 0:
            src = own.at[p, :, 0, 1 - at.row]
            return remote(src, first_in.at[p, 0], s1.at[p, 0], r1.at[p, 0], at.y_dev)
        src = own.at[p, :, 1, :, 1 - at.col]
        return remote(src, first_in.at[p, 1], s1.at[p, 1], r1.at[p, 1], at.x_dev)

    def second(p, h):
        if h == 0:
            src = own.at[p, :, 0, at.row, 1 - at.col]
            return remote(src, second_in.at[p, 0], s2.at[p, 0], r2.at[p, 0], at.x_dev)
        src = own.at[p, :, 1, 1 - at.row, at.col]
        return remote(src, second_in.at[p, 1], s2.at[p, 1], r2.at[p, 1], at.y_dev)

    def line_copy(p, k):
        z = at.other_line(k)
        src = own.at[p, z // 2, z % 2, at.row, at.col]
        return remote(src, line_in.at[p, at.line], zs.at[p, k], zr.at[p, at.line], at.line_dev(k))

    def line_arrival(p, k):
        z = at.other_line(k)
        src = own.at[p, z // 2, z % 2, at.row, at.col]
        return remote(src, line_in.at[p, z], zs.at[p, k], zr.at[p, z], at.line_dev(k))

    def add(dst, src):
        dst[...] = (dst[...].astype(F32) + src[...].astype(F32)).astype(BF16)

    def start(p):
        for g in range(4):
            cross(p, g).start()
            load(p, g).start()

    def start_first(p):
        for g in range(4):
            cross(p, g).wait_recv()
            load(p, g).wait()
        for h in (0, 1):
            for i in range(pairs):
                for g in range(4):
                    add(own.at[p, i, h, g // 2, g % 2], cross_in.at[p, i, h, g // 2, g % 2])
            first(p, h).start()

    def start_second(p):
        for h in (0, 1):
            first(p, h).wait_recv()
            for i in range(pairs):
                for j in (0, 1):
                    row, col = (at.row, j) if h == 0 else (j, at.col)
                    add(own.at[p, i, h, row, col], first_in.at[p, h, i, j])
            second(p, h).start()

    def start_lines(p):
        for h in (0, 1):
            second(p, h).wait_recv()
            for i in range(pairs):
                add(own.at[p, i, h, at.row, at.col], second_in.at[p, h, i])
        for k in range(1, lines):
            line_copy(p, k).start()

    def finish(p):
        total = own[p, at.line // 2, at.line % 2, at.row, at.col].astype(F32)
        for k in range(1, lines):
            line_arrival(p, k).wait_recv()
            total = total + line_in[p, at.other_line(k)].astype(F32)
        out_ref[p] = total.astype(BF16)
        for h in (0, 1):
            first(p, h).wait_send()
            second(p, h).wait_send()
        for g in range(4):
            cross(p, g).wait_send()
        for k in range(1, lines):
            line_copy(p, k).wait_send()

    at.enter()
    start(0)

    def step(t, carry):
        @pl.when(t + 1 < panels)
        def _():
            start(t + 1)

        @pl.when(t < panels)
        def _():
            start_first(t)

        @pl.when((t >= 1) & (t < panels + 1))
        def _():
            start_second(t - 1)

        @pl.when((t >= 2) & (t < panels + 2))
        def _():
            start_lines(t - 2)

        @pl.when(t >= 3)
        def _():
            finish(t - 3)

        return carry

    lax.fori_loop(0, panels + 3, step, 0)


def reduce_panels(grads, lines):
    panels = grads.shape[0]
    rows, wide, pairs = D // (2 * lines), D // 4, lines // 2
    dma = pltpu.SemaphoreType.DMA
    return pl.pallas_call(
        functools.partial(reduce_kernel, panels, lines),
        out_shape=jax.ShapeDtypeStruct((panels, rows, wide), BF16),
        in_specs=[pl.BlockSpec(memory_space=pl.ANY)],
        out_specs=pl.BlockSpec(memory_space=pltpu.VMEM),
        scratch_shapes=[
            pltpu.VMEM((panels, pairs, 2, 2, 2, rows, wide), BF16),
            pltpu.VMEM((panels, pairs, 2, 2, 2, rows, wide), BF16),
            pltpu.VMEM((panels, 2, pairs, 2, rows, wide), BF16),
            pltpu.VMEM((panels, 2, pairs, rows, wide), BF16),
            pltpu.VMEM((panels, lines, rows, wide), BF16),
            dma((panels, 4)),
            dma((panels, 4)),
            dma((panels, 4)),
            dma((panels, 2)),
            dma((panels, 2)),
            dma((panels, 2)),
            dma((panels, 2)),
            dma((panels, lines)),
            dma((panels, lines)),
        ],
        compiler_params=pltpu.CompilerParams(
            collective_id=1, has_side_effects=True, vmem_limit_bytes=56 * MIB
        ),
        name="reduce_panels",
    )(grads.reshape(panels, pairs, 2, 2, rows, D))


def key_window(seq, tok_dev):
    first_pos = seq * tok_dev
    memory = (first_pos // S - 1) * S
    raw_first = seq - (RAW_KEYS - QB + tok_dev - 1) // tok_dev
    comp_first = jnp.maximum(jnp.floor_divide(memory - 3 * CM, tok_dev), 0)
    return raw_first, comp_first


def block_window(seq, i, tok_dev, raw_rows, comp_rows):
    position = seq * tok_dev + i * QB
    memory = (position // S - 1) * S
    raw_first, comp_first = key_window(seq, tok_dev)
    raw_base = raw_first * tok_dev
    raw_at = jnp.minimum(memory - raw_base, raw_rows - RAW_KEYS)
    comp_end = jnp.floor_divide(memory, 3)
    comp_low = jnp.maximum(comp_end - CM, 0)
    comp_base = comp_first * (tok_dev // 3)
    comp_at = jnp.clip((comp_low - comp_base) // QB * QB, 0, comp_rows - COMP_KEYS)
    return (
        position,
        pl.multiple_of(raw_at, QB),
        pl.multiple_of(comp_at, QB),
        raw_base + raw_at,
        comp_base + comp_at,
        memory,
        comp_low,
        comp_end,
    )


def attend_kernel(tok_dev, q_ref, kr_ref, vr_ref, kc_ref, vc_ref, o_ref, lse_ref):
    seq = lax.axis_index("seq")
    scale = HEAD_DIM ** (-0.5)
    for i in range(tok_dev // QB):
        pos, raw_at, comp_at, raw_pos, comp_pos, memory, comp_low, comp_end = block_window(
            seq, i, tok_dev, kr_ref.shape[0], kc_ref.shape[0]
        )
        q = q_ref[pl.ds(i * QB, QB), :]
        raw = times_transposed(q, kr_ref[pl.ds(raw_at, RAW_KEYS), :]) * scale
        key_pos = raw_pos + lax.broadcasted_iota(jnp.int32, (QB, RAW_KEYS), 1)
        query_pos = pos + lax.broadcasted_iota(jnp.int32, (QB, RAW_KEYS), 0)
        seen = (key_pos >= jnp.maximum(memory, 0)) & (key_pos <= query_pos)
        raw = jnp.where(seen, raw, NEG_SCORE)
        comp = times_transposed(q, kc_ref[pl.ds(comp_at, COMP_KEYS), :]) * scale
        comp_idx = comp_pos + lax.broadcasted_iota(jnp.int32, (QB, COMP_KEYS), 1)
        comp = jnp.where((comp_idx >= comp_low) & (comp_idx < comp_end), comp, NEG_SCORE)
        top = jnp.maximum(
            jnp.max(raw, axis=1, keepdims=True), jnp.max(comp, axis=1, keepdims=True)
        )
        raw = jnp.exp(raw - top)
        comp = jnp.exp(comp - top)
        total = jnp.sum(raw, axis=1, keepdims=True) + jnp.sum(comp, axis=1, keepdims=True)
        out = matmul(raw.astype(BF16), vr_ref[pl.ds(raw_at, RAW_KEYS), :])
        out = out + matmul(comp.astype(BF16), vc_ref[pl.ds(comp_at, COMP_KEYS), :])
        o_ref[pl.ds(i * QB, QB), :] = out / total
        lse = jnp.broadcast_to(top + jnp.log(total), (QB, QB))
        lse_ref[0, :, pl.ds(i * QB, QB)] = lse.T[:8]


def attend(q, kr, vr, kc, vc):
    tok_dev = q.shape[0]

    def head(rows):
        return pl.BlockSpec((rows, HEAD_DIM), lambda h: (0, h))

    return pl.pallas_call(
        functools.partial(attend_kernel, tok_dev),
        grid=(HEADS,),
        in_specs=[head(x.shape[0]) for x in (q, kr, vr, kc, vc)],
        out_specs=[head(tok_dev), pl.BlockSpec((1, 8, tok_dev), lambda h: (h, 0, 0))],
        out_shape=[
            jax.ShapeDtypeStruct((tok_dev, D), F32),
            jax.ShapeDtypeStruct((HEADS, 8, tok_dev), F32),
        ],
        compiler_params=pltpu.CompilerParams(vmem_limit_bytes=32 * MIB),
        name="attend",
    )(q, kr, vr, kc, vc)


def attend_back_kernel(
    tok_dev, q_ref, kr_ref, vr_ref, kc_ref, vc_ref, do_ref, lse_ref, delta_ref,
    dq_ref, dkr_ref, dvr_ref, dkc_ref, dvc_ref, acc_kr, acc_vr, acc_kc, acc_vc,
):
    seq = lax.axis_index("seq")
    scale = HEAD_DIM ** (-0.5)
    for acc in (acc_kr, acc_vr, acc_kc, acc_vc):
        acc[...] = jnp.zeros_like(acc)
    for i in range(tok_dev // QB):
        pos, raw_at, comp_at, raw_pos, comp_pos, memory, comp_low, comp_end = block_window(
            seq, i, tok_dev, kr_ref.shape[0], kc_ref.shape[0]
        )
        rows = pl.ds(i * QB, QB)
        q = q_ref[rows, :]
        do = do_ref[rows, :]
        lse = lse_ref[0, 0:1, rows]
        delta = delta_ref[0, 0:1, rows]

        def part(k_ref, v_ref, acc_k, acc_v, keys, seen):
            k = k_ref[keys, :]
            s = times_transposed(k, q) * scale
            p = jnp.where(seen, jnp.exp(jnp.where(seen, s, NEG_SCORE) - lse), 0.0)
            dp = times_transposed(v_ref[keys, :], do)
            ds = (p * (dp - delta)).astype(BF16)
            acc_v[keys, :] += matmul(p.astype(BF16), do)
            acc_k[keys, :] += matmul(ds, q)
            return contract_rows(ds, k)

        key_pos = raw_pos + lax.broadcasted_iota(jnp.int32, (RAW_KEYS, QB), 0)
        query_pos = pos + lax.broadcasted_iota(jnp.int32, (RAW_KEYS, QB), 1)
        seen = (key_pos >= jnp.maximum(memory, 0)) & (key_pos <= query_pos)
        dq = part(kr_ref, vr_ref, acc_kr, acc_vr, pl.ds(raw_at, RAW_KEYS), seen)
        comp_idx = comp_pos + lax.broadcasted_iota(jnp.int32, (COMP_KEYS, QB), 0)
        seen = (comp_idx >= comp_low) & (comp_idx < comp_end)
        dq = dq + part(kc_ref, vc_ref, acc_kc, acc_vc, pl.ds(comp_at, COMP_KEYS), seen)
        dq_ref[rows, :] = (dq * scale).astype(BF16)
    dkr_ref[...] = (acc_kr[...] * scale).astype(BF16)
    dkc_ref[...] = (acc_kc[...] * scale).astype(BF16)
    dvr_ref[...] = acc_vr[...].astype(BF16)
    dvc_ref[...] = acc_vc[...].astype(BF16)


def attend_back(q, kr, vr, kc, vc, do, lse, delta):
    tok_dev, raw_rows, comp_rows = q.shape[0], kr.shape[0], kc.shape[0]

    def head(rows):
        return pl.BlockSpec((rows, HEAD_DIM), lambda h: (0, h))

    stat = pl.BlockSpec((1, 8, tok_dev), lambda h: (h, 0, 0))
    outs = [tok_dev, raw_rows, raw_rows, comp_rows, comp_rows]
    return pl.pallas_call(
        functools.partial(attend_back_kernel, tok_dev),
        grid=(HEADS,),
        in_specs=[head(x.shape[0]) for x in (q, kr, vr, kc, vc, do)] + [stat, stat],
        out_specs=[head(rows) for rows in outs],
        out_shape=[jax.ShapeDtypeStruct((rows, D), BF16) for rows in outs],
        scratch_shapes=[
            pltpu.VMEM((raw_rows, HEAD_DIM), F32),
            pltpu.VMEM((raw_rows, HEAD_DIM), F32),
            pltpu.VMEM((comp_rows, HEAD_DIM), F32),
            pltpu.VMEM((comp_rows, HEAD_DIM), F32),
        ],
        compiler_params=pltpu.CompilerParams(vmem_limit_bytes=40 * MIB),
        name="attend_back",
    )(q, kr, vr, kc, vc, do, lse, delta)


def local(
    tokens, cotangent, master, first_moment, second_moment, norm_params, norm_first, norm_second,
    seg_valid, book_of_group, panel_slot,
):
    seq_count = lax.axis_size("seq")
    group_count = lax.axis_size("grp")
    seq_index = lax.axis_index("seq")
    group_index = lax.axis_index("grp")
    lines = seq_count // 2
    tok_dev = tokens.shape[0]
    slot_count, slot_rows = master.shape[0], master.shape[1]
    all_slots = slot_count * group_count
    comp_dev = tok_dev // 3
    wide = D // group_count

    slot_ids = jnp.arange(all_slots, dtype=jnp.int32)
    is_panel = panel_slot[None, :] == slot_ids[:, None]
    slot_used = jnp.any(is_panel, 1)
    slot_panel = jnp.argmax(is_panel, 1).astype(jnp.int32)
    scale_all = jnp.sum(jnp.where(is_panel, panel_deviations()[None, :], 0.0), 1)
    slot_scale = lax.dynamic_slice_in_dim(scale_all, group_index * slot_count, slot_count, 0)
    scaled = (master * slot_scale[:, None, None]).astype(BF16)
    scaled = scaled.reshape(slot_count, slot_rows, group_count, wide).transpose(2, 0, 1, 3)
    slots_in = lax.all_to_all(scaled, "grp", 0, 0, tiled=True)
    block = slots_in.reshape(all_slots, slot_rows, wide)[panel_slot]
    weights = gather_panels(block, lines)
    query_weight, key_weight, value_weight, out_weight = [weights[i] for i in range(4)]
    up_weight = weights[4 : 4 + RATIO].reshape(FF, D)
    down_weight = weights[4 + RATIO : 4 + 2 * RATIO].reshape(FF, D)
    conv_weight = weights[4 + 2 * RATIO :]

    positions = seq_index * tok_dev + jnp.arange(tok_dev, dtype=jnp.int32)
    book_id = jnp.sum(jnp.where(jnp.arange(group_count) == group_index, book_of_group, 0))
    book_counts = jnp.sum(jnp.where((jnp.arange(group_count) == book_id)[:, None], seg_valid, 0), 0)
    segments = seg_valid.shape[1]
    row_counts = jnp.sum(
        jnp.where((positions // S)[:, None] == jnp.arange(segments)[None, :], book_counts[None, :], 0), 1
    )
    row_valid = (positions % S < row_counts).astype(F32)

    raw_first, comp_first = key_window(seq_index, tok_dev)
    raw_devs = (RAW_KEYS - QB + tok_dev - 1) // tok_dev + 1
    comp_devs = min((3 * CM + S) // tok_dev + 1, seq_count)
    all_tokens = lax.all_gather(tokens, "seq", axis=0, tiled=True)
    padded = jnp.concatenate([jnp.zeros(((raw_devs - 1) * tok_dev, D), BF16), all_tokens], 0)
    raw_tokens = lax.dynamic_slice_in_dim(padded, seq_index * tok_dev, raw_devs * tok_dev, 0)
    comp_tokens = lax.dynamic_slice_in_dim(all_tokens, comp_first * tok_dev, comp_devs * tok_dev, 0)

    def first_norm(rows):
        return layer_norm(rows.astype(F32), norm_params[0], norm_params[1]).astype(BF16)

    inputs = tokens.astype(F32)
    normed = first_norm(tokens)
    normed_raw = first_norm(raw_tokens)
    normed_comp = first_norm(comp_tokens).reshape(comp_devs * comp_dev, 3 * D)
    compressed = matmul(normed_comp, conv_weight.reshape(3 * D, D)).astype(BF16)
    queries = matmul(normed, query_weight).astype(BF16)
    keys_raw = matmul(normed_raw, key_weight).astype(BF16)
    values_raw = matmul(normed_raw, value_weight).astype(BF16)
    keys_comp = matmul(compressed, key_weight).astype(BF16)
    values_comp = matmul(compressed, value_weight).astype(BF16)
    attended_sum, log_total = attend(queries, keys_raw, values_raw, keys_comp, values_comp)
    attended = attended_sum.astype(BF16)

    hidden = inputs + matmul(attended, out_weight)
    normed_two = layer_norm(hidden, norm_params[2], norm_params[3]).astype(BF16)
    pre_act = times_transposed(normed_two, up_weight)
    active = jax.nn.gelu(pre_act).astype(BF16)
    output = hidden + matmul(active, down_weight)
    mixed = (output * row_valid[:, None]).astype(BF16)
    grad_out = cotangent.astype(F32) * row_valid[:, None]
    grad_out_low = grad_out.astype(BF16)
    grad_active = times_transposed(grad_out_low, down_weight)
    gelu_value, gelu_back = jax.vjp(jax.nn.gelu, pre_act)
    grad_pre = gelu_back(grad_active)[0].astype(BF16)
    grad_normed_two = matmul(grad_pre, up_weight)
    norm_value, norm_two_back = jax.vjp(layer_norm, hidden, norm_params[2], norm_params[3])
    grad_hidden_norm, grad_gain_two, grad_shift_two = norm_two_back(grad_normed_two)
    grad_hidden = grad_out + grad_hidden_norm
    grad_branch = grad_hidden.astype(BF16)
    grad_attended = times_transposed(grad_branch, out_weight).astype(BF16)
    delta = jnp.sum(
        (grad_attended.astype(F32) * attended_sum).reshape(tok_dev, HEADS, HEAD_DIM), -1
    ).T
    delta = jnp.broadcast_to(delta[:, None, :], (HEADS, 8, tok_dev))
    grad_queries, dkr, dvr, dkc, dvc = attend_back(
        queries, keys_raw, values_raw, keys_comp, values_comp, grad_attended, log_total, delta
    )

    grad_comp = (times_transposed(dkc, key_weight) + times_transposed(dvc, value_weight)).astype(BF16)
    placed = lax.dynamic_update_slice_in_dim(
        jnp.zeros((seq_count * comp_dev, D), BF16), grad_comp, comp_first * comp_dev, 0
    )
    grad_compressed = lax.psum_scatter(placed, "seq", scatter_dimension=0, tiled=True)
    grad_raw = times_transposed(dkr, key_weight) + times_transposed(dvr, value_weight)
    grad_normed = grad_raw[(raw_devs - 1) * tok_dev :]
    for back in range(1, raw_devs):
        rows = grad_raw[(raw_devs - 1 - back) * tok_dev : (raw_devs - back) * tok_dev].astype(BF16)
        pairs = [(s, s - back) for s in range(back, seq_count)]
        grad_normed = grad_normed + lax.ppermute(rows, "seq", pairs).astype(F32)
    grad_normed = grad_normed + times_transposed(grad_queries, query_weight)
    grad_windows = times_transposed(grad_compressed, conv_weight.reshape(3 * D, D))
    grad_normed = grad_normed + grad_windows.reshape(tok_dev, D)
    norm_value_one, norm_one_back = jax.vjp(layer_norm, inputs, norm_params[0], norm_params[1])
    grad_inputs_norm, grad_gain_one, grad_shift_one = norm_one_back(grad_normed)
    input_grad = grad_hidden + grad_inputs_norm
    norm_local = jnp.stack([grad_gain_one, grad_shift_one, grad_gain_two, grad_shift_two], 0)
    norm_grad = lax.psum(norm_local, ("grp", "seq"))

    windows = normed.reshape(comp_dev, 3, D)
    grads = [
        contract_rows(normed, grad_queries),
        contract_rows(normed_raw, dkr) + contract_rows(compressed, dkc),
        contract_rows(normed_raw, dvr) + contract_rows(compressed, dvc),
        contract_rows(attended, grad_branch),
    ]
    grads = grads + [contract_rows(grad_pre[:, i * D : (i + 1) * D], normed_two) for i in range(RATIO)]
    grads = grads + [contract_rows(active[:, i * D : (i + 1) * D], grad_out_low) for i in range(RATIO)]
    grads = grads + [contract_rows(windows[:, i], grad_compressed) for i in range(3)]
    row_grads = reduce_panels(jnp.stack([g.astype(BF16) for g in grads], 0), lines)

    slotted = row_grads[slot_panel].astype(F32) * scale_all[:, None, None]
    slotted = jnp.where(slot_used[:, None, None], slotted, 0.0).astype(BF16)
    slotted = slotted.reshape(group_count, slot_count, slot_rows, wide)
    slot_parts = lax.all_to_all(slotted, "grp", 0, 0, tiled=True)
    slot_grad = slot_parts.transpose(1, 2, 0, 3).reshape(slot_count, slot_rows, D).astype(F32)
    slot_first, slot_second, slot_weight = adam_update(
        slot_grad, first_moment, second_moment, master, SLOT_RATE
    )
    norm_first_new, norm_second_all, norm_weight = adam_update(
        norm_grad, norm_first, norm_second, norm_params, NORM_RATE
    )
    return (
        mixed, input_grad, slot_grad, slot_first, slot_second, slot_weight, norm_grad,
        norm_first_new, norm_second_all[:2], norm_second_all[2:], norm_weight,
    )


def solution(mesh):
    rows, slots, whole = P(("grp", "seq"), None), P("grp", "seq", None), P()
    return jax.shard_map(
        local,
        mesh=mesh,
        in_specs=(rows, rows, slots, slots, slots) + (whole,) * 6,
        out_specs=(rows, rows, slots, slots, slots, slots) + (whole,) * 5,
        check_vma=False,
    )
```

time: 1910 us -> 743 us (0.39)
  waiting for transfers between devices: 1100 us -> 12 us
  Pallas kernels: 0 us -> 378 us
  matrix products: 348 us -> 135 us
  local copies, waits for them, and re-layouts: 269 us -> 93.6 us
  other arithmetic: 89.9 us -> 32.8 us
  between operations: 43.8 us -> 15.8 us
    all_gather x4 -> x1, waiting for transfers between devices: 636 us -> 0.01 us  [local(): all_tokens = lax.all_gather(tokens, 'seq', axis=0, tiled=True)]
    reduce_scatter x3 -> x1, waiting for transfers between devices: 467 us -> 0.01 us  [local(): lax.psum_scatter(placed, 'seq', scatter_dimension=0, tiled=True)]
    pallas_call x0 -> x4, Pallas kernels: none -> 378 us  [the longest x1 171 us: gather_panels(): pl.pallas_call(functools.partial(gather_kernel, panels, lines, 3), out_sh...]
    dot_general x67 -> x9, matrix products: 258 us -> 35.5 us  [matmul(): return jnp.dot(left, right, preferred_element_type=F32)]
    gather x82 -> x2, local copies, waits for them, and re-layouts: 96.4 us -> 6.15 us  [the longest x1 3.16 us: local(): slotted = row_grads[slot_panel].astype(F32) * scale_all[:, None, None]]
    dynamic_update_slice x32 -> x0, local copies, waits for them, and re-layouts: 54.7 us -> none  [local(): lax.scan(grad_step, jnp.zeros((tok_dev, HEADS, HEAD_DIM), jnp.float32), p...]
    dynamic_slice x49 -> x1, local copies, waits for them, and re-layouts: 51.3 us -> 0.08 us  [local(): lax.dynamic_slice_in_dim(scale_all, group_index * slot_count, slot_count, 0)]
    reduce_sum x10 -> x2, other arithmetic: 36.3 us -> 2.01 us  [the longest x1 1.92 us: local(): jnp.sum((grad_attended.astype(F32) * attended_sum).reshape(tok_dev, HEADS...]
  transfers between devices with their start and end apart: 7 -> 7, of which waited for: 6 -> 1; matrix products, arithmetic and copies ran while one was open for 5% -> 14% of each run, Pallas kernels for 0% -> 23%
where the time goes in v1:
time: 743 us; the launch traced here: 732 us
  Pallas kernels  378 us (51%)
  matrix products  135 us (18%)
  local copies, waits for them, and re-layouts  93.6 us (13%)
  blocking collectives  51.8 us (7%)
  other arithmetic  32.8 us (4%)
  between operations  15.8 us (2%)
  starting transfers between devices  13.9 us (2%)
  waiting for transfers between devices  12 us (2%)
    pallas_call x1, Pallas kernels, gather_panels(): pl.pallas_call(functools.partial(gather_kernel, panels, lines, 3), out_sh...  171 us
    pallas_call x1, Pallas kernels, reduce_panels(): pl.pallas_call(functools.partial(reduce_kernel, panels, lines), out_shape...  163 us
    dot_general x9, matrix products, times_transposed(): lax.dot_general(left, right, (((1,), (1,)), ((), ())), preferred_element_...  64.7 us
    psum x1, blocking collectives, local(): norm_grad = lax.psum(norm_local, ('grp', 'seq'))  51.8 us
    unnamed x190, local copies, waits for them, and re-layouts  40.9 us
    dot_general x9, matrix products, matmul(): return jnp.dot(left, right, preferred_element_type=F32)  35.5 us
    dot_general x17, matrix products, contract_rows(): lax.dot_general(left, right, (((0,), (0,)), ((), ())), preferred_element_...  34.3 us
    pallas_call x1, Pallas kernels, attend_back(): pl.pallas_call(functools.partial(attend_back_kernel, tok_dev), grid=(HEAD...  27.3 us
  transfers between devices with their start and end apart: 7, of which 1 were waited for; matrix products, arithmetic and copies ran while one was open for 14% of the time, Pallas kernels for 23%

profile of v1, /device:TPU:0, one launch (start us, length us, event | category | flops | bytes accessed | tf_op | source)
XLA Modules:
  0.0 732.3 jit_solution(9302031380939679243)
XLA Ops:
  12.1 5.3 all-to-all-start
  25.4 11.3 %all-to-all-done = bf16[4,6,128,256]{2,3,1,0:T(8,128)(2,1)S(1)} async-done(((bf16[4,6,128,256]{2,3,1,0:T(8,128)(2,1)}), bf16[4,6,128,256]{2,3,1,0:T(8,128)(2,1)S(1)}, u32[]{:S(2)}, u32[]{:S(2)}) %all-to-all-start) | async-done | bytes 1572896 | tf_op jit(solution)/shard_map/all_to_all | solution.py:559
  41.2 171.0 %gather_panels.1 = bf16[15,2,2,2,128,1024]{5,4,3,2,1,0:T(8,128)(2,1)} custom-call(bf16[15,128,256]{2,1,0:T(8,128)(2,1)} %gather_fusion), custom_call_target="tpu_custom_call" | custom-call | tf_op jit(solution)/shard_map/gather_panels/pallas_call | solution.py:214
  212.2 6.5 slice.105
  218.7 5.7 fusion.80
  227.7 11.9 %fusion.79 = (bf16[4,2,2,2,128,1024]{5,4,3,2,1,0:T(8,128)(2,1)}, bf16[4,2,2,2,128,1024]{5,4,3,2,1,0:T(8,128)(2,1)}) fusion(bf16[15,2,2,2,128,1024]{5,4,3,2,1,0:T(8,128)(2,1)} %gather_panels.1), kind=kLoop, calls=%fused_computation.174 | loop fusion | bytes 33554432 | tf_op jit(solution)/shard_map/slice | solution.py:564
  249.4 5.0 convolution_convert_fusion.vr_ref
  260.0 8.3 %reshape.248 = bf16[768,3072]{1,0:T(8,128)(2,1)} reshape(bf16[2304,1024]{1,0:T(8,128)(2,1)} %fusion.5) | data formatting | bytes 9437184 | tf_op jit(solution)/shard_map/reshape | solution.py:590
  268.3 8.7 %convolution_convert_fusion.17 = bf16[768,1024]{1,0:T(8,128)(2,1)S(1)} fusion(bf16[768,3072]{1,0:T(8,128)(2,1)} %reshape.248, bf16[3072,1024]{1,0:T(8,128)(2,1)} %bitcast.105), kind=kOutput, calls=%fused_computation.71 | convolution fusion | flops 4832624640 | bytes 12582912 | tf_op jit(solution)/shard_map/dot_general | solution.py:61
  281.8 16.4 %attend.1 = (f32[384,1024]{1,0:T(8,128)S(1)}, f32[8,8,384]{2,1,0:T(8,128)S(1)}) custom-call(bf16[384,1024]{1,0:T(8,128)(2,1)S(1)} %copy-done.8, bf16[1536,1024]{1,0:T(8,128)(2,1)S(1)} %convolution_convert_fusion.1.kr_ref, bf16[1536,1024]{1,0:T(8,128)(2,1)S(1)} %copy-done.1, bf16[768,1024]{1,0:T(8,128)(2,1)S(1)} %convolution_convert_fusion.16.kc_ref, ...), custom_call_target="tpu_custom_call" | custom-call | tf_op jit(solution)/shard_map/attend/pallas_call | solution.py:455
  300.1 23.7 %multiply_convert_fusion = (bf16[384,4096]{1,0:T(8,128)(2,1)}, f32[384,4096]{1,0:T(8,128)}) fusion(bf16[384,1024]{1,0:T(8,128)(2,1)S(1)} %add_convert_fusion.3, bf16[4096,1024]{1,0:T(8,128)(2,1)} %bitcast.119), kind=kOutput, calls=%fused_computation.28 | convolution fusion | flops 3235381248 | bytes 18612224 | tf_op jit(solution)/shard_map/dot_general | solution.py:65
  323.8 12.6 %fusion.18 = bf16[384,4096]{1,0:T(8,128)(2,1)S(1)} fusion(f32[384,4096]{1,0:T(8,128)} %get-tuple-element.64, bf16[4096,1024]{1,0:T(8,128)(2,1)S(1)} %bitcast.115, bf16[384,1024]{1,0:T(8,128)(2,1)S(1)} %copy-done.31, f32[384]{0:T(512)S(1)} %fusion.61), kind=kOutput, calls=%fused_computation.27 | convolution fusion | flops 3253862400 | bytes 18613760 | tf_op jit(solution)/shard_map/dot_general | solution.py:65
  336.4 7.3 multiply_reduce_fusion
  351.9 27.3 %attend_back.1 = (bf16[384,1024]{1,0:T(8,128)(2,1)S(1)}, bf16[1536,1024]{1,0:T(8,128)(2,1)S(1)}, bf16[1536,1024]{1,0:T(8,128)(2,1)}, bf16[768,1024]{1,0:T(8,128)(2,1)S(1)}, bf16[768,1024]{1,0:T(8,128)(2,1)S(1)}) custom-call(bf16[384,1024]{1,0:T(8,128)(2,1)S(1)} %copy-done.9, bf16[1536,1024]{1,0:T(8,128)(2,1)} %copy-done, ...), custom_call_target="tpu_custom_call" | custom-call | tf_op jit(solution)/shard_map/attend_back/pallas_call | solution.py:519
  379.2 5.4 fusion.87
  384.7 5.5 fusion.90
  404.0 6.6 fusion.91
  410.6 7.4 %fusion.86 = (bf16[1536,1024]{1,0:T(8,128)(2,1)S(1)}, f32[1536,1024]{1,0:T(8,128)}) fusion(f32[1536,1024]{1,0:T(8,128)} %fusion.87, bf16[1536,1024]{1,0:T(8,128)(2,1)S(1)} %copy-done.72, bf16[1024,1024]{1,0:T(8,128)(2,1)S(1)} %bitcast.141), kind=kOutput, calls=%fused_computation.181 | convolution fusion | flops 3224371200 | bytes 20971520 | tf_op jit(solution)/shard_map/dot_general | solution.py:65
  464.9 5.1 fusion.89
  471.6 4.7 fusion.33
  483.1 163.2 %reduce_panels.1 = bf16[15,128,256]{2,1,0:T(8,128)(2,1)} custom-call(bf16[15,2,2,2,128,1024]{5,4,3,2,1,0:T(8,128)(2,1)} %constant_dynamic-update-slice_fusion.grad_ref), custom_call_target="tpu_custom_call" | custom-call | tf_op jit(solution)/shard_map/reduce_panels/pallas_call | solution.py:362
  652.7 4.5 all-to-all-start.1
  658.0 51.8 %psum.7 = f32[4,1024]{1,0:T(4,128)S(1)} all-reduce(f32[4,1024]{1,0:T(4,128)S(1)} %pad_maximum_fusion), channel_id=1, replica_groups=mesh['grp'=4,'seq'=8] {'grp','seq'}, use_global_device_ids=true, to_apply=%region_24.25 | all-reduce | flops 4096 | bytes 32768 | tf_op jit(solution)/shard_map/psum | solution.py:643
  720.4 4.6 multiply_subtract_fusion
  (294 shorter events, 136.7 us)
Async XLA Ops:
  7.2 232.4 %all-gather.2.cloned.1.call-start = ((), (), s32[]{:S(2)}) async-start(), calls=%async_computation.3 | async-start | bytes 7077888 | tf_op jit(solution)/shard_map/all_gather | solution.py:579
  12.1 24.5 %all-to-all-start = ((bf16[4,6,128,256]{2,3,1,0:T(8,128)(2,1)}), bf16[4,6,128,256]{2,3,1,0:T(8,128)(2,1)S(1)}, u32[]{:S(2)}, u32[]{:S(2)}) async-start(bf16[4,6,128,256]{2,3,1,0:T(8,128)(2,1)} %copy.34), calls=%async_computation | async-start | bytes 3145728 | tf_op jit(solution)/shard_map/all_to_all | solution.py:559
  17.4 447.5 %reduce-scatter.2.cloned.1.call-start = ((), (), s32[]{:S(2)}) async-start(), calls=%async_computation.4 | async-start | bytes 2359296 | tf_op jit(solution)/shard_map/reduce_scatter | solution.py:629
  19.4 237.1 %copy-start.56 = (f32[1,1024]{1,0:T(1,128)}, f32[1,1024]{1,0:T(1,128)S(1)}, u32[]{:S(2)}) copy-start(f32[1,1024]{1,0:T(1,128)S(1)} %get-tuple-element.59) | copy-start | bytes 12292
  19.8 204.7 %copy-start.29 = (bf16[384,1024]{1,0:T(8,128)(2,1)}, bf16[384,1024]{1,0:T(8,128)(2,1)S(1)}, u32[]{:S(2)}) copy-start(bf16[384,1024]{1,0:T(8,128)(2,1)S(1)} %fusion.30) | copy-start | bytes 2359300
  249.3 31.7 %copy-start = (bf16[1536,1024]{1,0:T(8,128)(2,1)}, bf16[1536,1024]{1,0:T(8,128)(2,1)S(1)}, u32[]{:S(2)}) copy-start(bf16[1536,1024]{1,0:T(8,128)(2,1)S(1)} %convolution_convert_fusion.1.kr_ref) | copy-start | bytes 9437188
  281.8 16.5 %copy-start.49 = (bf16[1,2,2,2,128,1024]{5,4,3,2,1,0:T(8,128)(2,1)S(1)}, bf16[1,2,2,2,128,1024]{5,4,3,2,1,0:T(8,128)(2,1)}, u32[]{:S(2)}) copy-start(bf16[1,2,2,2,128,1024]{5,4,3,2,1,0:T(8,128)(2,1)} %get-tuple-element.46) | copy-start | bytes 6291460
  298.3 47.4 %copy-start.2 = (f32[384,1024]{1,0:T(8,128)}, f32[384,1024]{1,0:T(8,128)S(1)}, u32[]{:S(2)}) copy-start(f32[384,1024]{1,0:T(8,128)S(1)} %get-tuple-element.19) | copy-start | bytes 4718596
  299.4 44.4 %copy-start.22 = (f32[384,1024]{1,0:T(8,128)}, f32[384,1024]{1,0:T(8,128)S(1)}, u32[]{:S(2)}) copy-start(f32[384,1024]{1,0:T(8,128)S(1)} %get-tuple-element.62) | copy-start | bytes 4718596
  299.7 24.0 %slice-start = ((s8[8388608]{0:T(1024)(128)(4,1)}), s8[4194304]{0:T(1024)(128)(4,1)S(1)}, s32[]{:S(2)}) async-start(s8[8388608]{0:T(1024)(128)(4,1)} %bitcast.113), calls=%async_computation.5 | async-start | bytes 8388608
  300.1 23.7 %copy-start.53 = (bf16[384,1024]{1,0:T(8,128)(2,1)}, bf16[384,1024]{1,0:T(8,128)(2,1)S(1)}, u32[]{:S(2)}) copy-start(bf16[384,1024]{1,0:T(8,128)(2,1)S(1)} %add_convert_fusion.3) | copy-start | bytes 2359300
  300.1 23.7 %slice-start.1 = ((s8[8388608]{0:T(1024)(128)(4,1)}), s8[4194304]{0:T(1024)(128)(4,1)S(1)}, s32[]{:S(2)}) async-start(s8[8388608]{0:T(1024)(128)(4,1)} %bitcast.113), calls=%async_computation.6 | async-start | bytes 8388608
  300.1 23.7 %copy-start.31 = (bf16[384,1024]{1,0:T(8,128)(2,1)S(1)}, bf16[384,1024]{1,0:T(8,128)(2,1)}, u32[]{:S(2)}) copy-start(bf16[384,1024]{1,0:T(8,128)(2,1)} %param.13) | copy-start | bytes 2359300
  351.9 27.3 %copy-start.48 = (bf16[1,2,2,2,128,1024]{5,4,3,2,1,0:T(8,128)(2,1)S(1)}, bf16[1,2,2,2,128,1024]{5,4,3,2,1,0:T(8,128)(2,1)}, u32[]{:S(2)}) copy-start(bf16[1,2,2,2,128,1024]{5,4,3,2,1,0:T(8,128)(2,1)} %get-tuple-element.47) | copy-start | bytes 6291460
  379.2 18.4 %copy-start.16 = (bf16[768,1024]{1,0:T(8,128)(2,1)}, bf16[768,1024]{1,0:T(8,128)(2,1)S(1)}, u32[]{:S(2)}) copy-start(bf16[768,1024]{1,0:T(8,128)(2,1)S(1)} %get-tuple-element.24) | copy-start | bytes 4718596
  379.2 21.8 %copy-start.14 = (bf16[768,1024]{1,0:T(8,128)(2,1)}, bf16[768,1024]{1,0:T(8,128)(2,1)S(1)}, u32[]{:S(2)}) copy-start(bf16[768,1024]{1,0:T(8,128)(2,1)S(1)} %get-tuple-element.25) | copy-start | bytes 4718596
  419.5 52.0 %collective-permute-start.2 = (bf16[384,1024]{1,0:T(8,128)(2,1)}, bf16[384,1024]{1,0:T(8,128)(2,1)}, u32[]{:S(2)}, u32[]{:S(2)}) collective-permute-start(bf16[384,1024]{1,0:T(8,128)(2,1)} %get-tuple-element.50), channel_id=1, source_target_pairs={{3,0},{4,1},{5,2},{6,3},{7,4},{11,8},{12,9},{13,10},{14,11},{15,12... | collective-permute-start | bytes 2359304 | tf_op jit(solution)/shard_map/ppermute | solution.py:635
  420.8 50.7 %collective-permute-start.1 = (bf16[384,1024]{1,0:T(8,128)(2,1)}, bf16[384,1024]{1,0:T(8,128)(2,1)}, u32[]{:S(2)}, u32[]{:S(2)}) collective-permute-start(bf16[384,1024]{1,0:T(8,128)(2,1)} %get-tuple-element.51), channel_id=1, source_target_pairs={{2,0},{3,1},{4,2},{5,3},{6,4},{7,5},{10,8},{11,9},{12,10},{13,11},... | collective-permute-start | bytes 2359304 | tf_op jit(solution)/shard_map/ppermute | solution.py:635
  422.1 49.4 %collective-permute-start = (bf16[384,1024]{1,0:T(8,128)(2,1)}, bf16[384,1024]{1,0:T(8,128)(2,1)}, u32[]{:S(2)}, u32[]{:S(2)}) collective-permute-start(bf16[384,1024]{1,0:T(8,128)(2,1)} %get-tuple-element.49), channel_id=1, source_target_pairs={{1,0},{2,1},{3,2},{4,3},{5,4},{6,5},{7,6},{9,8},{10,9},{11,10},{12... | collective-permute-start | bytes 2359304 | tf_op jit(solution)/shard_map/ppermute | solution.py:635
  652.7 57.2 %copy-start.61 = (f32[4,1024]{1,0:T(4,128)S(1)}, f32[4,1024]{1,0:T(4,128)}, u32[]{:S(2)}) copy-start(f32[4,1024]{1,0:T(4,128)} %param.17) | copy-start | bytes 49156
  652.7 57.2 %copy-start.67 = (f32[4,1024]{1,0:T(4,128)S(1)}, f32[4,1024]{1,0:T(4,128)}, u32[]{:S(2)}) copy-start(f32[4,1024]{1,0:T(4,128)} %param.19) | copy-start | bytes 49156
  652.7 57.2 %copy-start.68 = (f32[4,1024]{1,0:T(4,128)S(1)}, f32[4,1024]{1,0:T(4,128)}, u32[]{:S(2)}) copy-start(f32[4,1024]{1,0:T(4,128)} %param.18) | copy-start | bytes 49156
  652.7 58.5 %copy-start.33 = (bf16[384,1024]{1,0:T(8,128)(2,1)S(1)}, bf16[384,1024]{1,0:T(8,128)(2,1)}, u32[]{:S(2)}) copy-start(bf16[384,1024]{1,0:T(8,128)(2,1)} %param.13) | copy-start | bytes 2359300
  652.7 61.8 %all-to-all-start.1 = ((bf16[4,6,128,256]{3,2,1,0:T(8,128)(2,1)}), bf16[4,6,128,256]{3,2,1,0:T(8,128)(2,1)}, u32[]{:S(2)}, u32[]{:S(2)}) async-start(bf16[4,6,128,256]{3,2,1,0:T(8,128)(2,1)} %fusion.21), calls=%async_computation.2 | async-start | bytes 3145728 | tf_op jit(solution)/shard_map/all_to_all | solution.py:660
  (70 other events, 276.1 us)
Sparse Core Ops, SparseCore 0:
  9.7 104.6 all-gather.1
  404.1 47.4 reduce-scatter.1

commit v2 on v1

--- a/solution.py
+++ b/solution.py
@@ -108,129 +108,6 @@
         device_id=device,
         device_id_type=MESH,
     )
-
-
-def gather_kernel(panels, lines, ahead, block_ref, full_ref, own_sem, zs, zr, s1, r1, s2, r2, cs, cr):
-    at = Place(lines)
-    wide = block_ref.shape[-1]
-
-    def cols(g):
-        return pl.ds(pl.multiple_of(g * wide, wide), wide)
-
-    def line_copy(p, k):
-        dst = full_ref.at[p, at.line // 2, at.line % 2, at.core, :, cols(at.grp)]
-        return remote(block_ref.at[p], dst, zs.at[p, k], zr.at[p, at.line], at.line_dev(k))
-
-    def line_arrival(p, k):
-        z = at.other_line(k)
-        dst = full_ref.at[p, z // 2, z % 2, at.core, :, cols(at.grp)]
-        return remote(block_ref.at[p], dst, zs.at[p, k], zr.at[p, z], at.line_dev(k))
-
-    def part(p, h, g):
-        return full_ref.at[p, :, h, at.core, :, cols(g)]
-
-    def first(p, h, g):
-        device = at.x_dev if h == 0 else at.y_dev
-        return remote(part(p, h, g), part(p, h, g), s1.at[p, h], r1.at[p, h], device)
-
-    def second(p, h, j, g):
-        device = at.y_dev if h == 0 else at.x_dev
-        return remote(part(p, h, g), part(p, h, g), s2.at[p, h, j], r2.at[p, h, j], device)
-
-    def cross(p, h, core):
-        ref = full_ref.at[p, :, h, core]
-        return remote(ref, ref, cs.at[p, h], cr.at[p, h], at.core_dev)
-
-    def start_lines(p):
-        for k in range(1, lines):
-            line_copy(p, k).start()
-
-    def start_first(p):
-        for k in range(1, lines):
-            line_arrival(p, k).wait_recv()
-        for h in (0, 1):
-            first(p, h, at.grp).start()
-
-    def start_second(p):
-        for h in (0, 1):
-            near = at.grp_x if h == 0 else at.grp_y
-            first(p, h, near).wait_recv()
-            second(p, h, 0, at.grp).start()
-            second(p, h, 1, near).start()
-
-    def start_cross(p):
-        for h in (0, 1):
-            second(p, h, 0, at.grp_y if h == 0 else at.grp_x).wait_recv()
-            second(p, h, 1, 3 - at.grp).wait_recv()
-            cross(p, h, at.core).start()
-
-    def finish(p):
-        for h in (0, 1):
-            cross(p, h, 1 - at.core).wait_recv()
-            first(p, h, at.grp).wait_send()
-            second(p, h, 0, at.grp).wait_send()
-            second(p, h, 1, at.grp_x if h == 0 else at.grp_y).wait_send()
-            cross(p, h, at.core).wait_send()
-        for k in range(1, lines):
-            line_copy(p, k).wait_send()
-
-    at.enter()
-    own_place = full_ref.at[:, at.line // 2, at.line % 2, at.core, :, cols(at.grp)]
-    own = pltpu.make_async_copy(block_ref, own_place, own_sem)
-    own.start()
-    for p in range(ahead):
-        start_lines(p)
-    own.wait()
-
-    def step(t, carry):
-        @pl.when(t + ahead < panels)
-        def _():
-            start_lines(t + ahead)
-
-        @pl.when(t < panels)
-        def _():
-            start_first(t)
-
-        @pl.when((t >= 1) & (t < panels + 1))
-        def _():
-            start_second(t - 1)
-
-        @pl.when((t >= 2) & (t < panels + 2))
-        def _():
-            start_cross(t - 2)
-
-        @pl.when(t >= 3)
-        def _():
-            finish(t - 3)
-
-        return carry
-
-    lax.fori_loop(0, panels + 3, step, 0)
-
-
-def gather_panels(block, lines):
-    panels, rows, wide = block.shape
-    dma = pltpu.SemaphoreType.DMA
-    full = pl.pallas_call(
-        functools.partial(gather_kernel, panels, lines, 3),
-        out_shape=jax.ShapeDtypeStruct((panels, lines // 2, 2, 2, rows, 4 * wide), BF16),
-        in_specs=[pl.BlockSpec(memory_space=pl.ANY)],
-        out_specs=pl.BlockSpec(memory_space=pl.ANY),
-        scratch_shapes=[
-            dma(()),
-            dma((panels, lines)),
-            dma((panels, lines)),
-            dma((panels, 2)),
-            dma((panels, 2)),
-            dma((panels, 2, 2)),
-            dma((panels, 2, 2)),
-            dma((panels, 2)),
-            dma((panels, 2)),
-        ],
-        compiler_params=pltpu.CompilerParams(collective_id=0, has_side_effects=True),
-        name="gather_panels",
-    )(block)
-    return full.reshape(panels, D, D)
 
 
 def reduce_kernel(
@@ -387,24 +264,41 @@
     )(grads.reshape(panels, pairs, 2, 2, rows, D))
 
 
-def key_window(seq, tok_dev):
-    first_pos = seq * tok_dev
-    memory = (first_pos // S - 1) * S
-    raw_first = seq - (RAW_KEYS - QB + tok_dev - 1) // tok_dev
-    comp_first = jnp.maximum(jnp.floor_divide(memory - 3 * CM, tok_dev), 0)
-    return raw_first, comp_first
+def memory_start(position):
+    return (position // S - 1) * S
+
+
+def comp_window_first(seq, tok_dev):
+    return jnp.maximum(memory_start(seq * tok_dev) - 3 * CM, 0) // tok_dev
+
+
+def raw_devices(tok_dev):
+    return (RAW_KEYS - QB + tok_dev - 1) // tok_dev + 1
+
+
+def comp_devices(tok_dev, seq_count):
+    return min((3 * CM + S) // tok_dev + 1, seq_count)
+
+
+def needs_raw(reader, owner, tok_dev):
+    return (owner >= 0) & ((owner + 1) * tok_dev > memory_start(reader * tok_dev))
+
+
+def needs_comp(reader, owner, tok_dev):
+    last = jnp.maximum(memory_start(reader * tok_dev + tok_dev - 1), 0) // 3
+    inside = (owner >= 0) & (owner >= comp_window_first(reader, tok_dev))
+    return inside & (owner * (tok_dev // 3) < last)
 
 
 def block_window(seq, i, tok_dev, raw_rows, comp_rows):
     position = seq * tok_dev + i * QB
-    memory = (position // S - 1) * S
-    raw_first, comp_first = key_window(seq, tok_dev)
-    raw_base = raw_first * tok_dev
+    memory = memory_start(position)
+    raw_base = (seq + 1) * tok_dev - raw_rows
     raw_at = jnp.minimum(memory - raw_base, raw_rows - RAW_KEYS)
-    comp_end = jnp.floor_divide(memory, 3)
+    comp_end = jnp.maximum(memory, 0) // 3
     comp_low = jnp.maximum(comp_end - CM, 0)
-    comp_base = comp_first * (tok_dev // 3)
-    comp_at = jnp.clip((comp_low - comp_base) // QB * QB, 0, comp_rows - COMP_KEYS)
+    comp_base = comp_window_first(seq, tok_dev) * (tok_dev // 3)
+    comp_at = jnp.minimum((comp_low - comp_base) // QB * QB, comp_rows - COMP_KEYS)
     return (
         position,
         pl.multiple_of(raw_at, QB),
@@ -417,53 +311,419 @@
     )
 
 
-def attend_kernel(tok_dev, q_ref, kr_ref, vr_ref, kc_ref, vc_ref, o_ref, lse_ref):
-    seq = lax.axis_index("seq")
+def row_sum(values):
+    return jnp.sum(values, axis=1, keepdims=True)
+
+
+def norm_rows(values, params, first):
+    mean = row_sum(values) * (1.0 / D)
+    centered = values - mean
+    variance = row_sum(centered * centered) * (1.0 / D)
+    gain, shift = params[first : first + 1, :], params[first + 1 : first + 2, :]
+    return centered * lax.rsqrt(variance + NORM_EPS) * gain + shift
+
+
+GELU_IN = (2.0 / 3.141592653589793) ** 0.5
+GELU_CUBE = 0.044715
+
+
+def gelu_pair(f):
+    square = f * f
+    t = jnp.tanh(GELU_IN * f * (1.0 + GELU_CUBE * square))
+    half = 0.5 * (1.0 + t)
+    slope = half + 0.5 * f * (1.0 - t * t) * (GELU_IN * (1.0 + 3.0 * GELU_CUBE * square))
+    return f * half, slope
+
+
+class Attention:
+    def __init__(self, seq, i, tok_dev, raw_rows, comp_rows):
+        place = block_window(seq, i, tok_dev, raw_rows, comp_rows)
+        self.pos, raw_at, comp_at, self.raw_pos, self.comp_pos = place[:5]
+        self.memory, self.comp_low, self.comp_end = place[5:]
+        self.rows = pl.ds(i * QB, QB)
+        self.raw = pl.ds(raw_at, RAW_KEYS)
+        self.comp = pl.ds(comp_at, COMP_KEYS)
+
+    def sees_raw(self, shape, key_dim):
+        key_pos = self.raw_pos + lax.broadcasted_iota(jnp.int32, shape, key_dim)
+        query_pos = self.pos + lax.broadcasted_iota(jnp.int32, shape, 1 - key_dim)
+        return (key_pos >= jnp.maximum(self.memory, 0)) & (key_pos <= query_pos)
+
+    def sees_comp(self, shape, key_dim):
+        index = self.comp_pos + lax.broadcasted_iota(jnp.int32, shape, key_dim)
+        return (index >= self.comp_low) & (index < self.comp_end)
+
+
+def attend_head(seq, tok_dev, cols, q, kr, vr, kc, vc, out, lse, lse_row):
     scale = HEAD_DIM ** (-0.5)
     for i in range(tok_dev // QB):
-        pos, raw_at, comp_at, raw_pos, comp_pos, memory, comp_low, comp_end = block_window(
-            seq, i, tok_dev, kr_ref.shape[0], kc_ref.shape[0]
-        )
-        q = q_ref[pl.ds(i * QB, QB), :]
-        raw = times_transposed(q, kr_ref[pl.ds(raw_at, RAW_KEYS), :]) * scale
-        key_pos = raw_pos + lax.broadcasted_iota(jnp.int32, (QB, RAW_KEYS), 1)
-        query_pos = pos + lax.broadcasted_iota(jnp.int32, (QB, RAW_KEYS), 0)
-        seen = (key_pos >= jnp.maximum(memory, 0)) & (key_pos <= query_pos)
-        raw = jnp.where(seen, raw, NEG_SCORE)
-        comp = times_transposed(q, kc_ref[pl.ds(comp_at, COMP_KEYS), :]) * scale
-        comp_idx = comp_pos + lax.broadcasted_iota(jnp.int32, (QB, COMP_KEYS), 1)
-        comp = jnp.where((comp_idx >= comp_low) & (comp_idx < comp_end), comp, NEG_SCORE)
+        at = Attention(seq, i, tok_dev, kr.shape[0], kc.shape[0])
+        query = q[at.rows, cols]
+        raw = times_transposed(query, kr[at.raw, cols]) * scale
+        raw = jnp.where(at.sees_raw(raw.shape, 1), raw, NEG_SCORE)
+        comp = times_transposed(query, kc[at.comp, cols]) * scale
+        comp = jnp.where(at.sees_comp(comp.shape, 1), comp, NEG_SCORE)
         top = jnp.maximum(
             jnp.max(raw, axis=1, keepdims=True), jnp.max(comp, axis=1, keepdims=True)
         )
         raw = jnp.exp(raw - top)
         comp = jnp.exp(comp - top)
-        total = jnp.sum(raw, axis=1, keepdims=True) + jnp.sum(comp, axis=1, keepdims=True)
-        out = matmul(raw.astype(BF16), vr_ref[pl.ds(raw_at, RAW_KEYS), :])
-        out = out + matmul(comp.astype(BF16), vc_ref[pl.ds(comp_at, COMP_KEYS), :])
-        o_ref[pl.ds(i * QB, QB), :] = out / total
-        lse = jnp.broadcast_to(top + jnp.log(total), (QB, QB))
-        lse_ref[0, :, pl.ds(i * QB, QB)] = lse.T[:8]
-
-
-def attend(q, kr, vr, kc, vc):
-    tok_dev = q.shape[0]
-
-    def head(rows):
-        return pl.BlockSpec((rows, HEAD_DIM), lambda h: (0, h))
-
+        total = row_sum(raw) + row_sum(comp)
+        mixed = matmul(raw.astype(BF16), vr[at.raw, cols])
+        mixed = mixed + matmul(comp.astype(BF16), vc[at.comp, cols])
+        out[at.rows, cols] = mixed / total
+        stat = jnp.broadcast_to(top + jnp.log(total), (QB, QB))
+        lse[lse_row, :, at.rows] = stat.T[:8]
+
+
+TAPS = [4 + 2 * RATIO + i for i in range(3)]
+ARRIVAL = TAPS + [1, 2, 0, 3]
+for _i in range(RATIO):
+    ARRIVAL = ARRIVAL + [4 + _i, 4 + RATIO + _i]
+LAG = 4
+
+
+def forward_kernel(
+    panels, lines, ahead,
+    block_ref, tok_ref, tok3_ref, dy_ref, valid_ref, norm_ref,
+    full_ref, a_out, c_out, q_out, kr_out, vr_out, kc_out, vc_out, o_out, z_out, df_out, b_out,
+    h_out, db_out, lse_ref, mixed_ref,
+    wbuf, a_win, a3, c_win, q, kr, vr, kc, vc, o, z, df, b, h, y, db,
+    own_sem, zs, zr, s1, r1, s2, r2, cs, cr, wsem, a_s, a_r, c_s, c_r, out_sem,
+):
+    at = Place(lines)
+    seq = at.seq
+    seq_count = 2 * lines
+    tok_dev = tok_ref.shape[0]
+    comp_dev = tok_dev // 3
+    raw_devs = a_win.shape[0] // tok_dev
+    comp_devs = c_win.shape[0] // comp_dev
+    reach = min(seq_count - 1, (2 * S + 3 * CM + tok_dev - 1) // tok_dev)
+    wide = block_ref.shape[-1]
+
+    def cols(g):
+        return pl.ds(pl.multiple_of(g * wide, wide), wide)
+
+    def line_copy(p, k):
+        dst = full_ref.at[p, at.line // 2, at.line % 2, at.core, :, cols(at.grp)]
+        return remote(block_ref.at[p], dst, zs.at[p, k], zr.at[p, at.line], at.line_dev(k))
+
+    def line_arrival(p, k):
+        line = at.other_line(k)
+        dst = full_ref.at[p, line // 2, line % 2, at.core, :, cols(at.grp)]
+        return remote(block_ref.at[p], dst, zs.at[p, k], zr.at[p, line], at.line_dev(k))
+
+    def part(p, half, g):
+        return full_ref.at[p, :, half, at.core, :, cols(g)]
+
+    def first(p, half, g):
+        device = at.x_dev if half == 0 else at.y_dev
+        return remote(part(p, half, g), part(p, half, g), s1.at[p, half], r1.at[p, half], device)
+
+    def second(p, half, j, g):
+        device = at.y_dev if half == 0 else at.x_dev
+        ref = part(p, half, g)
+        return remote(ref, ref, s2.at[p, half, j], r2.at[p, half, j], device)
+
+    def cross(p, half, core):
+        ref = full_ref.at[p, :, half, core]
+        return remote(ref, ref, cs.at[p, half], cr.at[p, half], at.core_dev)
+
+    def load(p):
+        slot = lax.rem(p, wbuf.shape[0])
+        return pltpu.make_async_copy(full_ref.at[p], wbuf.at[slot], wsem.at[slot])
+
+    def start_lines(p):
+        for k in range(1, lines):
+            line_copy(p, k).start()
+
+    def start_first(p):
+        for k in range(1, lines):
+            line_arrival(p, k).wait_recv()
+        for half in (0, 1):
+            first(p, half, at.grp).start()
+
+    def start_second(p):
+        for half in (0, 1):
+            near = at.grp_x if half == 0 else at.grp_y
+            first(p, half, near).wait_recv()
+            second(p, half, 0, at.grp).start()
+            second(p, half, 1, near).start()
+
+    def start_cross(p):
+        for half in (0, 1):
+            second(p, half, 0, at.grp_y if half == 0 else at.grp_x).wait_recv()
+            second(p, half, 1, 3 - at.grp).wait_recv()
+            cross(p, half, at.core).start()
+
+    def finish(p):
+        for half in (0, 1):
+            cross(p, half, 1 - at.core).wait_recv()
+            first(p, half, at.grp).wait_send()
+            second(p, half, 0, at.grp).wait_send()
+            second(p, half, 1, at.grp_x if half == 0 else at.grp_y).wait_send()
+            cross(p, half, at.core).wait_send()
+        for k in range(1, lines):
+            line_copy(p, k).wait_send()
+        load(p).start()
+
+    def seq_dev(d):
+        return {"grp": at.grp, "seq": lax.rem(seq + d + seq_count, seq_count)}
+
+    def a_rows(d):
+        return a_win.at[pl.ds((raw_devs - 1 - d) * tok_dev, tok_dev), :]
+
+    def a_copy(d):
+        return remote(a_rows(0), a_rows(d), a_s.at[d], a_r.at[d], seq_dev(d))
+
+    def c_rows(reader, owner):
+        place = owner - comp_window_first(reader, tok_dev)
+        place = jnp.clip(place, 0, comp_devs - 1)
+        return c_win.at[pl.ds(pl.multiple_of(place * comp_dev, comp_dev), comp_dev), :]
+
+    def c_copy(d, own_c):
+        return remote(own_c, c_rows(seq + d, seq), c_s.at[d], c_r.at[d], seq_dev(d))
+
+    def c_arrival(d, own_c):
+        return remote(own_c, c_rows(seq, seq - d), c_s.at[d], c_r.at[d], seq_dev(-d))
+
+    def reads_a(d):
+        return (seq + d < seq_count) & needs_raw(seq + d, seq, tok_dev)
+
+    def reads_c(d):
+        return (seq + d < seq_count) & needs_comp(seq + d, seq, tok_dev)
+
+    outs = [
+        (a_win, a_out), (c_win, c_out), (q, q_out), (kr, kr_out), (vr, vr_out), (kc, kc_out),
+        (vc, vc_out), (o, o_out), (z, z_out), (df, df_out), (b, b_out), (h, h_out), (db, db_out),
+    ]
+
+    def flush(*names):
+        for i, (src, dst) in enumerate(outs):
+            if any(src is name for name in names):
+                pltpu.make_async_copy(src, dst, out_sem.at[i]).start()
+
+    barrier = pltpu.get_barrier_semaphore()
+    partners = [seq_dev(d) for d in range(1, seq_count)] + [at.x_dev, at.y_dev]
+    for device in partners:
+        pl.semaphore_signal(barrier, inc=1, device_id=device, device_id_type=MESH)
+    pl.semaphore_wait(barrier, seq_count + 1)
+
+    own_place = full_ref.at[:, at.line // 2, at.line % 2, at.core, :, cols(at.grp)]
+    own = pltpu.make_async_copy(block_ref, own_place, own_sem)
+    own.start()
+    for p in range(ahead):
+        start_lines(p)
+
+    params = norm_ref[...]
+    a_win[pl.ds((raw_devs - 1) * tok_dev, tok_dev), :] = norm_rows(
+        tok_ref[...].astype(F32), params, 0
+    ).astype(BF16)
+    for d in range(1, raw_devs):
+        pl.when(reads_a(d))(lambda d=d: a_copy(d).start())
+        absent = jnp.logical_not(needs_raw(seq, seq - d, tok_dev))
+
+        @pl.when(absent)
+        def _(d=d):
+            a_rows(d)[...] = jnp.zeros((tok_dev, D), BF16)
+
+    for k in range(3):
+        a3[k] = norm_rows(tok3_ref[k].astype(F32), params, 0).astype(BF16)
+    for i in range(comp_devs):
+        owner = comp_window_first(seq, tok_dev) + i
+        absent = jnp.logical_not(needs_comp(seq, owner, tok_dev))
+
+        @pl.when(absent)
+        def _(i=i):
+            c_win[pl.ds(i * comp_dev, comp_dev), :] = jnp.zeros((comp_dev, D), BF16)
+
+    own.wait()
+    own_c = b.at[pl.ds(0, comp_dev), :]
+    tile = 4 * wbuf.shape[4]
+
+    def weight(slot, col):
+        return wbuf[slot, :, :, :, :, col].reshape(D, wide)
+
+    def columns(body):
+        def one(j, carry):
+            body(pl.ds(pl.multiple_of(j * wide, wide), wide))
+            return carry
+
+        lax.fori_loop(0, D // wide, one, 0)
+
+    def tap(k, slot):
+        def body(col):
+            part_sum = matmul(a3[k], weight(slot, col))
+            if k == 0:
+                y[pl.ds(0, comp_dev), col] = part_sum
+            elif k == 1:
+                y[pl.ds(0, comp_dev), col] += part_sum
+            else:
+                own_c[:, col] = (y[pl.ds(0, comp_dev), col] + part_sum).astype(BF16)
+
+        columns(body)
+
+    def project(dst, src, slot):
+        block = min(src.shape[0], tok_dev)
+
+        def body(col):
+            for i in range(src.shape[0] // block):
+                rows = pl.ds(i * block, block)
+                dst[rows, col] = matmul(src[rows, :], weight(slot, col)).astype(BF16)
+
+        columns(body)
+
+    def heads(low, high):
+        def one(i, carry):
+            col = pl.ds(pl.multiple_of(i * HEAD_DIM, HEAD_DIM), HEAD_DIM)
+            attend_head(seq, tok_dev, col, q, kr, vr, kc, vc, o, lse_ref, i)
+            return carry
+
+        lax.fori_loop(low, high, one, 0)
+
+    def work(p):
+        slot = lax.rem(p, wbuf.shape[0])
+        for k in range(3):
+            pl.when(p == k)(lambda k=k: tap(k, slot))
+
+        @pl.when(p == 2)
+        def _():
+            for d in range(1, reach + 1):
+                pl.when(reads_c(d))(lambda d=d: c_copy(d, own_c).start())
+            place = seq - comp_window_first(seq, tok_dev)
+            for d in range(1, raw_devs):
+                pl.when(needs_raw(seq, seq - d, tok_dev))(lambda d=d: a_copy(d).wait_recv())
+                pl.when(reads_a(d))(lambda d=d: a_copy(d).wait_send())
+            flush(a_win)
+
+        @pl.when(p == 3)
+        def _():
+            project(kr, a_win, slot)
+            for d in range(1, reach + 1):
+                pl.when(needs_comp(seq, seq - d, tok_dev))(lambda d=d: c_arrival(d, own_c).wait_recv())
+            project(kc, c_win, slot)
+            flush(c_win, kr, kc)
+
+        @pl.when(p == 4)
+        def _():
+            project(vr, a_win, slot)
+            project(vc, c_win, slot)
+            flush(vr, vc)
+
+        @pl.when(p == 5)
+        def _():
+            project(q, a_win.at[pl.ds((raw_devs - 1) * tok_dev, tok_dev), :], slot)
+            flush(q)
+            heads(0, 2)
+
+        @pl.when(p == 6)
+        def _():
+            heads(2, 5)
+
+        @pl.when(p == 7)
+        def _():
+            heads(5, 8)
+            flush(o)
+            for d in range(1, reach + 1):
+                pl.when(reads_c(d))(lambda d=d: c_copy(d, own_c).wait_send())
+            out_slot = 6 % wbuf.shape[0]
+
+            def body(col):
+                sent = matmul(o[...].astype(BF16), weight(out_slot, col))
+                h[:, col] = tok_ref[:, col].astype(F32) + sent
+
+            columns(body)
+            for i in range(tok_dev // QB):
+                rows = pl.ds(i * QB, QB)
+                b[rows, :] = norm_rows(h[rows, :], params, 2).astype(BF16)
+            y[...] = h[...]
+            db[...] = jnp.zeros_like(db)
+            flush(b, h)
+
+        @pl.when((p >= 8) & (lax.rem(p, 2) == 0))
+        def _():
+            up = lax.rem(p - 1, wbuf.shape[0])
+            base = (p // 2 - 4) * D
+
+            def hidden(i, carry):
+                up_rows = wbuf[up, i].reshape(tile, D)
+                down_rows = wbuf[slot, i].reshape(tile, D)
+                value, slope = gelu_pair(times_transposed(b[...], up_rows))
+                units = pl.ds(pl.multiple_of(base + i * tile, tile), tile)
+                z[:, units] = value.astype(BF16)
+                df[:, units] = (times_transposed(dy_ref[...], down_rows) * slope).astype(BF16)
+                return carry
+
+            lax.fori_loop(0, wbuf.shape[1], hidden, 0)
+            units = pl.ds(pl.multiple_of(base, D), D)
+
+            def body(col):
+                y[:, col] += matmul(z[:, units], weight(slot, col))
+                db[:, col] += matmul(df[:, units], weight(up, col))
+
+            columns(body)
+
+    def step(t, carry):
+        pl.when(t + ahead < panels)(lambda: start_lines(t + ahead))
+        pl.when(t < panels)(lambda: start_first(t))
+        pl.when((t >= 1) & (t < panels + 1))(lambda: start_second(t - 1))
+        pl.when((t >= 2) & (t < panels + 2))(lambda: start_cross(t - 2))
+
+        @pl.when(t >= LAG)
+        def _():
+            load(t - LAG).wait()
+            work(t - LAG)
+
+        pl.when((t >= 3) & (t < panels + 3))(lambda: finish(t - 3))
+        return carry
+
+    lax.fori_loop(0, panels + LAG, step, 0)
+    flush(z, df, db)
+    mixed_ref[...] = (y[...] * valid_ref[...]).astype(BF16)
+    for i, (src, dst) in enumerate(outs):
+        pltpu.make_async_copy(src, dst, out_sem.at[i]).wait()
+
+
+def forward(block, tokens, tokens3, grad_out, valid, norm_params, lines):
+    panels, rows, wide = block.shape
+    tok_dev = tokens.shape[0]
+    raw = raw_devices(tok_dev) * tok_dev
+    comp = comp_devices(tok_dev, 2 * lines) * (tok_dev // 3)
+    dma = pltpu.SemaphoreType.DMA
+    shapes = [
+        ((raw, D), BF16), ((comp, D), BF16), ((tok_dev, D), BF16), ((raw, D), BF16),
+        ((raw, D), BF16), ((comp, D), BF16), ((comp, D), BF16), ((tok_dev, D), F32),
+        ((tok_dev, FF), BF16), ((tok_dev, FF), BF16), ((tok_dev, D), BF16), ((tok_dev, D), F32),
+        ((tok_dev, D), F32),
+    ]
+    scratch = [pltpu.VMEM(shape, kind) for shape, kind in shapes]
+    scratch.insert(1, pltpu.VMEM((3, tok_dev // 3, D), BF16))
+    scratch.insert(len(scratch) - 1, pltpu.VMEM((tok_dev, D), F32))
+    any_spec, vmem = pl.BlockSpec(memory_space=pl.ANY), pl.BlockSpec(memory_space=pltpu.VMEM)
     return pl.pallas_call(
-        functools.partial(attend_kernel, tok_dev),
-        grid=(HEADS,),
-        in_specs=[head(x.shape[0]) for x in (q, kr, vr, kc, vc)],
-        out_specs=[head(tok_dev), pl.BlockSpec((1, 8, tok_dev), lambda h: (h, 0, 0))],
-        out_shape=[
-            jax.ShapeDtypeStruct((tok_dev, D), F32),
-            jax.ShapeDtypeStruct((HEADS, 8, tok_dev), F32),
+        functools.partial(forward_kernel, panels, lines, 3),
+        out_shape=[jax.ShapeDtypeStruct((panels, lines // 2, 2, 2, rows, D), BF16)]
+        + [jax.ShapeDtypeStruct(shape, kind) for shape, kind in shapes]
+        + [jax.ShapeDtypeStruct((HEADS, 8, tok_dev), F32), jax.ShapeDtypeStruct((tok_dev, D), BF16)],
+        in_specs=[any_spec] + [vmem] * 5,
+        out_specs=[any_spec] * (1 + len(shapes)) + [vmem] * 2,
+        scratch_shapes=[pltpu.VMEM((4, lines // 2, 2, 2, rows, D), BF16)]
+        + scratch
+        + [
+            dma(()),
+            dma((panels, lines)), dma((panels, lines)),
+            dma((panels, 2)), dma((panels, 2)),
+            dma((panels, 2, 2)), dma((panels, 2, 2)),
+            dma((panels, 2)), dma((panels, 2)),
+            dma((4,)),
+            dma((8,)), dma((8,)), dma((8,)), dma((8,)),
+            dma((len(shapes),)),
         ],
-        compiler_params=pltpu.CompilerParams(vmem_limit_bytes=32 * MIB),
-        name="attend",
-    )(q, kr, vr, kc, vc)
+        compiler_params=pltpu.CompilerParams(
+            collective_id=0, has_side_effects=True, vmem_limit_bytes=58 * MIB
+        ),
+        name="forward",
+    )(block, tokens, tokens3, grad_out, valid, norm_params)
 
 
 def attend_back_kernel(
@@ -475,10 +735,8 @@
     for acc in (acc_kr, acc_vr, acc_kc, acc_vc):
         acc[...] = jnp.zeros_like(acc)
     for i in range(tok_dev // QB):
-        pos, raw_at, comp_at, raw_pos, comp_pos, memory, comp_low, comp_end = block_window(
-            seq, i, tok_dev, kr_ref.shape[0], kc_ref.shape[0]
-        )
-        rows = pl.ds(i * QB, QB)
+        at = Attention(seq, i, tok_dev, kr_ref.shape[0], kc_ref.shape[0])
+        rows = at.rows
         q = q_ref[rows, :]
         do = do_ref[rows, :]
         lse = lse_ref[0, 0:1, rows]
@@ -494,13 +752,10 @@
             acc_k[keys, :] += matmul(ds, q)
             return contract_rows(ds, k)
 
-        key_pos = raw_pos + lax.broadcasted_iota(jnp.int32, (RAW_KEYS, QB), 0)
-        query_pos = pos + lax.broadcasted_iota(jnp.int32, (RAW_KEYS, QB), 1)
-        seen = (key_pos >= jnp.maximum(memory, 0)) & (key_pos <= query_pos)
-        dq = part(kr_ref, vr_ref, acc_kr, acc_vr, pl.ds(raw_at, RAW_KEYS), seen)
-        comp_idx = comp_pos + lax.broadcasted_iota(jnp.int32, (COMP_KEYS, QB), 0)
-        seen = (comp_idx >= comp_low) & (comp_idx < comp_end)
-        dq = dq + part(kc_ref, vc_ref, acc_kc, acc_vc, pl.ds(comp_at, COMP_KEYS), seen)
+        seen = at.sees_raw((RAW_KEYS, QB), 0)
+        dq = part(kr_ref, vr_ref, acc_kr, acc_vr, at.raw, seen)
+        seen = at.sees_comp((COMP_KEYS, QB), 0)
+        dq = dq + part(kc_ref, vc_ref, acc_kc, acc_vc, at.comp, seen)
         dq_ref[rows, :] = (dq * scale).astype(BF16)
     dkr_ref[...] = (acc_kr[...] * scale).astype(BF16)
     dkc_ref[...] = (acc_kc[...] * scale).astype(BF16)
@@ -557,12 +812,7 @@
     scaled = (master * slot_scale[:, None, None]).astype(BF16)
     scaled = scaled.reshape(slot_count, slot_rows, group_count, wide).transpose(2, 0, 1, 3)
     slots_in = lax.all_to_all(scaled, "grp", 0, 0, tiled=True)
-    block = slots_in.reshape(all_slots, slot_rows, wide)[panel_slot]
-    weights = gather_panels(block, lines)
-    query_weight, key_weight, value_weight, out_weight = [weights[i] for i in range(4)]
-    up_weight = weights[4 : 4 + RATIO].reshape(FF, D)
-    down_weight = weights[4 + RATIO : 4 + 2 * RATIO].reshape(FF, D)
-    conv_weight = weights[4 + 2 * RATIO :]
+    block = slots_in.reshape(all_slots, slot_rows, wide)[panel_slot[jnp.array(ARRIVAL)]]
 
     positions = seq_index * tok_dev + jnp.arange(tok_dev, dtype=jnp.int32)
     book_id = jnp.sum(jnp.where(jnp.arange(group_count) == group_index, book_of_group, 0))
@@ -573,42 +823,21 @@
     )
     row_valid = (positions % S < row_counts).astype(F32)
 
-    raw_first, comp_first = key_window(seq_index, tok_dev)
-    raw_devs = (RAW_KEYS - QB + tok_dev - 1) // tok_dev + 1
-    comp_devs = min((3 * CM + S) // tok_dev + 1, seq_count)
-    all_tokens = lax.all_gather(tokens, "seq", axis=0, tiled=True)
-    padded = jnp.concatenate([jnp.zeros(((raw_devs - 1) * tok_dev, D), BF16), all_tokens], 0)
-    raw_tokens = lax.dynamic_slice_in_dim(padded, seq_index * tok_dev, raw_devs * tok_dev, 0)
-    comp_tokens = lax.dynamic_slice_in_dim(all_tokens, comp_first * tok_dev, comp_devs * tok_dev, 0)
-
-    def first_norm(rows):
-        return layer_norm(rows.astype(F32), norm_params[0], norm_params[1]).astype(BF16)
-
     inputs = tokens.astype(F32)
-    normed = first_norm(tokens)
-    normed_raw = first_norm(raw_tokens)
-    normed_comp = first_norm(comp_tokens).reshape(comp_devs * comp_dev, 3 * D)
-    compressed = matmul(normed_comp, conv_weight.reshape(3 * D, D)).astype(BF16)
-    queries = matmul(normed, query_weight).astype(BF16)
-    keys_raw = matmul(normed_raw, key_weight).astype(BF16)
-    values_raw = matmul(normed_raw, value_weight).astype(BF16)
-    keys_comp = matmul(compressed, key_weight).astype(BF16)
-    values_comp = matmul(compressed, value_weight).astype(BF16)
-    attended_sum, log_total = attend(queries, keys_raw, values_raw, keys_comp, values_comp)
-    attended = attended_sum.astype(BF16)
-
-    hidden = inputs + matmul(attended, out_weight)
-    normed_two = layer_norm(hidden, norm_params[2], norm_params[3]).astype(BF16)
-    pre_act = times_transposed(normed_two, up_weight)
-    active = jax.nn.gelu(pre_act).astype(BF16)
-    output = hidden + matmul(active, down_weight)
-    mixed = (output * row_valid[:, None]).astype(BF16)
+    tokens3 = tokens.reshape(comp_dev, 3, D).transpose(1, 0, 2)
     grad_out = cotangent.astype(F32) * row_valid[:, None]
     grad_out_low = grad_out.astype(BF16)
-    grad_active = times_transposed(grad_out_low, down_weight)
-    gelu_value, gelu_back = jax.vjp(jax.nn.gelu, pre_act)
-    grad_pre = gelu_back(grad_active)[0].astype(BF16)
-    grad_normed_two = matmul(grad_pre, up_weight)
+    (
+        weights, normed_raw, compressed, queries, keys_raw, values_raw, keys_comp, values_comp,
+        attended_sum, active, grad_pre, normed_two, hidden, grad_normed_two, log_total, mixed,
+    ) = forward(block, tokens, tokens3, grad_out_low, row_valid[:, None], norm_params, lines)
+    weights = weights.reshape(PANELS, D, D)
+    key_weight, value_weight, query_weight, out_weight = [weights[i] for i in range(3, 7)]
+    conv_weight = weights[:3]
+    raw_devs = raw_devices(tok_dev)
+    comp_first = comp_window_first(seq_index, tok_dev)
+    normed = normed_raw[(raw_devs - 1) * tok_dev :]
+    attended = attended_sum.astype(BF16)
     norm_value, norm_two_back = jax.vjp(layer_norm, hidden, norm_params[2], norm_params[3])
     grad_hidden_norm, grad_gain_two, grad_shift_two = norm_two_back(grad_normed_two)
     grad_hidden = grad_out + grad_hidden_norm

time: 743 us -> 672 us (0.904)
  matrix products: 135 us -> 64.7 us
  Pallas kernels: 378 us -> 407 us
  local copies, waits for them, and re-layouts: 93.6 us -> 77.1 us
  waiting for transfers between devices: 12 us -> 21.8 us
  other arithmetic: 32.8 us -> 23.8 us
  blocking collectives: 51.8 us -> 44.2 us
    dot_general x9 -> x7, matrix products: 64.7 us -> 27.3 us  [times_transposed(): lax.dot_general(left, right, (((1,), (1,)), ((), ())), preferred_element_...]
    dot_general x9 -> x0, matrix products: 35.5 us -> none  [matmul(): return jnp.dot(left, right, preferred_element_type=F32)]
    pallas_call x2 -> x1, Pallas kernels: 187 us -> 218 us  [forward(): pl.pallas_call(functools.partial(forward_kernel, panels, lines, 3), out_s...]
    slice x3, local copies, waits for them, and re-layouts: 18.5 us -> 8.92 us  [the longest x1 6.7 us: local(): conv_weight = weights[:3]]
    reduce_scatter x1, waiting for transfers between devices: 0.01 us -> 8.92 us  [local(): lax.psum_scatter(placed, 'seq', scatter_dimension=0, tiled=True)]
    psum x1, blocking collectives: 51.8 us -> 44.2 us  [local(): norm_grad = lax.psum(norm_local, ('grp', 'seq'))]
    unnamed x190 -> x115, local copies, waits for them, and re-layouts: 40.9 us -> 44.2 us
  transfers between devices with their start and end apart: 7 -> 6, of which waited for: 1 -> 2; matrix products, arithmetic and copies ran while one was open for 14% -> 14% of each run, Pallas kernels for 23% -> 24%
where the time goes in v2:
time: 672 us; the launch traced here: 667 us
  Pallas kernels  407 us (61%)
  local copies, waits for them, and re-layouts  77.1 us (11%)
  matrix products  64.7 us (10%)
  blocking collectives  44.2 us (7%)
  other arithmetic  23.8 us (4%)
  waiting for transfers between devices  21.8 us (3%)
  between operations  15 us (2%)
  starting transfers between devices  13.6 us (2%)
    pallas_call x1, Pallas kernels, forward(): pl.pallas_call(functools.partial(forward_kernel, panels, lines, 3), out_s...  218 us
    pallas_call x1, Pallas kernels, reduce_panels(): pl.pallas_call(functools.partial(reduce_kernel, panels, lines), out_shape...  162 us
    unnamed x115, local copies, waits for them, and re-layouts  44.2 us
    psum x1, blocking collectives, local(): norm_grad = lax.psum(norm_local, ('grp', 'seq'))  44.2 us
    dot_general x17, matrix products, contract_rows(): lax.dot_general(left, right, (((0,), (0,)), ((), ())), preferred_element_...  37.4 us
    pallas_call x1, Pallas kernels, attend_back(): pl.pallas_call(functools.partial(attend_back_kernel, tok_dev), grid=(HEAD...  27.3 us
    dot_general x7, matrix products, times_transposed(): lax.dot_general(left, right, (((1,), (1,)), ((), ())), preferred_element_...  27.3 us
  transfers between devices with their start and end apart: 6, of which 2 were waited for; matrix products, arithmetic and copies ran while one was open for 14% of the time, Pallas kernels for 24%

profile of v2, /device:TPU:0, one launch (start us, length us, event | category | flops | bytes accessed | tf_op | source)
XLA Modules:
  0.0 666.8 jit_solution(15971852568725043116)
XLA Ops:
  7.2 3.5 copy.47
  14.4 5.3 all-to-all-start
  26.8 12.9 %all-to-all-done = bf16[4,6,128,256]{2,3,1,0:T(8,128)(2,1)} async-done(((bf16[4,6,128,256]{2,3,1,0:T(8,128)(2,1)}), bf16[4,6,128,256]{2,3,1,0:T(8,128)(2,1)}, u32[]{:S(2)}, u32[]{:S(2)}) %all-to-all-start) | async-done | bytes 1572896 | tf_op jit(solution)/shard_map/all_to_all | solution.py:814
  43.0 217.5 %forward.1 = (bf16[15,2,2,2,128,1024]{5,4,3,2,1,0:T(8,128)(2,1)}, bf16[1536,1024]{1,0:T(8,128)(2,1)}, bf16[768,1024]{1,0:T(8,128)(2,1)}, bf16[384,1024]{1,0:T(8,...) custom-call(bf16[15,128,256]{2,1,0:T(8,128)(2,1)} %gather_fusion.1, ...), custom_call_target="tpu_custom_call" | custom-call | tf_op jit(solution)/shard_map/forward/pallas_call | solution.py:703
  260.5 6.5 fusion.52
  267.1 6.7 %slice.92 = bf16[3,2,2,2,128,1024]{5,4,3,2,1,0:T(8,128)(2,1)} slice(bf16[15,2,2,2,128,1024]{5,4,3,2,1,0:T(8,128)(2,1)} %get-tuple-element.41), slice={[0:3], [0:2], [0:2], [0:2], [0:128], [0:1024]} | slice | bytes 12582912 | tf_op jit(solution)/shard_map/slice | solution.py:836
  280.1 2.6 convolution_convert_fusion.8
  290.0 27.3 %attend_back.1 = (bf16[384,1024]{1,0:T(8,128)(2,1)S(1)}, bf16[1536,1024]{1,0:T(8,128)(2,1)S(1)}, bf16[1536,1024]{1,0:T(8,128)(2,1)}, bf16[768,1024]{1,0:T(8,128)(2,1)S(1)}, bf16[768,1024]{1,0:T(8,128)(2,1)S(1)}) custom-call(bf16[384,1024]{1,0:T(8,128)(2,1)S(1)} %copy-done.2, bf16[1536,1024]{1,0:T(8,128)(2,1)} %get-tuple-element.37.kr_ref, ...), custom_call_target="tpu_custom_call" | custom-call | tf_op jit(solution)/shard_map/attend_back/pallas_call | solution.py:774
  317.4 5.1 fusion.61
  322.5 5.5 fusion.58
  334.6 6.6 fusion.62
  341.2 7.4 %fusion.57 = (bf16[1536,1024]{1,0:T(8,128)(2,1)S(1)}, f32[1536,1024]{1,0:T(8,128)}) fusion(f32[1536,1024]{1,0:T(8,128)} %fusion.58, bf16[1536,1024]{1,0:T(8,128)(2,1)S(1)} %copy-done.43, bf16[1024,1024]{1,0:T(8,128)(2,1)S(1)} %bitcast.116), kind=kOutput, calls=%fused_computation.144 | convolution fusion | flops 3224371200 | bytes 20971520 | tf_op jit(solution)/shard_map/dot_general | solution.py:65
  359.1 3.3 add_convert_fusion.1
  362.5 3.3 add_convert_fusion
  366.5 3.2 constant_dynamic-update-slice_fusion.13
  400.6 8.9 %reduce-scatter.2.cloned.1.call-done = bf16[128,1024]{1,0:T(8,128)(2,1)} async-done(((bf16[1024,1024]{1,0:T(8,128)(2,1)}), bf16[128,1024]{1,0:T(8,128)(2,1)}) %reduce-scatter.2.cloned.1.call-update) | async-done | bytes 262160 | tf_op jit(solution)/shard_map/reduce_scatter | solution.py:858
  413.2 5.0 fusion.60
  424.2 161.7 %reduce_panels.1 = bf16[15,128,256]{2,1,0:T(8,128)(2,1)} custom-call(bf16[15,2,2,2,128,1024]{5,4,3,2,1,0:T(8,128)(2,1)} %constant_dynamic-update-slice_fusion.grad_ref), custom_call_target="tpu_custom_call" | custom-call | tf_op jit(solution)/shard_map/reduce_panels/pallas_call | solution.py:239
  589.5 4.5 all-to-all-start.1
  594.0 4.7 fusion.8
  599.6 44.2 %psum.7 = f32[4,1024]{1,0:T(4,128)S(1)} all-reduce(f32[4,1024]{1,0:T(4,128)S(1)} %pad_maximum_fusion), channel_id=1, replica_groups=mesh['grp'=4,'seq'=8] {'grp','seq'}, use_global_device_ids=true, to_apply=%region_20.21 | all-reduce | flops 4096 | bytes 32768 | tf_op jit(solution)/shard_map/psum | solution.py:872
  645.1 3.3 add_add_fusion.2
  650.7 2.7 copy-done.13
  654.3 4.6 multiply_subtract_fusion
  (196 shorter events, 95.4 us)
Async XLA Ops:
  14.4 6.1 copy-start.40
  14.4 6.8 %copy-start.9 = (bf16[384,1024]{1,0:T(8,128)(2,1)S(1)}, bf16[384,1024]{1,0:T(8,128)(2,1)}, u32[]{:S(2)}) copy-start(bf16[384,1024]{1,0:T(8,128)(2,1)} %tok_ref.1) | copy-start | bytes 2359300
  14.4 25.3 %all-to-all-start = ((bf16[4,6,128,256]{2,3,1,0:T(8,128)(2,1)}), bf16[4,6,128,256]{2,3,1,0:T(8,128)(2,1)}, u32[]{:S(2)}, u32[]{:S(2)}) async-start(bf16[4,6,128,256]{2,3,1,0:T(8,128)(2,1)} %copy.48), calls=%async_computation | async-start | bytes 3145728 | tf_op jit(solution)/shard_map/all_to_all | solution.py:814
  19.7 389.8 %reduce-scatter.2.cloned.1.call-start = ((), (), s32[]{:S(2)}) async-start(), calls=%async_computation.3 | async-start | bytes 2359296 | tf_op jit(solution)/shard_map/reduce_scatter | solution.py:858
  267.0 6.7 %copy-start.11 = (f32[384,1024]{1,0:T(8,128)S(1)}, f32[384,1024]{1,0:T(8,128)}, u32[]{:S(2)}) copy-start(f32[384,1024]{1,0:T(8,128)} %get-tuple-element.35) | copy-start | bytes 4718596
  290.0 27.3 %copy-start.33 = (bf16[1536,1024]{1,0:T(8,128)(2,1)S(1)}, bf16[1536,1024]{1,0:T(8,128)(2,1)}, u32[]{:S(2)}) copy-start(bf16[1536,1024]{1,0:T(8,128)(2,1)} %get-tuple-element.49) | copy-start | bytes 9437188
  317.3 10.7 %copy-start.6 = (bf16[768,1024]{1,0:T(8,128)(2,1)}, bf16[768,1024]{1,0:T(8,128)(2,1)S(1)}, u32[]{:S(2)}) copy-start(bf16[768,1024]{1,0:T(8,128)(2,1)S(1)} %get-tuple-element.47) | copy-start | bytes 4718596
  317.3 12.8 %copy-start.4 = (bf16[768,1024]{1,0:T(8,128)(2,1)}, bf16[768,1024]{1,0:T(8,128)(2,1)S(1)}, u32[]{:S(2)}) copy-start(bf16[768,1024]{1,0:T(8,128)(2,1)S(1)} %get-tuple-element.48) | copy-start | bytes 4718596
  317.4 5.1 copy-start.29
  334.6 6.6 copy-start.28
  334.6 6.6 copy-start.43
  350.0 244.0 %collective-permute-start.2 = (bf16[384,1024]{1,0:T(8,128)(2,1)}, bf16[384,1024]{1,0:T(8,128)(2,1)}, u32[]{:S(2)}, u32[]{:S(2)}) collective-permute-start(bf16[384,1024]{1,0:T(8,128)(2,1)} %get-tuple-element.77), channel_id=1, source_target_pairs={{3,0},{4,1},{5,2},{6,3},{7,4},{11,8},{12,9},{13,10},{14,11},{15,12... | collective-permute-start | bytes 2359304 | tf_op jit(solution)/shard_map/ppermute | solution.py:864
  351.3 242.7 %collective-permute-start.1 = (bf16[384,1024]{1,0:T(8,128)(2,1)}, bf16[384,1024]{1,0:T(8,128)(2,1)}, u32[]{:S(2)}, u32[]{:S(2)}) collective-permute-start(bf16[384,1024]{1,0:T(8,128)(2,1)} %get-tuple-element.78), channel_id=1, source_target_pairs={{2,0},{3,1},{4,2},{5,3},{6,4},{7,5},{10,8},{11,9},{12,10},{13,11},... | collective-permute-start | bytes 2359304 | tf_op jit(solution)/shard_map/ppermute | solution.py:864
  352.6 241.4 %collective-permute-start = (bf16[384,1024]{1,0:T(8,128)(2,1)}, bf16[384,1024]{1,0:T(8,128)(2,1)}, u32[]{:S(2)}, u32[]{:S(2)}) collective-permute-start(bf16[384,1024]{1,0:T(8,128)(2,1)} %get-tuple-element.76), channel_id=1, source_target_pairs={{1,0},{2,1},{3,2},{4,3},{5,4},{6,5},{7,6},{9,8},{10,9},{11,10},{12... | collective-permute-start | bytes 2359304 | tf_op jit(solution)/shard_map/ppermute | solution.py:864
  413.2 5.0 copy-start.31
  589.5 4.5 copy-start.10
  589.5 58.8 %all-to-all-start.1 = ((bf16[4,6,128,256]{3,2,1,0:T(8,128)(2,1)}), bf16[4,6,128,256]{3,2,1,0:T(8,128)(2,1)}, u32[]{:S(2)}, u32[]{:S(2)}) async-start(bf16[4,6,128,256]{3,2,1,0:T(8,128)(2,1)} %fusion.2), calls=%async_computation.2 | async-start | bytes 3145728 | tf_op jit(solution)/shard_map/all_to_all | solution.py:889
  598.7 45.1 %copy-start.35 = (f32[4,1024]{1,0:T(4,128)S(1)}, f32[4,1024]{1,0:T(4,128)}, u32[]{:S(2)}) copy-start(f32[4,1024]{1,0:T(4,128)} %norm_ref.1) | copy-start | bytes 49156
  598.7 45.0 %copy-start.37 = (f32[4,1024]{1,0:T(4,128)S(1)}, f32[4,1024]{1,0:T(4,128)}, u32[]{:S(2)}) copy-start(f32[4,1024]{1,0:T(4,128)} %param.20) | copy-start | bytes 49156
  598.8 45.0 %copy-start.38 = (f32[4,1024]{1,0:T(4,128)S(1)}, f32[4,1024]{1,0:T(4,128)}, u32[]{:S(2)}) copy-start(f32[4,1024]{1,0:T(4,128)} %param.19) | copy-start | bytes 49156
  598.8 46.3 %copy-start.18 = (bf16[384,1024]{1,0:T(8,128)(2,1)S(1)}, bf16[384,1024]{1,0:T(8,128)(2,1)}, u32[]{:S(2)}) copy-start(bf16[384,1024]{1,0:T(8,128)(2,1)} %param.14) | copy-start | bytes 2359300
  643.8 4.6 copy-start.36
  650.7 8.2 %copy-start.14 = (f32[4,6,16,8,256]{4,3,0,2,1:T(8,128)}, f32[4,6,16,8,256]{4,3,0,2,1:T(8,128)S(1)}, u32[]{:S(2)}) copy-start(f32[4,6,16,8,256]{4,3,0,2,1:T(8,128)S(1)} %copy.57) | copy-start | bytes 9437188
  654.3 4.6 copy-start.32
  (31 other events, 87.2 us)
Sparse Core Ops, SparseCore 0:
  334.7 74.7 reduce-scatter.1

commit v3 on v2

--- a/solution.py
+++ b/solution.py
@@ -108,160 +108,6 @@
         device_id=device,
         device_id_type=MESH,
     )
-
-
-def reduce_kernel(
-    panels, lines, grad_ref, out_ref, own, cross_in, first_in, second_in, line_in,
-    own_sem, cs, cr, s1, r1, s2, r2, zs, zr,
-):
-    at = Place(lines)
-    wide = out_ref.shape[-1]
-    pairs = lines // 2
-
-    def cols(g):
-        return pl.ds(g * wide, wide)
-
-    def load(p, g):
-        src = grad_ref.at[p, :, :, at.core, :, cols(g)]
-        return pltpu.make_async_copy(src, own.at[p, :, :, g // 2, g % 2], own_sem.at[p, g])
-
-    def cross(p, g):
-        src = grad_ref.at[p, :, :, 1 - at.core, :, cols(g)]
-        dst = cross_in.at[p, :, :, g // 2, g % 2]
-        return remote(src, dst, cs.at[p, g], cr.at[p, g], at.core_dev)
-
-    def first(p, h):
-        if h == 0:
-            src = own.at[p, :, 0, 1 - at.row]
-            return remote(src, first_in.at[p, 0], s1.at[p, 0], r1.at[p, 0], at.y_dev)
-        src = own.at[p, :, 1, :, 1 - at.col]
-        return remote(src, first_in.at[p, 1], s1.at[p, 1], r1.at[p, 1], at.x_dev)
-
-    def second(p, h):
-        if h == 0:
-            src = own.at[p, :, 0, at.row, 1 - at.col]
-            return remote(src, second_in.at[p, 0], s2.at[p, 0], r2.at[p, 0], at.x_dev)
-        src = own.at[p, :, 1, 1 - at.row, at.col]
-        return remote(src, second_in.at[p, 1], s2.at[p, 1], r2.at[p, 1], at.y_dev)
-
-    def line_copy(p, k):
-        z = at.other_line(k)
-        src = own.at[p, z // 2, z % 2, at.row, at.col]
-        return remote(src, line_in.at[p, at.line], zs.at[p, k], zr.at[p, at.line], at.line_dev(k))
-
-    def line_arrival(p, k):
-        z = at.other_line(k)
-        src = own.at[p, z // 2, z % 2, at.row, at.col]
-        return remote(src, line_in.at[p, z], zs.at[p, k], zr.at[p, z], at.line_dev(k))
-
-    def add(dst, src):
-        dst[...] = (dst[...].astype(F32) + src[...].astype(F32)).astype(BF16)
-
-    def start(p):
-        for g in range(4):
-            cross(p, g).start()
-            load(p, g).start()
-
-    def start_first(p):
-        for g in range(4):
-            cross(p, g).wait_recv()
-            load(p, g).wait()
-        for h in (0, 1):
-            for i in range(pairs):
-                for g in range(4):
-                    add(own.at[p, i, h, g // 2, g % 2], cross_in.at[p, i, h, g // 2, g % 2])
-            first(p, h).start()
-
-    def start_second(p):
-        for h in (0, 1):
-            first(p, h).wait_recv()
-            for i in range(pairs):
-                for j in (0, 1):
-                    row, col = (at.row, j) if h == 0 else (j, at.col)
-                    add(own.at[p, i, h, row, col], first_in.at[p, h, i, j])
-            second(p, h).start()
-
-    def start_lines(p):
-        for h in (0, 1):
-            second(p, h).wait_recv()
-            for i in range(pairs):
-                add(own.at[p, i, h, at.row, at.col], second_in.at[p, h, i])
-        for k in range(1, lines):
-            line_copy(p, k).start()
-
-    def finish(p):
-        total = own[p, at.line // 2, at.line % 2, at.row, at.col].astype(F32)
-        for k in range(1, lines):
-            line_arrival(p, k).wait_recv()
-            total = total + line_in[p, at.other_line(k)].astype(F32)
-        out_ref[p] = total.astype(BF16)
-        for h in (0, 1):
-            first(p, h).wait_send()
-            second(p, h).wait_send()
-        for g in range(4):
-            cross(p, g).wait_send()
-        for k in range(1, lines):
-            line_copy(p, k).wait_send()
-
-    at.enter()
-    start(0)
-
-    def step(t, carry):
-        @pl.when(t + 1 < panels)
-        def _():
-            start(t + 1)
-
-        @pl.when(t < panels)
-        def _():
-            start_first(t)
-
-        @pl.when((t >= 1) & (t < panels + 1))
-        def _():
-            start_second(t - 1)
-
-        @pl.when((t >= 2) & (t < panels + 2))
-        def _():
-            start_lines(t - 2)
-
-        @pl.when(t >= 3)
-        def _():
-            finish(t - 3)
-
-        return carry
-
-    lax.fori_loop(0, panels + 3, step, 0)
-
-
-def reduce_panels(grads, lines):
-    panels = grads.shape[0]
-    rows, wide, pairs = D // (2 * lines), D // 4, lines // 2
-    dma = pltpu.SemaphoreType.DMA
-    return pl.pallas_call(
-        functools.partial(reduce_kernel, panels, lines),
-        out_shape=jax.ShapeDtypeStruct((panels, rows, wide), BF16),
-        in_specs=[pl.BlockSpec(memory_space=pl.ANY)],
-        out_specs=pl.BlockSpec(memory_space=pltpu.VMEM),
-        scratch_shapes=[
-            pltpu.VMEM((panels, pairs, 2, 2, 2, rows, wide), BF16),
-            pltpu.VMEM((panels, pairs, 2, 2, 2, rows, wide), BF16),
-            pltpu.VMEM((panels, 2, pairs, 2, rows, wide), BF16),
-            pltpu.VMEM((panels, 2, pairs, rows, wide), BF16),
-            pltpu.VMEM((panels, lines, rows, wide), BF16),
-            dma((panels, 4)),
-            dma((panels, 4)),
-            dma((panels, 4)),
-            dma((panels, 2)),
-            dma((panels, 2)),
-            dma((panels, 2)),
-            dma((panels, 2)),
-            dma((panels, lines)),
-            dma((panels, lines)),
-        ],
-        compiler_params=pltpu.CompilerParams(
-            collective_id=1, has_side_effects=True, vmem_limit_bytes=56 * MIB
-        ),
-        name="reduce_panels",
-    )(grads.reshape(panels, pairs, 2, 2, rows, D))
 
 
 def memory_start(position):
@@ -387,7 +233,7 @@
     panels, lines, ahead,
     block_ref, tok_ref, tok3_ref, dy_ref, valid_ref, norm_ref,
     full_ref, a_out, c_out, q_out, kr_out, vr_out, kc_out, vc_out, o_out, z_out, df_out, b_out,
-    h_out, db_out, lse_ref, mixed_ref,
+    h_out, db_out, a3_out, lse_ref, mixed_ref,
     wbuf, a_win, a3, c_win, q, kr, vr, kc, vc, o, z, df, b, h, y, db,
     own_sem, zs, zr, s1, r1, s2, r2, cs, cr, wsem, a_s, a_r, c_s, c_r, out_sem,
 ):
@@ -496,6 +342,7 @@
     outs = [
         (a_win, a_out), (c_win, c_out), (q, q_out), (kr, kr_out), (vr, vr_out), (kc, kc_out),
         (vc, vc_out), (o, o_out), (z, z_out), (df, df_out), (b, b_out), (h, h_out), (db, db_out),
+        (a3, a3_out),
     ]
 
     def flush(*names):
@@ -594,7 +441,7 @@
             for d in range(1, raw_devs):
                 pl.when(needs_raw(seq, seq - d, tok_dev))(lambda d=d: a_copy(d).wait_recv())
                 pl.when(reads_a(d))(lambda d=d: a_copy(d).wait_send())
-            flush(a_win)
+            flush(a_win, a3)
 
         @pl.when(p == 3)
         def _():
@@ -694,10 +541,10 @@
         ((raw, D), BF16), ((comp, D), BF16), ((tok_dev, D), BF16), ((raw, D), BF16),
         ((raw, D), BF16), ((comp, D), BF16), ((comp, D), BF16), ((tok_dev, D), F32),
         ((tok_dev, FF), BF16), ((tok_dev, FF), BF16), ((tok_dev, D), BF16), ((tok_dev, D), F32),
-        ((tok_dev, D), F32),
+        ((tok_dev, D), F32), ((3, tok_dev // 3, D), BF16),
     ]
     scratch = [pltpu.VMEM(shape, kind) for shape, kind in shapes]
-    scratch.insert(1, pltpu.VMEM((3, tok_dev // 3, D), BF16))
+    scratch.insert(1, scratch.pop())
     scratch.insert(len(scratch) - 1, pltpu.VMEM((tok_dev, D), F32))
     any_spec, vmem = pl.BlockSpec(memory_space=pl.ANY), pl.BlockSpec(memory_space=pltpu.VMEM)
     return pl.pallas_call(
@@ -726,66 +573,565 @@
     )(block, tokens, tokens3, grad_out, valid, norm_params)
 
 
-def attend_back_kernel(
-    tok_dev, q_ref, kr_ref, vr_ref, kc_ref, vc_ref, do_ref, lse_ref, delta_ref,
-    dq_ref, dkr_ref, dvr_ref, dkc_ref, dvc_ref, acc_kr, acc_vr, acc_kc, acc_vc,
+RETURN = [4 + RATIO + _i for _i in range(RATIO)] + [4 + _i for _i in range(RATIO)] + [3, 0, 1, 2] + TAPS
+RING = 3
+HELD = 5
+BACK_LAG = 4
+
+
+def norm_back(grad, values, params, first):
+    mean = row_sum(values) * (1.0 / D)
+    centered = values - mean
+    scale = lax.rsqrt(row_sum(centered * centered) * (1.0 / D) + NORM_EPS)
+    unit = centered * scale
+    inner = grad * params[first : first + 1, :]
+    back = inner - row_sum(inner) * (1.0 / D) - unit * (row_sum(inner * unit) * (1.0 / D))
+    gain = jnp.sum(grad * unit, axis=0, keepdims=True)
+    return back * scale, gain, jnp.sum(grad, axis=0, keepdims=True)
+
+
+def attend_head_back(
+    seq, tok_dev, cols, q, do, o, kr, vr, kc, vc, lse, lse_row, dkr, dvr, dkc, dvc,
+    acc_kr, acc_vr, acc_kc, acc_vc,
 ):
-    seq = lax.axis_index("seq")
     scale = HEAD_DIM ** (-0.5)
     for acc in (acc_kr, acc_vr, acc_kc, acc_vc):
         acc[...] = jnp.zeros_like(acc)
     for i in range(tok_dev // QB):
-        at = Attention(seq, i, tok_dev, kr_ref.shape[0], kc_ref.shape[0])
-        rows = at.rows
-        q = q_ref[rows, :]
-        do = do_ref[rows, :]
-        lse = lse_ref[0, 0:1, rows]
-        delta = delta_ref[0, 0:1, rows]
+        at = Attention(seq, i, tok_dev, kr.shape[0], kc.shape[0])
+        query = q[at.rows, cols]
+        grad = do[at.rows, cols]
+        delta = row_sum(grad.astype(F32) * o[at.rows, cols])
+        delta = jnp.broadcast_to(delta, (QB, QB)).T[0:1]
+        stat = lse[lse_row, 0:1, at.rows]
 
         def part(k_ref, v_ref, acc_k, acc_v, keys, seen):
             k = k_ref[keys, :]
-            s = times_transposed(k, q) * scale
-            p = jnp.where(seen, jnp.exp(jnp.where(seen, s, NEG_SCORE) - lse), 0.0)
-            dp = times_transposed(v_ref[keys, :], do)
+            s = times_transposed(k, query) * scale
+            p = jnp.where(seen, jnp.exp(jnp.where(seen, s, NEG_SCORE) - stat), 0.0)
+            dp = times_transposed(v_ref[keys, :], grad)
             ds = (p * (dp - delta)).astype(BF16)
-            acc_v[keys, :] += matmul(p.astype(BF16), do)
-            acc_k[keys, :] += matmul(ds, q)
+            acc_v[keys, :] += matmul(p.astype(BF16), grad)
+            acc_k[keys, :] += matmul(ds, query)
             return contract_rows(ds, k)
 
-        seen = at.sees_raw((RAW_KEYS, QB), 0)
-        dq = part(kr_ref, vr_ref, acc_kr, acc_vr, at.raw, seen)
+        dq = part(kr, vr, acc_kr, acc_vr, at.raw, at.sees_raw((RAW_KEYS, QB), 0))
         seen = at.sees_comp((COMP_KEYS, QB), 0)
-        dq = dq + part(kc_ref, vc_ref, acc_kc, acc_vc, at.comp, seen)
-        dq_ref[rows, :] = (dq * scale).astype(BF16)
-    dkr_ref[...] = (acc_kr[...] * scale).astype(BF16)
-    dkc_ref[...] = (acc_kc[...] * scale).astype(BF16)
-    dvr_ref[...] = acc_vr[...].astype(BF16)
-    dvc_ref[...] = acc_vc[...].astype(BF16)
-
-
-def attend_back(q, kr, vr, kc, vc, do, lse, delta):
-    tok_dev, raw_rows, comp_rows = q.shape[0], kr.shape[0], kc.shape[0]
-
-    def head(rows):
-        return pl.BlockSpec((rows, HEAD_DIM), lambda h: (0, h))
-
-    stat = pl.BlockSpec((1, 8, tok_dev), lambda h: (h, 0, 0))
-    outs = [tok_dev, raw_rows, raw_rows, comp_rows, comp_rows]
+        dq = dq + part(kc, vc, acc_kc, acc_vc, at.comp, seen)
+        q[at.rows, cols] = (dq * scale).astype(BF16)
+    dkr[:, cols] = (acc_kr[...] * scale).astype(BF16)
+    dkc[:, cols] = (acc_kc[...] * scale).astype(BF16)
+    dvr[:, cols] = acc_vr[...].astype(BF16)
+    dvc[:, cols] = acc_vc[...].astype(BF16)
+
+
+def backward_kernel(
+    panels, lines,
+    full_ref, a_hbm, c_hbm, a3_hbm, q_hbm, kr_hbm, vr_hbm, kc_hbm, vc_hbm, o_hbm, z_hbm, df_hbm,
+    b_hbm, h_hbm, db_hbm, dy_hbm, tok_hbm, lse_ref, norm_ref,
+    out_ref, in_grad_out, norm_out,
+    held, cross_in, first_in, second_in, line_in,
+    opnd, lhs_t, c_win, a3, h, db, o, pair, q, kr, vr, kc, vc, acc_kr, acc_vr, acc_kc, acc_vc,
+    dkr, dvr, dkc, dvc, wbuf, dc, dc_in, da_in, n_src, n_in, n_line,
+    cs, cr, s1, r1, s2, r2, zs, zr, free_cross, free_first, free_second,
+    lsem, osem, hsem, wsem, dcs, dcr, das, dar, ns, nr, nzs, nzr,
+):
+    at = Place(lines)
+    seq = at.seq
+    seq_count = 2 * lines
+    tok_dev = q.shape[0]
+    comp_dev = tok_dev // 3
+    raw_devs = dkr.shape[0] // tok_dev
+    comp_devs = dkc.shape[0] // comp_dev
+    reach = min(seq_count - 1, (2 * S + 3 * CM + tok_dev - 1) // tok_dev)
+    wide = out_ref.shape[-1]
+    rows_dev = out_ref.shape[1]
+    pairs = lines // 2
+    params = norm_ref[...]
+    block = [pl.ds(i * tok_dev, tok_dev) for i in range(raw_devs)]
+    dhb, do = pair.at[block[0], :], pair.at[block[1], :]
+
+    def cross(p):
+        src = held.at[lax.rem(p, HELD), :, :, 1 - at.core]
+        slot = lax.rem(p, RING)
+        return remote(src, cross_in.at[slot], cs.at[slot], cr.at[slot], at.core_dev)
+
+    def mine(p):
+        return held.at[lax.rem(p, HELD), :, :, at.core]
+
+    def first(p, half):
+        slot = lax.rem(p, RING)
+        if half == 0:
+            src, device = mine(p).at[:, 0, 1 - at.row], at.y_dev
+        else:
+            src, device = mine(p).at[:, 1, :, 1 - at.col], at.x_dev
+        return remote(src, first_in.at[slot, half], s1.at[slot, half], r1.at[slot, half], device)
+
+    def second(p, half):
+        slot = lax.rem(p, RING)
+        if half == 0:
+            src, device = mine(p).at[:, 0, at.row, 1 - at.col], at.x_dev
+        else:
+            src, device = mine(p).at[:, 1, 1 - at.row, at.col], at.y_dev
+        return remote(src, second_in.at[slot, half], s2.at[slot, half], r2.at[slot, half], device)
+
+    def line_copy(p, k):
+        line = at.other_line(k)
+        src = mine(p).at[line // 2, line % 2, at.row, at.col]
+        return remote(src, line_in.at[p, at.line], zs.at[p, k], zr.at[p, at.line], at.line_dev(k))
+
+    def line_arrival(p, k):
+        line = at.other_line(k)
+        src = mine(p).at[line // 2, line % 2, at.row, at.col]
+        return remote(src, line_in.at[p, line], zs.at[p, k], zr.at[p, line], at.line_dev(k))
+
+    def give(semaphore, device):
+        pl.semaphore_signal(semaphore, inc=1, device_id=device, device_id_type=MESH)
+
+    def add(dst, src):
+        dst[...] = (dst[...].astype(F32) + src[...].astype(F32)).astype(BF16)
+
+    def start_first(p):
+        cross(p).wait_recv()
+        for half in (0, 1):
+            for i in range(pairs):
+                for g in range(4):
+                    add(
+                        mine(p).at[i, half, g // 2, g % 2],
+                        cross_in.at[lax.rem(p, RING), i, half, g // 2, g % 2],
+                    )
+            pl.when(p >= RING)(lambda half=half: pl.semaphore_wait(free_first.at[half], 1))
+            first(p, half).start()
+        cross(p).wait_send()
+        pl.when(p + RING < panels)(lambda: give(free_cross, at.core_dev))
+
+    def start_second(p):
+        slot = lax.rem(p, RING)
+        for half in (0, 1):
+            first(p, half).wait_recv()
+            for i in range(pairs):
+                for j in (0, 1):
+                    row, col = (at.row, j) if half == 0 else (j, at.col)
+                    add(mine(p).at[i, half, row, col], first_in.at[slot, half, i, j])
+            pl.when(p >= RING)(lambda half=half: pl.semaphore_wait(free_second.at[half], 1))
+            second(p, half).start()
+            first(p, half).wait_send()
+            device = at.y_dev if half == 0 else at.x_dev
+            pl.when(p + RING < panels)(
+                lambda half=half, device=device: give(free_first.at[half], device)
+            )
+
+    def start_lines(p):
+        slot = lax.rem(p, RING)
+        for half in (0, 1):
+            second(p, half).wait_recv()
+            for i in range(pairs):
+                add(mine(p).at[i, half, at.row, at.col], second_in.at[slot, half, i])
+            second(p, half).wait_send()
+            device = at.x_dev if half == 0 else at.y_dev
+            pl.when(p + RING < panels)(
+                lambda half=half, device=device: give(free_second.at[half], device)
+            )
+        for k in range(1, lines):
+            line_copy(p, k).start()
+
+    def finish(p):
+        total = mine(p)[at.line // 2, at.line % 2, at.row, at.col].astype(F32)
+        for k in range(1, lines):
+            line_arrival(p, k).wait_recv()
+            total = total + line_in[p, at.other_line(k)].astype(F32)
+        out_ref[p] = total.astype(BF16)
+        for k in range(1, lines):
+            line_copy(p, k).wait_send()
+
+    def produce(p, *terms):
+        slot = lax.rem(p, HELD)
+        lefts = []
+        for left, right in terms:
+            rows = left.shape[0]
+            lhs_t[:, pl.ds(0, rows)] = left[...].astype(BF16).T
+
+            def columns(j, carry, right=right, rows=rows):
+                col = pl.ds(pl.multiple_of(j * wide, wide), wide)
+                total = matmul(lhs_t[:, pl.ds(0, rows)], right[:, col])
+                total = total.reshape(pairs, 2, 2, rows_dev, wide)
+                place = held.at[slot, :, :, :, j // 2, j % 2]
+                if len(lefts) > 0:
+                    total = total + place[...].astype(F32)
+                place[...] = total.astype(BF16)
+                return carry
+
+            lax.fori_loop(0, 4, columns, 0)
+            lefts.append(left)
+        pl.when(p >= RING)(lambda: pl.semaphore_wait(free_cross, 1))
+        cross(p).start()
+
+    def left_load(p):
+        rows = block[2] if p % 2 == 0 else block[3]
+        src = z_hbm if p < RATIO else df_hbm
+        place = opnd.at[rows, :]
+        units = pl.ds((p % RATIO) * D, D)
+        return pltpu.make_async_copy(src.at[:, units], place, lsem.at[p % 2])
+
+    early = [
+        (dy_hbm, opnd.at[block[0], :]), (b_hbm, opnd.at[block[1], :]), (h_hbm, h), (db_hbm, db),
+        (o_hbm, o), (q_hbm, q), (c_hbm, c_win), (a3_hbm, a3),
+    ]
+
+    def early_load(i):
+        return pltpu.make_async_copy(early[i][0], early[i][1], osem.at[i])
+
+    def late_load(i):
+        if i == 0:
+            return pltpu.make_async_copy(a_hbm, opnd, osem.at[len(early)])
+        if i == 1:
+            return pltpu.make_async_copy(tok_hbm, dhb, osem.at[len(early) + 1])
+        return pltpu.make_async_copy(h, in_grad_out, osem.at[len(early) + 2])
+
+    def head_loads(i):
+        col = pl.ds(pl.multiple_of(i * HEAD_DIM, HEAD_DIM), HEAD_DIM)
+        refs = [(kr_hbm, kr), (vr_hbm, vr), (kc_hbm, kc), (vc_hbm, vc)]
+        return [
+            pltpu.make_async_copy(src.at[:, col], dst, hsem.at[j])
+            for j, (src, dst) in enumerate(refs)
+        ]
+
+    def weight_load(panel, slot):
+        return pltpu.make_async_copy(full_ref.at[panel], wbuf.at[slot], wsem.at[slot])
+
+    def weight(slot):
+        return wbuf[slot].reshape(D, D)
+
+    def seq_dev(d):
+        return {"grp": at.grp, "seq": lax.rem(seq + d + seq_count, seq_count)}
+
+    def comp_rows(reader, owner):
+        place = jnp.clip(owner - comp_window_first(reader, tok_dev), 0, comp_devs - 1)
+        return pair.at[pl.ds(pl.multiple_of(place * comp_dev, comp_dev), comp_dev), :]
+
+    def dc_copy(d):
+        return remote(comp_rows(seq, seq - d), dc_in.at[d - 1], dcs.at[d], dcr.at[d], seq_dev(-d))
+
+    def da_copy(d):
+        src = dkr.at[block[raw_devs - 1 - d], :]
+        return remote(src, da_in.at[d - 1], das.at[d], dar.at[d], seq_dev(-d))
+
+    def reads_comp(d):
+        return needs_comp(seq, seq - d, tok_dev)
+
+    def read_comp(d):
+        return (seq + d < seq_count) & needs_comp(seq + d, seq, tok_dev)
+
+    def reads_raw(d):
+        return needs_raw(seq, seq - d, tok_dev)
+
+    def read_raw(d):
+        return (seq + d < seq_count) & needs_raw(seq + d, seq, tok_dev)
+
+    def norm_copy(i):
+        device = (at.core_dev, at.x_dev, at.y_dev)[i]
+        return remote(n_src.at[i], n_in.at[i], ns.at[i], nr.at[i], device)
+
+    def norm_line(k):
+        return remote(n_src.at[3], n_line.at[at.line], nzs.at[k], nzr.at[at.line], at.line_dev(k))
+
+    def norm_line_arrival(k):
+        line = at.other_line(k)
+        return remote(n_src.at[3], n_line.at[line], nzs.at[k], nzr.at[line], at.line_dev(k))
+
+    def second_norm_back():
+        gains, shifts = [], []
+        for i in range(tok_dev // QB):
+            rows = pl.ds(i * QB, QB)
+            back, gain, shift = norm_back(db[rows, :], h[rows, :], params, 2)
+            db[rows, :] = opnd[rows, :].astype(F32) + back
+            dhb[rows, :] = db[rows, :].astype(BF16)
+            gains.append(gain)
+            shifts.append(shift)
+        n_src[0, 2:3, :] = sum(gains)
+        n_src[0, 3:4, :] = sum(shifts)
+        do[...] = times_transposed(dhb[...], weight(0)).astype(BF16)
+
+    def work(t):
+        @pl.when(t == 0)
+        def _():
+            for i in range(2, 6):
+                early_load(i).wait()
+            weight_load(6, 0).wait()
+            second_norm_back()
+            weight_load(5, 0).start()
+
+        @pl.when((t >= 1) & (t <= HEADS))
+        def _():
+            for copy in head_loads(t - 1):
+                copy.wait()
+            cols = pl.ds(pl.multiple_of((t - 1) * HEAD_DIM, HEAD_DIM), HEAD_DIM)
+            attend_head_back(
+                seq, tok_dev, cols, q, do, o, kr, vr, kc, vc, lse_ref, t - 1, dkr, dvr, dkc, dvc,
+                acc_kr, acc_vr, acc_kc, acc_vc,
+            )
+
+            @pl.when(t < HEADS)
+            def _():
+                for copy in head_loads(t):
+                    copy.start()
+
+        @pl.when(t == HEADS + 1)
+        def _():
+            weight_load(3, 1).wait()
+            weight_load(4, 2).wait()
+            half = pair.shape[0] // 2
+            for i in range(2):
+                rows = pl.ds(i * half, half)
+                total = times_transposed(dkc[rows, :], weight(1))
+                total = total + times_transposed(dvc[rows, :], weight(2))
+                pair[rows, :] = total.astype(BF16)
+            for d in range(1, reach + 1):
+                pl.when(reads_comp(d))(lambda d=d: dc_copy(d).start())
+
+        @pl.when(t == HEADS + 2)
+        def _():
+            weight_load(5, 0).wait()
+            h[...] = times_transposed(q[...], weight(0))
+            weight_load(0, 0).start()
+
+        @pl.when(t == HEADS + 4)
+        def _():
+            for i in range(raw_devs):
+                total = times_transposed(dkr[block[i], :], weight(1))
+                total = total + times_transposed(dvr[block[i], :], weight(2))
+                if i < raw_devs - 1:
+                    dkr[block[i], :] = total.astype(BF16)
+                    d = raw_devs - 1 - i
+                    pl.when(reads_raw(d))(lambda d=d: da_copy(d).start())
+                else:
+                    h[...] += total
+            weight_load(1, 1).start()
+            weight_load(2, 2).start()
+
+        @pl.when(t == HEADS + 5)
+        def _():
+            weight_load(0, 0).wait()
+            weight_load(1, 1).wait()
+            weight_load(2, 2).wait()
+            heads_of = acc_kr.shape[0] // tok_dev
+            for k in range(3):
+                total = times_transposed(dc[...], weight(k))
+                for c in range(HEADS):
+                    acc = (acc_kr, acc_vr)[c // heads_of]
+                    place = pl.ds(c % heads_of * tok_dev + k, comp_dev, stride=3)
+                    acc[place, :] = total[:, c * HEAD_DIM : (c + 1) * HEAD_DIM]
+            for c in range(HEADS):
+                acc = (acc_kr, acc_vr)[c // heads_of]
+                cols = pl.ds(c * HEAD_DIM, HEAD_DIM)
+                h[:, cols] += acc[pl.ds(c % heads_of * tok_dev, tok_dev), :]
+            for d in range(1, reach + 1):
+                pl.when(reads_comp(d))(lambda d=d: dc_copy(d).wait_send())
+            late_load(1).start()
+
+        @pl.when(t == HEADS + 6)
+        def _():
+            for d in range(1, raw_devs):
+
+                @pl.when(read_raw(d))
+                def _(d=d):
+                    da_copy(d).wait_recv()
+                    h[...] += da_in[d - 1].astype(F32)
+
+                pl.when(reads_raw(d))(lambda d=d: da_copy(d).wait_send())
+            late_load(1).wait()
+            gains, shifts = [], []
+            for i in range(tok_dev // QB):
+                rows = pl.ds(i * QB, QB)
+                x = dhb[rows, :].astype(F32)
+                back, gain, shift = norm_back(h[rows, :], x, params, 0)
+                h[rows, :] = db[rows, :] + back
+                gains.append(gain)
+                shifts.append(shift)
+            n_src[0, 0:1, :] = sum(gains)
+            n_src[0, 1:2, :] = sum(shifts)
+            norm_copy(0).start()
+            late_load(2).start()
+
+        @pl.when(t == HEADS + 7)
+        def _():
+            norm_copy(0).wait_recv()
+            n_src[1] = n_src[0] + n_in[0]
+            norm_copy(1).start()
+
+        @pl.when(t == HEADS + 8)
+        def _():
+            norm_copy(1).wait_recv()
+            n_src[2] = n_src[1] + n_in[1]
+            norm_copy(2).start()
+
+        @pl.when(t == HEADS + 9)
+        def _():
+            norm_copy(2).wait_recv()
+            n_src[3] = n_src[2] + n_in[2]
+            n_line[at.line] = n_src[3]
+            for k in range(1, lines):
+                norm_line(k).start()
+
+    def make(t):
+        for p in range(2 * RATIO):
+
+            @pl.when(t == p)
+            def _(p=p):
+                if p + 1 < 2 * RATIO:
+                    left_load(p + 1).start()
+                left_load(p).wait()
+                right = 0 if p < RATIO else 1
+                if p == right * RATIO:
+                    early_load(right).wait()
+                produce(t, (opnd.at[block[2 + p % 2], :], opnd.at[block[right], :]))
+                if p + 1 == 2 * RATIO:
+                    late_load(0).start()
+
+        pl.when(t == 8)(lambda: produce(t, (o, dhb)))
+
+        @pl.when(t == 9)
+        def _():
+            late_load(0).wait()
+            early_load(6).wait()
+            early_load(7).wait()
+            produce(t, (opnd.at[block[raw_devs - 1], :], q))
+
+        def window(dr, dcomp):
+            terms = [(opnd.at[rows, :], dr.at[rows, :]) for rows in block]
+            comp = [pl.ds(i * tok_dev, tok_dev) for i in range(dcomp.shape[0] // tok_dev)]
+            terms = terms + [(c_win.at[rows, :], dcomp.at[rows, :]) for rows in comp]
+            produce(t, *terms)
+
+        pl.when(t == 10)(lambda: window(dkr, dkc))
+        pl.when(t == 11)(lambda: window(dvr, dvc))
+
+        @pl.when(t == 12)
+        def _():
+            acc = lhs_t
+            h_dc = o.at[pl.ds(0, comp_dev), :]
+            h_dc[...] = jnp.zeros_like(h_dc)
+            for d in range(1, reach + 1):
+
+                @pl.when(read_comp(d))
+                def _(d=d):
+                    dc_copy(d).wait_recv()
+                    h_dc[...] += dc_in[d - 1].astype(F32)
+
+            dc[...] = h_dc[...].astype(BF16)
+
+        for k in range(3):
+            pl.when(t == 12 + k)(lambda k=k: produce(t, (a3.at[k], dc)))
+
+    for i in range(len(early)):
+        early_load(i).start()
+    left_load(0).start()
+    for panel, slot in ((6, 0), (3, 1), (4, 2)):
+        weight_load(panel, slot).start()
+    for copy in head_loads(0):
+        copy.start()
+    barrier = pltpu.get_barrier_semaphore()
+    partners = [seq_dev(d) for d in range(1, seq_count)] + [at.x_dev, at.y_dev]
+    for device in partners:
+        pl.semaphore_signal(barrier, inc=1, device_id=device, device_id_type=MESH)
+    pl.semaphore_wait(barrier, seq_count + 1)
+
+    def step(t, carry):
+        pl.when((t >= 1) & (t < panels + 1))(lambda: start_first(t - 1))
+        pl.when((t >= 2) & (t < panels + 2))(lambda: start_second(t - 2))
+        pl.when((t >= 3) & (t < panels + 3))(lambda: start_lines(t - 3))
+        pl.when(t >= BACK_LAG)(lambda: finish(t - BACK_LAG))
+        pl.when(t < panels)(lambda: make(t))
+        work(t)
+        return carry
+
+    lax.fori_loop(0, panels + BACK_LAG, step, 0)
+    for i in range(3):
+        norm_copy(i).wait_send()
+    for k in range(1, lines):
+        norm_line_arrival(k).wait_recv()
+        norm_line(k).wait_send()
+    total = n_line[0]
+    for i in range(1, lines):
+        total = total + n_line[i]
+    norm_out[...] = total
+    late_load(2).wait()
+
+
+def backward(weights, arrays, lse, norm_params, lines):
+    panels, rows = weights.shape[0], weights.shape[4]
+    wide, pairs, seq_count = D // 4, lines // 2, 2 * lines
+    a_win, c_win = arrays[0], arrays[1]
+    tok_dev = arrays[3].shape[0]
+    raw, comp, comp_dev = a_win.shape[0], c_win.shape[0], tok_dev // 3
+    raw_devs = raw // tok_dev
+    reach = min(seq_count - 1, (2 * S + 3 * CM + tok_dev - 1) // tok_dev)
+    dma = pltpu.SemaphoreType.DMA
+    regular = pltpu.SemaphoreType.REGULAR
+    any_spec, vmem = pl.BlockSpec(memory_space=pl.ANY), pl.BlockSpec(memory_space=pltpu.VMEM)
+
+    def buffer(kind, *shape):
+        return pltpu.VMEM(shape, kind)
+
     return pl.pallas_call(
-        functools.partial(attend_back_kernel, tok_dev),
-        grid=(HEADS,),
-        in_specs=[head(x.shape[0]) for x in (q, kr, vr, kc, vc, do)] + [stat, stat],
-        out_specs=[head(rows) for rows in outs],
-        out_shape=[jax.ShapeDtypeStruct((rows, D), BF16) for rows in outs],
+        functools.partial(backward_kernel, panels, lines),
+        out_shape=[
+            jax.ShapeDtypeStruct((panels, rows, wide), BF16),
+            jax.ShapeDtypeStruct((tok_dev, D), F32),
+            jax.ShapeDtypeStruct((4, D), F32),
+        ],
+        in_specs=[any_spec] * (1 + len(arrays)) + [vmem] * 2,
+        out_specs=[vmem, any_spec, vmem],
         scratch_shapes=[
-            pltpu.VMEM((raw_rows, HEAD_DIM), F32),
-            pltpu.VMEM((raw_rows, HEAD_DIM), F32),
-            pltpu.VMEM((comp_rows, HEAD_DIM), F32),
-            pltpu.VMEM((comp_rows, HEAD_DIM), F32),
+            buffer(BF16, HELD, pairs, 2, 2, 2, 2, rows, wide),
+            buffer(BF16, RING, pairs, 2, 2, 2, rows, wide),
+            buffer(BF16, RING, 2, pairs, 2, rows, wide),
+            buffer(BF16, RING, 2, pairs, rows, wide),
+            buffer(BF16, panels, lines, rows, wide),
+            buffer(BF16, raw, D),
+            buffer(BF16, D, tok_dev),
+            buffer(BF16, comp, D),
+            buffer(BF16, 3, comp_dev, D),
+            buffer(F32, tok_dev, D),
+            buffer(F32, tok_dev, D),
+            buffer(F32, tok_dev, D),
+            buffer(BF16, max(comp, 2 * tok_dev), D),
+            buffer(BF16, tok_dev, D),
+            buffer(BF16, raw, HEAD_DIM),
+            buffer(BF16, raw, HEAD_DIM),
+            buffer(BF16, comp, HEAD_DIM),
+            buffer(BF16, comp, HEAD_DIM),
+            buffer(F32, raw, HEAD_DIM),
+            buffer(F32, raw, HEAD_DIM),
+            buffer(F32, comp, HEAD_DIM),
+            buffer(F32, comp, HEAD_DIM),
+            buffer(BF16, raw, D),
+            buffer(BF16, raw, D),
+            buffer(BF16, comp, D),
+            buffer(BF16, comp, D),
+            buffer(BF16, 3, pairs, 2, 2, rows, D),
+            buffer(BF16, comp_dev, D),
+            buffer(BF16, reach, comp_dev, D),
+            buffer(BF16, raw_devs - 1, tok_dev, D),
+            buffer(F32, 4, 4, D),
+            buffer(F32, 3, 4, D),
+            buffer(F32, lines, 4, D),
+            dma((RING,)), dma((RING,)),
+            dma((RING, 2)), dma((RING, 2)),
+            dma((RING, 2)), dma((RING, 2)),
+            dma((panels, lines)), dma((panels, lines)),
+            regular, regular((2,)), regular((2,)),
+            dma((2,)), dma((11,)), dma((4,)), dma((3,)),
+            dma((reach + 1,)), dma((reach + 1,)),
+            dma((raw_devs,)), dma((raw_devs,)),
+            dma((3,)), dma((3,)),
+            dma((lines,)), dma((lines,)),
         ],
-        compiler_params=pltpu.CompilerParams(vmem_limit_bytes=40 * MIB),
-        name="attend_back",
-    )(q, kr, vr, kc, vc, do, lse, delta)
+        compiler_params=pltpu.CompilerParams(
+            collective_id=1, has_side_effects=True, vmem_limit_bytes=62 * MIB
+        ),
+        name="backward",
+    )(weights, *arrays, lse, norm_params)
 
 
 def local(
@@ -823,67 +1169,16 @@
     )
     row_valid = (positions % S < row_counts).astype(F32)
 
-    inputs = tokens.astype(F32)
     tokens3 = tokens.reshape(comp_dev, 3, D).transpose(1, 0, 2)
-    grad_out = cotangent.astype(F32) * row_valid[:, None]
-    grad_out_low = grad_out.astype(BF16)
-    (
-        weights, normed_raw, compressed, queries, keys_raw, values_raw, keys_comp, values_comp,
-        attended_sum, active, grad_pre, normed_two, hidden, grad_normed_two, log_total, mixed,
-    ) = forward(block, tokens, tokens3, grad_out_low, row_valid[:, None], norm_params, lines)
-    weights = weights.reshape(PANELS, D, D)
-    key_weight, value_weight, query_weight, out_weight = [weights[i] for i in range(3, 7)]
-    conv_weight = weights[:3]
-    raw_devs = raw_devices(tok_dev)
-    comp_first = comp_window_first(seq_index, tok_dev)
-    normed = normed_raw[(raw_devs - 1) * tok_dev :]
-    attended = attended_sum.astype(BF16)
-    norm_value, norm_two_back = jax.vjp(layer_norm, hidden, norm_params[2], norm_params[3])
-    grad_hidden_norm, grad_gain_two, grad_shift_two = norm_two_back(grad_normed_two)
-    grad_hidden = grad_out + grad_hidden_norm
-    grad_branch = grad_hidden.astype(BF16)
-    grad_attended = times_transposed(grad_branch, out_weight).astype(BF16)
-    delta = jnp.sum(
-        (grad_attended.astype(F32) * attended_sum).reshape(tok_dev, HEADS, HEAD_DIM), -1
-    ).T
-    delta = jnp.broadcast_to(delta[:, None, :], (HEADS, 8, tok_dev))
-    grad_queries, dkr, dvr, dkc, dvc = attend_back(
-        queries, keys_raw, values_raw, keys_comp, values_comp, grad_attended, log_total, delta
-    )
-
-    grad_comp = (times_transposed(dkc, key_weight) + times_transposed(dvc, value_weight)).astype(BF16)
-    placed = lax.dynamic_update_slice_in_dim(
-        jnp.zeros((seq_count * comp_dev, D), BF16), grad_comp, comp_first * comp_dev, 0
-    )
-    grad_compressed = lax.psum_scatter(placed, "seq", scatter_dimension=0, tiled=True)
-    grad_raw = times_transposed(dkr, key_weight) + times_transposed(dvr, value_weight)
-    grad_normed = grad_raw[(raw_devs - 1) * tok_dev :]
-    for back in range(1, raw_devs):
-        rows = grad_raw[(raw_devs - 1 - back) * tok_dev : (raw_devs - back) * tok_dev].astype(BF16)
-        pairs = [(s, s - back) for s in range(back, seq_count)]
-        grad_normed = grad_normed + lax.ppermute(rows, "seq", pairs).astype(F32)
-    grad_normed = grad_normed + times_transposed(grad_queries, query_weight)
-    grad_windows = times_transposed(grad_compressed, conv_weight.reshape(3 * D, D))
-    grad_normed = grad_normed + grad_windows.reshape(tok_dev, D)
-    norm_value_one, norm_one_back = jax.vjp(layer_norm, inputs, norm_params[0], norm_params[1])
-    grad_inputs_norm, grad_gain_one, grad_shift_one = norm_one_back(grad_normed)
-    input_grad = grad_hidden + grad_inputs_norm
-    norm_local = jnp.stack([grad_gain_one, grad_shift_one, grad_gain_two, grad_shift_two], 0)
-    norm_grad = lax.psum(norm_local, ("grp", "seq"))
-
-    windows = normed.reshape(comp_dev, 3, D)
-    grads = [
-        contract_rows(normed, grad_queries),
-        contract_rows(normed_raw, dkr) + contract_rows(compressed, dkc),
-        contract_rows(normed_raw, dvr) + contract_rows(compressed, dvc),
-        contract_rows(attended, grad_branch),
-    ]
-    grads = grads + [contract_rows(grad_pre[:, i * D : (i + 1) * D], normed_two) for i in range(RATIO)]
-    grads = grads + [contract_rows(active[:, i * D : (i + 1) * D], grad_out_low) for i in range(RATIO)]
-    grads = grads + [contract_rows(windows[:, i], grad_compressed) for i in range(3)]
-    row_grads = reduce_panels(jnp.stack([g.astype(BF16) for g in grads], 0), lines)
-
-    slotted = row_grads[slot_panel].astype(F32) * scale_all[:, None, None]
+    grad_out = (cotangent.astype(F32) * row_valid[:, None]).astype(BF16)
+    results = forward(block, tokens, tokens3, grad_out, row_valid[:, None], norm_params, lines)
+    weights, saved, log_total, mixed = results[0], results[1:-2], results[-2], results[-1]
+    a_win, c_win, q, kr, vr, kc, vc, o, z, df, b, h, db, a3 = saved
+    arrays = (a_win, c_win, a3, q, kr, vr, kc, vc, o, z, df, b, h, db, grad_out, tokens)
+    row_grads, input_grad, norm_grad = backward(weights, arrays, log_total, norm_params, lines)
+
+    place = jnp.argsort(jnp.array(RETURN, jnp.int32))
+    slotted = row_grads[place[slot_panel]].astype(F32) * scale_all[:, None, None]
     slotted = jnp.where(slot_used[:, None, None], slotted, 0.0).astype(BF16)
     slotted = slotted.reshape(group_count, slot_count, slot_rows, wide)
     slot_parts = lax.all_to_all(slotted, "grp", 0, 0, tiled=True)

time: 672 us -> 566 us (0.84)
  Pallas kernels: 407 us -> 489 us
  matrix products: 64.7 us -> 0 us
  local copies, waits for them, and re-layouts: 77.1 us -> 20.1 us
  blocking collectives: 44.2 us -> 0 us
  between operations: 15 us -> 1.38 us
  other arithmetic: 23.8 us -> 11.7 us
  waiting for transfers between devices: 21.8 us -> 29.8 us
    pallas_call x2 -> x1, Pallas kernels: 189 us -> 272 us  [backward(): pl.pallas_call(functools.partial(backward_kernel, panels, lines), out_sha...]
    dot_general x24 -> x0, matrix products: 64.7 us -> none  [the longest x17 37.4 us: contract_rows(): lax.dot_general(left, right, (((0,), (0,)), ((), ())), preferred_element_...]
    psum x1 -> x0, blocking collectives: 44.2 us -> none  [local(): norm_grad = lax.psum(norm_local, ('grp', 'seq'))]
    unnamed x115 -> x40, local copies, waits for them, and re-layouts: 44.2 us -> 9.28 us
    slice x6 -> x0, local copies, waits for them, and re-layouts: 18.8 us -> none  [the longest x1 6.7 us: local(): conv_weight = weights[:3]]
    all_to_all x1, waiting for transfers between devices: 0.01 us -> 17.4 us  [local(): slot_parts = lax.all_to_all(slotted, 'grp', 0, 0, tiled=True)]
    reduce_scatter x1 -> x0, waiting for transfers between devices: 8.92 us -> none  [local(): lax.psum_scatter(placed, 'seq', scatter_dimension=0, tiled=True)]
  transfers between devices with their start and end apart: 6 -> 2, of which waited for: 2 -> 2; matrix products, arithmetic and copies ran while one was open for 14% -> 2% of each run, Pallas kernels for 24% -> 0%
where the time goes in v3:
time: 566 us; the launch traced here: 561 us
  Pallas kernels  489 us (86%)
  waiting for transfers between devices  29.8 us (5%)
  local copies, waits for them, and re-layouts  20.1 us (4%)
  other arithmetic  11.7 us (2%)
  starting transfers between devices  8.86 us (2%)
    pallas_call x1, Pallas kernels, backward(): pl.pallas_call(functools.partial(backward_kernel, panels, lines), out_sha...  272 us
    pallas_call x1, Pallas kernels, forward(): pl.pallas_call(functools.partial(forward_kernel, panels, lines, 3), out_s...  218 us
    all_to_all x1, waiting for transfers between devices, local(): slot_parts = lax.all_to_all(slotted, 'grp', 0, 0, tiled=True)  17.4 us
    all_to_all x1, waiting for transfers between devices, local(): slots_in = lax.all_to_all(scaled, 'grp', 0, 0, tiled=True)  12.5 us
  transfers between devices with their start and end apart: 2, of which 2 were waited for; matrix products, arithmetic and copies ran while one was open for 2% of the time, Pallas kernels for 0%

profile of v3, /device:TPU:0, one launch (start us, length us, event | category | flops | bytes accessed | tf_op | source)
XLA Modules:
  0.0 561.1 jit_solution(9506155089389256524)
XLA Ops:
  0.7 2.4 copy.46
  3.6 1.2 copy.47
  4.9 5.3 all-to-all-start
  11.5 0.6 iota_compare_fusion.2
  12.5 0.7 gather_fusion
  13.7 1.2 copy.54
  15.0 0.7 convert_element_type.46.valid_ref
  15.8 0.7 gather_fusion.2
  16.6 1.1 multiply_convert_fusion.1.dy_ref.dy_hbm
  17.7 12.5 %all-to-all-done = bf16[4,6,128,256]{2,3,1,0:T(8,128)(2,1)} async-done(((bf16[4,6,128,256]{2,3,1,0:T(8,128)(2,1)}), bf16[4,6,128,256]{2,3,1,0:T(8,128)(2,1)}, u32[]{:S(2)}, u32[]{:S(2)}) %all-to-all-start) | async-done | bytes 1572896 | tf_op jit(solution)/shard_map/all_to_all | solution.py:1160
  30.1 1.7 copy.48
  31.9 1.6 gather_fusion.1
  33.4 217.5 %forward.1 = (bf16[15,2,2,2,128,1024]{5,4,3,2,1,0:T(8,128)(2,1)}, bf16[1536,1024]{1,0:T(8,128)(2,1)}, bf16[768,1024]{1,0:T(8,128)(2,1)}, bf16[384,1024]{1,0:T(8,...) custom-call(bf16[15,128,256]{2,1,0:T(8,128)(2,1)} %gather_fusion.1, ...), custom_call_target="tpu_custom_call" | custom-call | tf_op jit(solution)/shard_map/forward/pallas_call | solution.py:550
  250.9 271.7 %backward.1 = (bf16[15,128,256]{2,1,0:T(8,128)(2,1)}, f32[384,1024]{1,0:T(8,128)}, f32[4,1024]{1,0:T(4,128)}) custom-call(bf16[15,2,2,2,128,1024]{5,4,3,2,1,0:T(8,128)(2,1)} %get-tuple-element.34.full_ref, bf16[1536,1024]{1,0:T(8,128)(2,1)} %get-tuple-element.35.a_hbm, bf16[768,1024]{1,0:T(8,128)(2,1)} %get-tuple-element.36.c_hbm, ...), custom_call_target="tpu_custom_call" | custom-call | tf_op jit(solution)/shard_map/backward/pallas_call | solution.py:1076
  522.6 1.8 gather_fusion.3
  524.5 1.7 fusion.2
  526.2 3.6 all-to-all-start.1
  531.1 17.4 %all-to-all-done.1 = bf16[4,6,128,256]{3,2,1,0:T(8,128)(2,1)S(1)} async-done(((bf16[4,6,128,256]{3,2,1,0:T(8,128)(2,1)}), bf16[4,6,128,256]{3,2,1,0:T(8,128)(2,1)S(1)}, u32[]{:S(2)}, u32[]{:S(2)}) %all-to-all-start.1) | async-done | bytes 1572896 | tf_op jit(solution)/shard_map/all_to_all | solution.py:1184
  549.3 1.4 copy-done.6
  550.7 1.9 copy-done.2
  552.6 0.9 copy-done.5
  553.5 4.6 multiply_subtract_fusion
  558.1 0.9 copy.58
  558.9 1.1 copy.59
  (60 shorter events, 5.6 us)
Async XLA Ops:
  0.6 2.4 copy-start
  0.7 2.4 copy-start.17
  3.6 7.3 %copy-start.15 = (s32[15]{0:T(128)S(1)}, s32[15]{0:T(128)}, u32[]{:S(2)}) copy-start(s32[15]{0:T(128)} %constant.102) | copy-start | bytes 184
  3.6 7.3 %copy-start.16 = (s32[4]{0:T(128)S(1)}, s32[4]{0:T(128)}, u32[]{:S(2)}) copy-start(s32[4]{0:T(128)} %param.23) | copy-start | bytes 52
  3.6 8.6 %copy-start.14 = (s32[4,6]{1,0:T(4,128)S(1)}, s32[4,6]{1,0:T(4,128)}, u32[]{:S(2)}) copy-start(s32[4,6]{1,0:T(4,128)} %param.22) | copy-start | bytes 292
  3.6 9.6 %copy-start.4 = (bf16[384,1024]{1,0:T(8,128)(2,1)S(1)}, bf16[384,1024]{1,0:T(8,128)(2,1)}, u32[]{:S(2)}) copy-start(bf16[384,1024]{1,0:T(8,128)(2,1)} %tok_hbm.1) | copy-start | bytes 2359300
  4.9 11.0 %copy-start.1 = (s32[15]{0:T(128)S(1)}, s32[15]{0:T(128)}, u32[]{:S(2)}) copy-start(s32[15]{0:T(128)} %constant.101) | copy-start | bytes 184
  4.9 25.3 %all-to-all-start = ((bf16[4,6,128,256]{2,3,1,0:T(8,128)(2,1)}), bf16[4,6,128,256]{2,3,1,0:T(8,128)(2,1)}, u32[]{:S(2)}, u32[]{:S(2)}) async-start(bf16[4,6,128,256]{2,3,1,0:T(8,128)(2,1)} %copy.47), calls=%async_computation | async-start | bytes 3145728 | tf_op jit(solution)/shard_map/all_to_all | solution.py:1160
  10.2 6.4 %copy-start.8 = (bf16[384,1024]{1,0:T(8,128)(2,1)S(1)}, bf16[384,1024]{1,0:T(8,128)(2,1)}, u32[]{:S(2)}) copy-start(bf16[384,1024]{1,0:T(8,128)(2,1)} %param.15) | copy-start | bytes 2359300
  524.5 5.4 copy-start.10
  524.5 5.4 copy-start.11
  524.5 5.4 copy-start.12
  524.5 5.4 copy-start.13
  526.2 22.2 %all-to-all-start.1 = ((bf16[4,6,128,256]{3,2,1,0:T(8,128)(2,1)}), bf16[4,6,128,256]{3,2,1,0:T(8,128)(2,1)S(1)}, u32[]{:S(2)}, u32[]{:S(2)}) async-start(bf16[4,6,128,256]{3,2,1,0:T(8,128)(2,1)} %fusion.2), calls=%async_computation.1 | async-start | bytes 3145728 | tf_op jit(solution)/shard_map/all_to_all | solution.py:1184
  548.5 2.2 copy-start.6
  548.9 3.7 copy-start.2
  548.9 4.6 copy-start.5
  549.3 8.8 %copy-start.3 = (f32[4,6,16,8,256]{4,3,0,2,1:T(8,128)}, f32[4,6,16,8,256]{4,3,0,2,1:T(8,128)S(1)}, u32[]{:S(2)}) copy-start(f32[4,6,16,8,256]{4,3,0,2,1:T(8,128)S(1)} %copy.52) | copy-start | bytes 9437188
  553.5 4.6 copy-start.9
  553.5 5.5 copy-start.7

commit v4 on v3

v4 whole, which is shorter than its diff:
```python
import functools

import jax
import jax.numpy as jnp
from jax import lax
from jax.experimental import pallas as pl
from jax.experimental.pallas import tpu as pltpu
from jax.sharding import PartitionSpec as P

D = 1024
HEADS = 8
HEAD_DIM = 128
FF = 4096
S = 512
CM = 512
STEP = 10
PANELS = 15
RATIO = FF // D
QB = 128
RAW_KEYS = 2 * S
COMP_KEYS = CM + QB
MIB = 1 << 20

NEG_SCORE = -1e30
NORM_EPS = 1e-05
BETA_ONE = 0.9
BETA_TWO = 0.999
WEIGHT_DECAY = 0.1
ADAM_EPS = 1e-08
NORM_RATE = 1.0
SLOT_RATE = 2.0
BF16 = jnp.bfloat16
F32 = jnp.float32
MESH = pl.DeviceIdType.MESH


def layer_norm(values, gain, shift):
    row_mean = jnp.mean(values, axis=-1, keepdims=True)
    centered = values - row_mean
    variance = jnp.mean(centered * centered, axis=-1, keepdims=True)
    return centered * lax.rsqrt(variance + NORM_EPS) * gain + shift


def panel_deviations():
    inner_dev = D ** (-0.5)
    deviations = [inner_dev] * 3 + [(D // (2 * S)) ** (-0.5)] + [inner_dev] * RATIO
    deviations = deviations + [FF ** (-0.5)] * RATIO + [(3 * D) ** (-0.5)] * 3
    return jnp.array(deviations, F32)


def adam_update(gradient, first_old, second_old, weight_old, step_rate):
    first_new = BETA_ONE * first_old + (1.0 - BETA_ONE) * gradient
    second_new = BETA_TWO * second_old + (1.0 - BETA_TWO) * gradient * gradient
    fix_one = 1.0 - BETA_ONE**STEP
    fix_two = 1.0 - BETA_TWO**STEP
    movement = first_new / fix_one / (jnp.sqrt(second_new / fix_two) + ADAM_EPS)
    return (first_new, second_new, weight_old - step_rate * (movement + WEIGHT_DECAY * weight_old))


def matmul(left, right):
    return jnp.dot(left, right, preferred_element_type=F32)


def times_transposed(left, right):
    return lax.dot_general(left, right, (((1,), (1,)), ((), ())), preferred_element_type=F32)


def contract_rows(left, right):
    return lax.dot_general(left, right, (((0,), (0,)), ((), ())), preferred_element_type=F32)


class Place:
    def __init__(self, lines):
        self.lines = lines
        self.grp = lax.axis_index("grp")
        self.seq = lax.axis_index("seq")
        self.line = self.seq // 2
        self.core = self.seq % 2
        self.row = self.grp // 2
        self.col = self.grp % 2
        self.grp_x = self.row * 2 + 1 - self.col
        self.grp_y = (1 - self.row) * 2 + self.col
        self.x_dev = {"grp": self.grp_x, "seq": self.seq}
        self.y_dev = {"grp": self.grp_y, "seq": self.seq}
        self.far_dev = {"grp": 3 - self.grp, "seq": self.seq}
        self.core_dev = {"grp": self.grp, "seq": self.line * 2 + 1 - self.core}

    def other_line(self, k):
        return lax.rem(self.line + k, self.lines)

    def line_dev(self, k):
        return {"grp": self.grp, "seq": self.other_line(k) * 2 + self.core}

    def seq_dev(self, d):
        count = 2 * self.lines
        return {"grp": self.grp, "seq": lax.rem(self.seq + d + count, count)}

    def announce(self):
        barrier = pltpu.get_barrier_semaphore()
        partners = [self.seq_dev(d) for d in range(1, 2 * self.lines)]
        for device in partners + [self.x_dev, self.y_dev, self.far_dev]:
            pl.semaphore_signal(barrier, inc=1, device_id=device, device_id_type=MESH)

    def enter(self):
        pl.semaphore_wait(pltpu.get_barrier_semaphore(), 2 * self.lines + 2)

    def exchange(self, parts, arrived, send, recv):
        count = parts.shape[0] // 4
        copies = []
        for i, device in enumerate((self.x_dev, self.y_dev, self.far_dev)):
            src = parts.at[pl.ds(device["grp"] * count, count)]
            dst = arrived.at[pl.ds(self.grp * count, count)]
            copies.append(remote(src, dst, send.at[i], recv.at[i], device))
        return copies


def remote(src, dst, send, recv, device):
    return pltpu.make_async_remote_copy(
        src_ref=src,
        dst_ref=dst,
        send_sem=send,
        recv_sem=recv,
        device_id=device,
        device_id_type=MESH,
    )


def memory_start(position):
    return (position // S - 1) * S


def comp_window_first(seq, tok_dev):
    return jnp.maximum(memory_start(seq * tok_dev) - 3 * CM, 0) // tok_dev


def raw_devices(tok_dev):
    return (RAW_KEYS - QB + tok_dev - 1) // tok_dev + 1


def comp_devices(tok_dev, seq_count):
    return min((3 * CM + S) // tok_dev + 1, seq_count)


def needs_raw(reader, owner, tok_dev):
    return (owner >= 0) & ((owner + 1) * tok_dev > memory_start(reader * tok_dev))


def needs_comp(reader, owner, tok_dev):
    last = jnp.maximum(memory_start(reader * tok_dev + tok_dev - 1), 0) // 3
    inside = (owner >= 0) & (owner >= comp_window_first(reader, tok_dev))
    return inside & (owner * (tok_dev // 3) < last)


def chip_needs_comp(reader, owner, tok_dev):
    even = reader // 2 * 2
    return needs_comp(even, owner, tok_dev) | needs_comp(even + 1, owner, tok_dev)


def chain_needs_comp(reader, owner, tok_dev, seq_count, reach):
    needed = chip_needs_comp(reader, owner, tok_dev)
    for ahead in range(2, reach + 1, 2):
        later = reader + ahead
        needed = needed | ((later < seq_count) & chip_needs_comp(later, owner, tok_dev))
    return needed & (owner >= 0) & (reader < seq_count)


def block_window(seq, i, tok_dev, raw_rows, comp_rows):
    position = seq * tok_dev + i * QB
    memory = memory_start(position)
    raw_base = (seq + 1) * tok_dev - raw_rows
    raw_at = jnp.minimum(memory - raw_base, raw_rows - RAW_KEYS)
    comp_end = jnp.maximum(memory, 0) // 3
    comp_low = jnp.maximum(comp_end - CM, 0)
    comp_base = comp_window_first(seq, tok_dev) * (tok_dev // 3)
    comp_at = jnp.minimum((comp_low - comp_base) // QB * QB, comp_rows - COMP_KEYS)
    return (
        position,
        pl.multiple_of(raw_at, QB),
        pl.multiple_of(comp_at, QB),
        raw_base + raw_at,
        comp_base + comp_at,
        memory,
        comp_low,
        comp_end,
    )


def row_sum(values):
    return jnp.sum(values, axis=1, keepdims=True)


def norm_rows(values, params, first):
    mean = row_sum(values) * (1.0 / D)
    centered = values - mean
    variance = row_sum(centered * centered) * (1.0 / D)
    gain, shift = params[first : first + 1, :], params[first + 1 : first + 2, :]
    return centered * lax.rsqrt(variance + NORM_EPS) * gain + shift


GELU_IN = (2.0 / 3.141592653589793) ** 0.5
GELU_CUBE = 0.044715


def gelu_pair(f):
    square = f * f
    t = jnp.tanh(GELU_IN * f * (1.0 + GELU_CUBE * square))
    half = 0.5 * (1.0 + t)
    slope = half + 0.5 * f * (1.0 - t * t) * (GELU_IN * (1.0 + 3.0 * GELU_CUBE * square))
    return f * half, slope


class Attention:
    def __init__(self, seq, i, tok_dev, raw_rows, comp_rows):
        place = block_window(seq, i, tok_dev, raw_rows, comp_rows)
        self.pos, raw_at, comp_at, self.raw_pos, self.comp_pos = place[:5]
        self.memory, self.comp_low, self.comp_end = place[5:]
        self.rows = pl.ds(i * QB, QB)
        self.raw = pl.ds(raw_at, RAW_KEYS)
        self.comp = pl.ds(comp_at, COMP_KEYS)

    def sees_raw(self, shape, key_dim):
        key_pos = self.raw_pos + lax.broadcasted_iota(jnp.int32, shape, key_dim)
        query_pos = self.pos + lax.broadcasted_iota(jnp.int32, shape, 1 - key_dim)
        return (key_pos >= jnp.maximum(self.memory, 0)) & (key_pos <= query_pos)

    def sees_comp(self, shape, key_dim):
        index = self.comp_pos + lax.broadcasted_iota(jnp.int32, shape, key_dim)
        return (index >= self.comp_low) & (index < self.comp_end)


def attend_head(seq, tok_dev, cols, q, kr, vr, kc, vc, out, lse, lse_row):
    scale = HEAD_DIM ** (-0.5)
    for i in range(tok_dev // QB):
        at = Attention(seq, i, tok_dev, kr.shape[0], kc.shape[0])
        query = q[at.rows, cols]
        raw = times_transposed(query, kr[at.raw, cols]) * scale
        raw = jnp.where(at.sees_raw(raw.shape, 1), raw, NEG_SCORE)
        comp = times_transposed(query, kc[at.comp, cols]) * scale
        comp = jnp.where(at.sees_comp(comp.shape, 1), comp, NEG_SCORE)
        top = jnp.maximum(
            jnp.max(raw, axis=1, keepdims=True), jnp.max(comp, axis=1, keepdims=True)
        )
        raw = jnp.exp(raw - top)
        comp = jnp.exp(comp - top)
        total = row_sum(raw) + row_sum(comp)
        mixed = matmul(raw.astype(BF16), vr[at.raw, cols])
        mixed = mixed + matmul(comp.astype(BF16), vc[at.comp, cols])
        out[at.rows, cols] = mixed / total
        stat = jnp.broadcast_to(top + jnp.log(total), (QB, QB))
        lse[lse_row, :, at.rows] = stat.T[:8]


TAPS = [4 + 2 * RATIO + i for i in range(3)]
ARRIVAL = TAPS + [0, 1, 2, 3]
for _i in range(RATIO):
    ARRIVAL = ARRIVAL + [4 + _i, 4 + RATIO + _i]
AHEAD = 4
LAG = 4
SEMS = 8
KEPT = 4


def forward_kernel(
    panels, lines,
    scale_ref, order_ref, master_ref, tok_ref, tok3_ref, dy_ref, valid_ref, norm_ref,
    full_ref, a_out, c_out, q_out, kr_out, vr_out, kc_out, vc_out, o_out, z_out, df_out, b_out,
    h_out, db_out, a3_out, lse_ref, mixed_ref,
    wbuf, a_win, a3, c_win, q, kr, vr, kc, vc, o, z, df, b, h, y, db, slots, slots_in, block,
    own_sem, zs, zr, s1, r1, s2, r2, cs, cr, wsem, a_s, a_r, c_s, c_r, f_s, f_r, es, er, out_sem,
):
    at = Place(lines)
    seq = at.seq
    seq_count = 2 * lines
    chunks = 2 * panels
    tok_dev = tok_ref.shape[0]
    comp_dev = tok_dev // 3
    raw_devs = a_win.shape[0] // tok_dev
    comp_devs = c_win.shape[0] // comp_dev
    reach = min(seq_count - 1, (2 * S + 3 * CM + tok_dev - 1) // tok_dev)
    wide = block.shape[-1]
    half_rows = block.shape[1] // 2

    def cols(g):
        return pl.ds(pl.multiple_of(g * wide, wide), wide)

    def rows_of(u):
        return pl.ds(pl.multiple_of(u % 2 * half_rows, half_rows), half_rows)

    def line_place(u, line):
        return full_ref.at[u // 2, line // 2, line % 2, at.core, rows_of(u), cols(at.grp)]

    def line_copy(u, k):
        src = block.at[u // 2, rows_of(u), :]
        return remote(src, line_place(u, at.line), zs.at[u, k], zr.at[u, at.line], at.line_dev(k))

    def line_arrival(u, k):
        src, line = block.at[u // 2, rows_of(u), :], at.other_line(k)
        return remote(src, line_place(u, line), zs.at[u, k], zr.at[u, line], at.line_dev(k))

    def part(u, half, g):
        return full_ref.at[u // 2, :, half, at.core, rows_of(u), cols(g)]

    def first(u, half, g):
        device, i = (at.x_dev if half == 0 else at.y_dev), u % SEMS
        return remote(part(u, half, g), part(u, half, g), s1.at[i, half], r1.at[i, half], device)

    def second(u, half, j, g):
        device, i = (at.y_dev if half == 0 else at.x_dev), u % SEMS
        ref = part(u, half, g)
        return remote(ref, ref, s2.at[i, half, j], r2.at[i, half, j], device)

    def cross(u, half, core):
        ref, i = full_ref.at[u // 2, :, half, core, rows_of(u)], u % SEMS
        return remote(ref, ref, cs.at[i, half], cr.at[i, half], at.core_dev)

    def load(u):
        src = full_ref.at[u // 2, :, :, :, rows_of(u)]
        dst = wbuf.at[u // 2 % KEPT, :, :, :, rows_of(u)]
        return pltpu.make_async_copy(src, dst, wsem.at[u % SEMS])

    def start_lines(u):
        for k in range(1, lines):
            line_copy(u, k).start()

    def start_first(u):
        for k in range(1, lines):
            line_arrival(u, k).wait_recv()
        for half in (0, 1):
            first(u, half, at.grp).start()

    def start_second(u):
        for half in (0, 1):
            near = at.grp_x if half == 0 else at.grp_y
            first(u, half, near).wait_recv()
            second(u, half, 0, at.grp).start()
            second(u, half, 1, near).start()

    def start_cross(u):
        for half in (0, 1):
            second(u, half, 0, at.grp_y if half == 0 else at.grp_x).wait_recv()
            second(u, half, 1, 3 - at.grp).wait_recv()
            cross(u, half, at.core).start()

    def finish(u):
        for half in (0, 1):
            cross(u, half, 1 - at.core).wait_recv()
            first(u, half, at.grp).wait_send()
            second(u, half, 0, at.grp).wait_send()
            second(u, half, 1, at.grp_x if half == 0 else at.grp_y).wait_send()
            cross(u, half, at.core).wait_send()
        for k in range(1, lines):
            line_copy(u, k).wait_send()
        load(u).start()

    def a_rows(d):
        return a_win.at[pl.ds((raw_devs - 1 - d) * tok_dev, tok_dev), :]

    def a_copy(d, place, i, device):
        return remote(a_rows(d), a_rows(place), a_s.at[i], a_r.at[place - 1], device)

    def a_next():
        return a_copy(0, 2, 0, at.seq_dev(2))

    def a_beside():
        return a_copy(0, 1, 1, at.core_dev)

    def a_on(place):
        return a_copy(2, place, 2, at.core_dev)

    odd = at.core == 1
    even = at.core == 0
    gives_next = (seq + 2 < seq_count) & needs_raw(seq + 2, seq, tok_dev)
    gives_beside = even & needs_raw(seq + 1, seq, tok_dev)
    gives_on_far = even & needs_raw(seq + 1, seq - 2, tok_dev)
    gives_on_near = odd & needs_raw(seq - 1, seq - 2, tok_dev)

    def c_rows(reader, owner):
        place = jnp.clip(owner - comp_window_first(reader, tok_dev), 0, comp_devs - 1)
        return c_win.at[pl.ds(pl.multiple_of(place * comp_dev, comp_dev), comp_dev), :]

    def c_from(d):
        return own_c if d == 0 else c_rows(seq, seq - d)

    def c_next(d):
        dst = c_rows(seq + 2, seq - d)
        return remote(c_from(d), dst, c_s.at[d // 2], c_r.at[d // 2 + 1], at.seq_dev(2))

    def c_arrival(d):
        return remote(own_c, c_rows(seq, seq - d), c_s.at[0], c_r.at[d // 2], at.seq_dev(2))

    def c_across(d):
        other = seq + 1 - 2 * at.core
        dst = c_rows(other, seq - d)
        return remote(c_from(d), dst, f_s.at[d // 2], f_r.at[d // 2], at.core_dev)

    def c_across_arrival(d):
        other = seq + 1 - 2 * at.core
        return remote(own_c, c_rows(seq, other - d), f_s.at[0], f_r.at[d // 2], at.core_dev)

    steps_back = [d for d in range(0, reach + 1, 2)]

    def gives_c(d):
        return chain_needs_comp(seq + 2, seq - d, tok_dev, seq_count, reach - 1)

    def takes_c(d):
        return chain_needs_comp(seq, seq - d, tok_dev, seq_count, reach - 1)

    def gives_c_across(d):
        return needs_comp(seq + 1 - 2 * at.core, seq - d, tok_dev)

    def takes_c_across(d):
        return needs_comp(seq, seq + 1 - 2 * at.core - d, tok_dev)

    def pass_c(d):
        if d > 0:
            pl.when(takes_c(d))(lambda: c_arrival(d).wait_recv())
        pl.when(gives_c(d))(lambda: c_next(d).start())
        pl.when(gives_c_across(d))(lambda: c_across(d).start())

    outs = [
        (a_win, a_out), (c_win, c_out), (q, q_out), (kr, kr_out), (vr, vr_out), (kc, kc_out),
        (vc, vc_out), (o, o_out), (z, z_out), (df, df_out), (b, b_out), (h, h_out), (db, db_out),
        (a3, a3_out),
    ]

    def flush(*names):
        for i, (src, dst) in enumerate(outs):
            if any(src is name for name in names):
                pltpu.make_async_copy(src, dst, out_sem.at[i]).start()

    at.announce()
    count = master_ref.shape[0]
    for j in range(count):
        scaled = (master_ref[j] * scale_ref[j]).astype(BF16)
        for g in range(4):
            slots[g * count + j] = scaled[:, g * wide : (g + 1) * wide]
    at.enter()
    handed = at.exchange(slots, slots_in, es, er)
    for copy in handed:
        copy.start()
    slots_in[pl.ds(at.grp * count, count)] = slots[pl.ds(at.grp * count, count)]

    params = norm_ref[...]
    for i in range(tok_dev // QB):
        rows = pl.ds(i * QB, QB)
        mine = norm_rows(tok_ref[rows, :].astype(F32), params, 0).astype(BF16)
        a_win[pl.ds((raw_devs - 1) * tok_dev + i * QB, QB), :] = mine
    pl.when(gives_next)(lambda: a_next().start())
    pl.when(gives_beside)(lambda: a_beside().start())
    for d in range(1, raw_devs):
        absent = jnp.logical_not(needs_raw(seq, seq - d, tok_dev))

        @pl.when(absent)
        def _(d=d):
            a_rows(d)[...] = jnp.zeros((tok_dev, D), BF16)

    for k in range(3):
        a3[k] = norm_rows(tok3_ref[k].astype(F32), params, 0).astype(BF16)
    for i in range(comp_devs):
        owner = comp_window_first(seq, tok_dev) + i
        taken = needs_comp(seq, owner, tok_dev)
        for d in steps_back[1:]:
            taken = taken | ((owner == seq - d) & takes_c(d))

        @pl.when(jnp.logical_not(taken))
        def _(i=i):
            c_win[pl.ds(i * comp_dev, comp_dev), :] = jnp.zeros((comp_dev, D), BF16)

    for copy in handed:
        copy.wait_recv()
    for p in range(panels):
        block[p] = slots_in[order_ref[p]]
    for u in range(AHEAD):
        start_lines(u)
    own_place = full_ref.at[:, at.line // 2, at.line % 2, at.core, :, cols(at.grp)]
    own = pltpu.make_async_copy(block, own_place, own_sem)
    own.start()
    own.wait()

    own_c = b.at[pl.ds(0, comp_dev), :]
    tile = 8 * half_rows

    def weight(slot, col):
        return wbuf[slot, :, :, :, :, col].reshape(D, wide)

    def columns(body):
        def one(j, carry):
            body(pl.ds(pl.multiple_of(j * wide, wide), wide))
            return carry

        lax.fori_loop(0, D // wide, one, 0)

    def tap(k, slot):
        def body(col):
            part_sum = matmul(a3[k], weight(slot, col))
            if k == 0:
                y[pl.ds(0, comp_dev), col] = part_sum
            elif k == 1:
                y[pl.ds(0, comp_dev), col] += part_sum
            else:
                own_c[:, col] = (y[pl.ds(0, comp_dev), col] + part_sum).astype(BF16)

        columns(body)

    def project(dst, src, slot):
        block_rows = min(src.shape[0], tok_dev)

        def body(col):
            for i in range(src.shape[0] // block_rows):
                rows = pl.ds(i * block_rows, block_rows)
                dst[rows, col] = matmul(src[rows, :], weight(slot, col)).astype(BF16)

        columns(body)

    def heads(low, high):
        def one(i, carry):
            col = pl.ds(pl.multiple_of(i * HEAD_DIM, HEAD_DIM), HEAD_DIM)
            attend_head(seq, tok_dev, col, q, kr, vr, kc, vc, o, lse_ref, i)
            return carry

        lax.fori_loop(low, high, one, 0)

    def hidden(pair, low, high):
        up, down = (2 * pair + 7) % KEPT, (2 * pair + 8) % KEPT

        def one(i, carry):
            up_rows = wbuf[up, i].reshape(tile, D)
            down_rows = wbuf[down, i].reshape(tile, D)
            value, slope = gelu_pair(times_transposed(b[...], up_rows))
            units = pl.ds(pl.multiple_of(pair * D + i * tile, tile), tile)
            z[:, units] = value.astype(BF16)
            df[:, units] = (times_transposed(dy_ref[...], down_rows) * slope).astype(BF16)
            return carry

        lax.fori_loop(low, high, one, 0)

    def gather_hidden(pair):
        up, down = (2 * pair + 7) % KEPT, (2 * pair + 8) % KEPT
        units = pl.ds(pl.multiple_of(pair * D, D), D)

        def body(col):
            y[:, col] += matmul(z[:, units], weight(down, col))
            db[:, col] += matmul(df[:, units], weight(up, col))

        columns(body)

    def work(w):
        slot = w // 2 % KEPT
        for k in range(3):
            pl.when(w == 2 * k)(lambda k=k: tap(k, slot))

        @pl.when(w == 1)
        def _():
            for copy in handed:
                copy.wait_send()
            pl.when(needs_raw(seq, seq - 2, tok_dev))(lambda: a_next().wait_recv())
            pl.when(gives_on_far)(lambda: a_on(3).start())
            pl.when(gives_on_near)(lambda: a_on(1).start())

        pl.when(w == 4)(lambda: pass_c(0))

        @pl.when(w == 5)
        def _():
            pl.when(even & needs_raw(seq, seq - 1, tok_dev))(lambda: a_on(1).wait_recv())
            pl.when(odd & needs_raw(seq, seq - 1, tok_dev))(lambda: a_beside().wait_recv())
            pl.when(needs_raw(seq, seq - 3, tok_dev))(lambda: a_on(3).wait_recv())
            pl.when(gives_next)(lambda: a_next().wait_send())
            pl.when(gives_beside)(lambda: a_beside().wait_send())
            pl.when(gives_on_far)(lambda: a_on(3).wait_send())
            pl.when(gives_on_near)(lambda: a_on(1).wait_send())
            flush(a_win, a3)

        @pl.when(w == 6)
        def _():
            project(q, a_win.at[pl.ds((raw_devs - 1) * tok_dev, tok_dev), :], slot)
            flush(q)

        for i, d in enumerate(steps_back[1:]):
            pl.when(w == 6 + 2 * i)(lambda d=d: pass_c(d))

        @pl.when(w == 8)
        def _():
            project(kr, a_win, slot)
            flush(kr)

        @pl.when(w == 10)
        def _():
            project(vr, a_win, slot)
            flush(vr)

        @pl.when(w == 12)
        def _():
            for d in steps_back:
                pl.when(takes_c_across(d))(lambda d=d: c_across_arrival(d).wait_recv())
            flush(c_win)
            project(kc, c_win, 4 % KEPT)
            project(vc, c_win, 5 % KEPT)
            flush(kc, vc)

        @pl.when((w >= 13) & (w < 17))
        def _():
            low = (w - 13) * (HEADS // 4)
            heads(low, low + HEADS // 4)

        @pl.when(w == 17)
        def _():
            flush(o)
            for d in steps_back:
                pl.when(gives_c(d))(lambda d=d: c_next(d).wait_send())
                pl.when(gives_c_across(d))(lambda d=d: c_across(d).wait_send())

            def body(col):
                sent = matmul(o[...].astype(BF16), weight(6 % KEPT, col))
                h[:, col] = tok_ref[:, col].astype(F32) + sent

            columns(body)
            for i in range(tok_dev // QB):
                rows = pl.ds(i * QB, QB)
                b[rows, :] = norm_rows(h[rows, :], params, 2).astype(BF16)
            y[...] = h[...]
            db[...] = jnp.zeros_like(db)
            flush(b, h)

        turn = w - 16
        lines_half = wbuf.shape[1] // 2
        first_turn = ((turn >= 4) & (turn % 4 == 0)) | (turn == 2)
        second_turn = ((turn >= 4) & (turn % 4 == 1)) | (turn == 3)
        pl.when(first_turn)(lambda: hidden(turn // 4, 0, lines_half))

        @pl.when(second_turn)
        def _():
            hidden(turn // 4, lines_half, 2 * lines_half)
            gather_hidden(turn // 4)

    def step(t, carry):
        pl.when(t + AHEAD < chunks)(lambda: start_lines(t + AHEAD))
        pl.when(t < chunks)(lambda: start_first(t))
        pl.when((t >= 1) & (t < chunks + 1))(lambda: start_second(t - 1))
        pl.when((t >= 2) & (t < chunks + 2))(lambda: start_cross(t - 2))

        pl.when((t >= LAG) & (t < chunks + LAG))(lambda: load(t - LAG).wait())
        pl.when(t >= LAG + 1)(lambda: work(t - LAG - 1))
        pl.when((t >= 3) & (t < chunks + 3))(lambda: finish(t - 3))
        return carry

    lax.fori_loop(0, chunks + LAG + 1, step, 0)
    flush(z, df, db)
    mixed_ref[...] = (y[...] * valid_ref[...]).astype(BF16)
    for i, (src, dst) in enumerate(outs):
        pltpu.make_async_copy(src, dst, out_sem.at[i]).wait()


def forward(scale, order, master, tokens, tokens3, grad_out, valid, norm_params, lines):
    panels, slot_count, rows = order.shape[0], master.shape[0], master.shape[1]
    wide = D // 4
    tok_dev = tokens.shape[0]
    raw = raw_devices(tok_dev) * tok_dev
    comp = comp_devices(tok_dev, 2 * lines) * (tok_dev // 3)
    dma = pltpu.SemaphoreType.DMA
    shapes = [
        ((raw, D), BF16), ((comp, D), BF16), ((tok_dev, D), BF16), ((raw, D), BF16),
        ((raw, D), BF16), ((comp, D), BF16), ((comp, D), BF16), ((tok_dev, D), F32),
        ((tok_dev, FF), BF16), ((tok_dev, FF), BF16), ((tok_dev, D), BF16), ((tok_dev, D), F32),
        ((tok_dev, D), F32), ((3, tok_dev // 3, D), BF16),
    ]
    scratch = [pltpu.VMEM(shape, kind) for shape, kind in shapes]
    scratch.insert(1, scratch.pop())
    scratch.insert(len(scratch) - 1, pltpu.VMEM((tok_dev, D), F32))
    any_spec, vmem = pl.BlockSpec(memory_space=pl.ANY), pl.BlockSpec(memory_space=pltpu.VMEM)
    smem = pl.BlockSpec(memory_space=pltpu.SMEM)
    return pl.pallas_call(
        functools.partial(forward_kernel, panels, lines),
        out_shape=[jax.ShapeDtypeStruct((panels, lines // 2, 2, 2, rows, D), BF16)]
        + [jax.ShapeDtypeStruct(shape, kind) for shape, kind in shapes]
        + [jax.ShapeDtypeStruct((HEADS, 8, tok_dev), F32), jax.ShapeDtypeStruct((tok_dev, D), BF16)],
        in_specs=[smem] * 2 + [vmem] * 6,
        out_specs=[any_spec] * (1 + len(shapes)) + [vmem] * 2,
        scratch_shapes=[pltpu.VMEM((KEPT, lines // 2, 2, 2, rows, D), BF16)]
        + scratch
        + [
            pltpu.VMEM((4 * slot_count, rows, wide), BF16),
            pltpu.VMEM((4 * slot_count, rows, wide), BF16),
            pltpu.VMEM((panels, rows, wide), BF16),
            dma(()),
            dma((2 * panels, lines)), dma((2 * panels, lines)),
            dma((SEMS, 2)), dma((SEMS, 2)),
            dma((SEMS, 2, 2)), dma((SEMS, 2, 2)),
            dma((SEMS, 2)), dma((SEMS, 2)),
            dma((SEMS,)),
            dma((3,)), dma((3,)), dma((5,)), dma((5,)), dma((5,)), dma((5,)),
            dma((3,)), dma((3,)),
            dma((len(shapes),)),
        ],
        compiler_params=pltpu.CompilerParams(
            collective_id=0, has_side_effects=True, vmem_limit_bytes=60 * MIB
        ),
        name="forward",
    )(scale, order, master, tokens, tokens3, grad_out, valid, norm_params)


RETURN = [4 + RATIO + _i for _i in range(RATIO)] + [4 + _i for _i in range(RATIO)] + [3, 0, 1, 2] + TAPS
RING = 4
HELD = 5
BACK_LAG = 4


def norm_back(grad, values, params, first):
    mean = row_sum(values) * (1.0 / D)
    centered = values - mean
    scale = lax.rsqrt(row_sum(centered * centered) * (1.0 / D) + NORM_EPS)
    unit = centered * scale
    inner = grad * params[first : first + 1, :]
    back = inner - row_sum(inner) * (1.0 / D) - unit * (row_sum(inner * unit) * (1.0 / D))
    gain = jnp.sum(grad * unit, axis=0, keepdims=True)
    return back * scale, gain, jnp.sum(grad, axis=0, keepdims=True)


def attend_head_back(
    seq, tok_dev, cols, q, do, o, kr, vr, kc, vc, lse, lse_row, dkr, dvr, dkc, dvc,
    acc_kr, acc_vr, acc_kc, acc_vc,
):
    scale = HEAD_DIM ** (-0.5)
    for acc in (acc_kr, acc_vr, acc_kc, acc_vc):
        acc[...] = jnp.zeros_like(acc)
    for i in range(tok_dev // QB):
        at = Attention(seq, i, tok_dev, kr.shape[0], kc.shape[0])
        query = q[at.rows, cols]
        grad = do[at.rows, cols]
        delta = row_sum(grad.astype(F32) * o[at.rows, cols])
        delta = jnp.broadcast_to(delta, (QB, QB)).T[0:1]
        stat = lse[lse_row, 0:1, at.rows]

        def part(k_ref, v_ref, acc_k, acc_v, keys, seen):
            k = k_ref[keys, :]
            s = times_transposed(k, query) * scale
            p = jnp.where(seen, jnp.exp(jnp.where(seen, s, NEG_SCORE) - stat), 0.0)
            dp = times_transposed(v_ref[keys, :], grad)
            ds = (p * (dp - delta)).astype(BF16)
            acc_v[keys, :] += matmul(p.astype(BF16), grad)
            acc_k[keys, :] += matmul(ds, query)
            return contract_rows(ds, k)

        dq = part(kr, vr, acc_kr, acc_vr, at.raw, at.sees_raw((RAW_KEYS, QB), 0))
        seen = at.sees_comp((COMP_KEYS, QB), 0)
        dq = dq + part(kc, vc, acc_kc, acc_vc, at.comp, seen)
        q[at.rows, cols] = (dq * scale).astype(BF16)
    dkr[:, cols] = (acc_kr[...] * scale).astype(BF16)
    dkc[:, cols] = (acc_kc[...] * scale).astype(BF16)
    dvr[:, cols] = acc_vr[...].astype(BF16)
    dvc[:, cols] = acc_vc[...].astype(BF16)


def backward_kernel(
    panels, lines,
    place_ref, slot_scale_ref,
    full_ref, a_hbm, c_hbm, a3_hbm, q_hbm, kr_hbm, vr_hbm, kc_hbm, vc_hbm, o_hbm, z_hbm, df_hbm,
    b_hbm, h_hbm, db_hbm, dy_hbm, tok_hbm, lse_ref, norm_ref,
    slot_out, in_grad_out, norm_out,
    held, cross_in, first_in, second_in, line_in, out, slots, slots_in,
    opnd, lhs_t, c_win, a3, h, db, o, pair, q, kr, vr, kc, vc, acc_kr, acc_vr, acc_kc, acc_vc,
    dkr, dvr, dkc, dvc, wbuf, dc, dc_beside, dc_chain, da_in, n_src, n_in, n_line,
    cs, cr, s1, r1, s2, r2, zs, zr, free_cross, free_first, free_second,
    lsem, osem, hsem, wsem, dbs, dbr, dcs, dcr, das, dar, ns, nr, nzs, nzr, es, er,
):
    at = Place(lines)
    seq = at.seq
    seq_count = 2 * lines
    chunks = 2 * panels
    tok_dev = q.shape[0]
    comp_dev = tok_dev // 3
    raw_devs = dkr.shape[0] // tok_dev
    comp_devs = dkc.shape[0] // comp_dev
    reach = min(seq_count - 1, (2 * S + 3 * CM + tok_dev - 1) // tok_dev)
    wide = out.shape[-1]
    half_rows = out.shape[1] // 2
    pairs = lines // 2
    params = norm_ref[...]
    raw, comp = dkr.shape[0], dkc.shape[0]

    def token_rows(i):
        return pl.ds(pl.multiple_of(i * tok_dev, tok_dev), tok_dev)

    dhb, do = pair.at[token_rows(0), :], pair.at[token_rows(1), :]

    def mine(u):
        return held.at[u % HELD, :, :, at.core]

    def cross(u):
        src, i = held.at[u % HELD, :, :, 1 - at.core], u % RING
        return remote(src, cross_in.at[i], cs.at[i], cr.at[i], at.core_dev)

    def first(u, half):
        i = u % RING
        if half == 0:
            src, device = mine(u).at[:, 0, 1 - at.row], at.y_dev
        else:
            src, device = mine(u).at[:, 1, :, 1 - at.col], at.x_dev
        return remote(src, first_in.at[i, half], s1.at[i, half], r1.at[i, half], device)

    def second(u, half):
        i = u % RING
        if half == 0:
            src, device = mine(u).at[:, 0, at.row, 1 - at.col], at.x_dev
        else:
            src, device = mine(u).at[:, 1, 1 - at.row, at.col], at.y_dev
        return remote(src, second_in.at[i, half], s2.at[i, half], r2.at[i, half], device)

    def line_copy(u, k):
        line = at.other_line(k)
        src = mine(u).at[line // 2, line % 2, at.row, at.col]
        return remote(src, line_in.at[u, at.line], zs.at[u, k], zr.at[u, at.line], at.line_dev(k))

    def line_arrival(u, k):
        line = at.other_line(k)
        src = mine(u).at[line // 2, line % 2, at.row, at.col]
        return remote(src, line_in.at[u, line], zs.at[u, k], zr.at[u, line], at.line_dev(k))

    def give(semaphore, device):
        pl.semaphore_signal(semaphore, inc=1, device_id=device, device_id_type=MESH)

    def add(dst, src):
        dst[...] = (dst[...].astype(F32) + src[...].astype(F32)).astype(BF16)

    def start_first(u):
        cross(u).wait_recv()
        for half in (0, 1):
            for i in range(pairs):
                for g in range(4):
                    add(
                        mine(u).at[i, half, g // 2, g % 2],
                        cross_in.at[u % RING, i, half, g // 2, g % 2],
                    )
            pl.when(u >= RING)(lambda half=half: pl.semaphore_wait(free_first.at[half], 1))
            first(u, half).start()
        cross(u).wait_send()
        pl.when(u + RING < chunks)(lambda: give(free_cross, at.core_dev))

    def start_second(u):
        for half in (0, 1):
            first(u, half).wait_recv()
            for i in range(pairs):
                for j in (0, 1):
                    row, col = (at.row, j) if half == 0 else (j, at.col)
                    add(mine(u).at[i, half, row, col], first_in.at[u % RING, half, i, j])
            pl.when(u >= RING)(lambda half=half: pl.semaphore_wait(free_second.at[half], 1))
            second(u, half).start()
            first(u, half).wait_send()
            device = at.y_dev if half == 0 else at.x_dev
            pl.when(u + RING < chunks)(
                lambda half=half, device=device: give(free_first.at[half], device)
            )

    def start_lines(u):
        for half in (0, 1):
            second(u, half).wait_recv()
            for i in range(pairs):
                add(mine(u).at[i, half, at.row, at.col], second_in.at[u % RING, half, i])
            second(u, half).wait_send()
            device = at.x_dev if half == 0 else at.y_dev
            pl.when(u + RING < chunks)(
                lambda half=half, device=device: give(free_second.at[half], device)
            )
        for k in range(1, lines):
            line_copy(u, k).start()

    def finish(u):
        total = mine(u)[at.line // 2, at.line % 2, at.row, at.col].astype(F32)
        for k in range(1, lines):
            line_arrival(u, k).wait_recv()
            total = total + line_in[u, at.other_line(k)].astype(F32)
        rows = pl.ds(pl.multiple_of(u % 2 * half_rows, half_rows), half_rows)
        out[u // 2, rows, :] = total.astype(BF16)
        for k in range(1, lines):
            line_copy(u, k).wait_send()

    def turn(left, first_row):
        turned = left[...].astype(BF16).T
        count = left.shape[0]
        turned = turned.reshape(2 * pairs, 2, 2, half_rows, count)
        lhs_t[:, :, :, :, pl.ds(first_row, count)] = turned

    def produce(u, *terms):
        def columns(j, carry):
            col = pl.ds(pl.multiple_of(j * wide, wide), wide)
            total = None
            for first_row, right in terms:
                count = right.shape[0]
                left = lhs_t[:, :, u % 2, :, pl.ds(first_row, count)].reshape(D // 2, count)
                term = matmul(left, right[:, col])
                total = term if total is None else total + term
            total = total.reshape(pairs, 2, 2, half_rows, wide)
            held[u % HELD, :, :, :, j // 2, j % 2] = total.astype(BF16)
            return carry

        lax.fori_loop(0, 4, columns, 0)
        pl.when(u >= RING)(lambda: pl.semaphore_wait(free_cross, 1))
        cross(u).start()

    def left_load(p, src):
        units = pl.ds(pl.multiple_of(p % RATIO * D, D), D)
        return pltpu.make_async_copy(src.at[:, units], opnd.at[token_rows(2 + p % 2), :], lsem.at[p % 2])

    def left_start(p):
        pl.when(p < RATIO)(lambda: left_load(p, z_hbm).start())
        pl.when(p >= RATIO)(lambda: left_load(p, df_hbm).start())

    early = [
        (dy_hbm, opnd.at[token_rows(0), :]), (b_hbm, opnd.at[token_rows(1), :]), (h_hbm, h),
        (db_hbm, db), (o_hbm, o), (q_hbm, q), (c_hbm, c_win), (a3_hbm, a3),
    ]

    def early_load(i):
        return pltpu.make_async_copy(early[i][0], early[i][1], osem.at[i])

    def late_load(i):
        src, dst = ((a_hbm, opnd), (tok_hbm, dhb), (h, in_grad_out))[i]
        return pltpu.make_async_copy(src, dst, osem.at[len(early) + i])

    def head_loads(i):
        col = pl.ds(pl.multiple_of(i * HEAD_DIM, HEAD_DIM), HEAD_DIM)
        refs = [(kr_hbm, kr), (vr_hbm, vr), (kc_hbm, kc), (vc_hbm, vc)]
        return [
            pltpu.make_async_copy(src.at[:, col], dst, hsem.at[j])
            for j, (src, dst) in enumerate(refs)
        ]

    def weight_load(panel, slot):
        return pltpu.make_async_copy(full_ref.at[panel], wbuf.at[slot], wsem.at[slot])

    def weight(slot):
        return wbuf[slot].reshape(D, D)

    other = seq + 1 - 2 * at.core

    def comp_rows(owner):
        place = jnp.clip(owner - comp_window_first(seq, tok_dev), 0, comp_devs - 1)
        return pair.at[pl.ds(pl.multiple_of(place * comp_dev, comp_dev), comp_dev), :]

    def dc_across(d):
        i = (d + 1) // 2 - at.core
        return remote(comp_rows(seq - d), dc_beside.at[i], dbs.at[d // 2], dbr.at[i], at.core_dev)

    def dc_join(d):
        i = d // 2

        @pl.when(needs_comp(other, seq - d, tok_dev))
        def _():
            remote(comp_rows(seq - d), dc_beside.at[i], dbs.at[0], dbr.at[i], at.core_dev).wait_recv()
            add(comp_rows(seq - d), dc_beside.at[i])

    def gives_back(d):
        return chain_needs_comp(seq, seq - d, tok_dev, seq_count, reach - 1)

    def takes_back(d):
        return chain_needs_comp(seq + 2, seq - d, tok_dev, seq_count, reach - 1)

    def dc_back(d):
        i = d // 2 - 1
        return remote(comp_rows(seq - d), dc_chain.at[i], dcs.at[i], dcr.at[i], at.seq_dev(-2))

    def dc_arrival(d):
        i = d // 2
        return remote(comp_rows(seq), dc_chain.at[i], dcs.at[0], dcr.at[i], at.seq_dev(-2))

    def pass_back(d):
        @pl.when((d + 2 < reach) & takes_back(d))
        def _():
            dc_arrival(d).wait_recv()
            add(comp_rows(seq - d), dc_chain.at[d // 2])

        pl.when(gives_back(d))(lambda: dc_back(d).start())

    chain = [d for d in range(2, reach + 1, 2)]
    odds = [d for d in range(1, reach + 1, 2)]

    odd = at.core == 1
    even = at.core == 0

    def raw_rows(d):
        return dkr.at[token_rows(raw_devs - 1 - d), :]

    def da_copy(d, i, place, device):
        return remote(raw_rows(d), da_in.at[place], das.at[i], dar.at[place], device)

    def da_join(d):
        return da_copy(d, 0, 0, at.core_dev)

    def da_beside():
        return da_copy(1, 1, 1, at.core_dev)

    def da_back():
        return da_copy(2, 2, 2, at.seq_dev(-2))

    joins_near = even & needs_raw(seq, seq - 1, tok_dev)
    joins_far = odd & needs_raw(seq, seq - 3, tok_dev)
    joined = needs_raw(other, seq - 2, tok_dev)
    gives_beside = odd & needs_raw(seq, seq - 1, tok_dev)
    takes_beside = even & needs_raw(seq + 1, seq, tok_dev)
    gives_raw = needs_raw(seq, seq - 2, tok_dev)
    takes_raw = (seq + 2 < seq_count) & needs_raw(seq + 2, seq, tok_dev)

    def share(i):
        total = times_transposed(dkr[token_rows(i), :], weight(1))
        return total + times_transposed(dvr[token_rows(i), :], weight(2))

    def norm_copy(i):
        device = (at.core_dev, at.x_dev, at.y_dev)[i]
        return remote(n_src.at[i], n_in.at[i], ns.at[i], nr.at[i], device)

    def norm_next(i):
        norm_copy(i).wait_recv()
        n_src[i + 1] = n_src[i] + n_in[i]

    def norm_line(k):
        return remote(n_src.at[3], n_line.at[at.line], nzs.at[k], nzr.at[at.line], at.line_dev(k))

    def norm_line_arrival(k):
        line = at.other_line(k)
        return remote(n_src.at[3], n_line.at[line], nzs.at[k], nzr.at[line], at.line_dev(k))

    def second_norm_back():
        gains, shifts = [], []
        for i in range(tok_dev // QB):
            rows = pl.ds(i * QB, QB)
            back, gain, shift = norm_back(db[rows, :], h[rows, :], params, 2)
            db[rows, :] = opnd[rows, :].astype(F32) + back
            dhb[rows, :] = db[rows, :].astype(BF16)
            gains.append(gain)
            shifts.append(shift)
        n_src[0, 2:3, :] = sum(gains)
        n_src[0, 3:4, :] = sum(shifts)
        do[...] = times_transposed(dhb[...], weight(0)).astype(BF16)

    def first_norm_back():
        gains, shifts = [], []
        for i in range(tok_dev // QB):
            rows = pl.ds(i * QB, QB)
            back, gain, shift = norm_back(h[rows, :], dhb[rows, :].astype(F32), params, 0)
            h[rows, :] = db[rows, :] + back
            gains.append(gain)
            shifts.append(shift)
        n_src[0, 0:1, :] = sum(gains)
        n_src[0, 1:2, :] = sum(shifts)

    def work(t):
        @pl.when(t == 1)
        def _():
            for i in range(2, 6):
                early_load(i).wait()
            weight_load(6, 0).wait()
            second_norm_back()
            weight_load(3, 0).start()

        @pl.when((t >= 3) & (t < 3 + 2 * HEADS) & (t % 2 == 1))
        def _():
            head = (t - 3) // 2
            for copy in head_loads(head):
                copy.wait()
            cols = pl.ds(pl.multiple_of(head * HEAD_DIM, HEAD_DIM), HEAD_DIM)
            attend_head_back(
                seq, tok_dev, cols, q, do, o, kr, vr, kc, vc, lse_ref, head, dkr, dvr, dkc, dvc,
                acc_kr, acc_vr, acc_kc, acc_vc,
            )

            @pl.when(head + 1 < HEADS)
            def _():
                for copy in head_loads(head + 1):
                    copy.start()

        @pl.when(t == 18)
        def _():
            weight_load(4, 1).wait()
            weight_load(5, 2).wait()
            half = comp // 2
            for i in range(2):
                rows = pl.ds(i * half, half)
                total = times_transposed(dkc[rows, :], weight(1))
                total = total + times_transposed(dvc[rows, :], weight(2))
                pair[rows, :] = total.astype(BF16)
            for d in odds:
                pl.when(needs_comp(seq, seq - d, tok_dev))(lambda d=d: dc_across(d).start())

        @pl.when(t == 19)
        def _():
            for d in chain:
                dc_join(d)

        for i, d in enumerate(reversed(chain)):
            pl.when(t == 19 + i)(lambda d=d: pass_back(d))

        @pl.when(t == 20)
        def _():
            weight_load(3, 0).wait()
            h[...] = times_transposed(q[...], weight(0))
            weight_load(0, 0).start()

        @pl.when(t == 22)
        def _():
            raw_rows(1)[...] = share(raw_devs - 2).astype(BF16)
            pl.when(joins_near)(lambda: da_join(1).start())
            pl.when(gives_beside)(lambda: da_beside().start())

            @pl.when(joins_far)
            def _():
                raw_rows(3)[...] = share(raw_devs - 4).astype(BF16)
                da_join(3).start()

        @pl.when(t == 23)
        def _():
            raw_rows(2)[...] = share(raw_devs - 3).astype(BF16)
            h[...] += share(raw_devs - 1)
            weight_load(1, 1).start()
            weight_load(2, 2).start()
            taken = takes_back(0)

            @pl.when(taken)
            def _():
                dc_arrival(0).wait_recv()
                dc[...] = dc_chain[0]

            @pl.when(jnp.logical_not(taken))
            def _():
                dc[...] = jnp.zeros_like(dc)

        @pl.when(t == 25)
        def _():
            @pl.when(joined)
            def _():
                da_join(2).wait_recv()
                add(raw_rows(2), da_in.at[0])

            pl.when(gives_raw)(lambda: da_back().start())

        @pl.when(t == 26)
        def _():
            for panel in range(3):
                weight_load(panel, panel).wait()
            heads_of = acc_kr.shape[0] // tok_dev
            for k in range(3):
                total = times_transposed(dc[...], weight(k))
                for c in range(HEADS):
                    acc = (acc_kr, acc_vr)[c // heads_of]
                    place = pl.ds(c % heads_of * tok_dev + k, comp_dev, stride=3)
                    acc[place, :] = total[:, c * HEAD_DIM : (c + 1) * HEAD_DIM]
            for c in range(HEADS):
                acc = (acc_kr, acc_vr)[c // heads_of]
                cols = pl.ds(c * HEAD_DIM, HEAD_DIM)
                h[:, cols] += acc[pl.ds(c % heads_of * tok_dev, tok_dev), :]
            for d in odds:
                pl.when(needs_comp(seq, seq - d, tok_dev))(lambda d=d: dc_across(d).wait_send())
            for d in chain:
                pl.when(gives_back(d))(lambda d=d: dc_back(d).wait_send())
            late_load(1).start()

        @pl.when(t == 28)
        def _():
            @pl.when(takes_raw)
            def _():
                da_back().wait_recv()
                h[...] += da_in[2].astype(F32)

            @pl.when(takes_beside)
            def _():
                da_beside().wait_recv()
                h[...] += da_in[1].astype(F32)

            pl.when(joins_near)(lambda: da_join(1).wait_send())
            pl.when(joins_far)(lambda: da_join(3).wait_send())
            pl.when(gives_beside)(lambda: da_beside().wait_send())
            pl.when(gives_raw)(lambda: da_back().wait_send())
            late_load(1).wait()
            first_norm_back()
            norm_copy(0).start()
            late_load(2).start()

        for i in range(2):

            @pl.when(t == 29 + i)
            def _(i=i):
                norm_next(i)
                norm_copy(i + 1).start()

        @pl.when(t == 31)
        def _():
            norm_next(2)
            n_line[at.line] = n_src[3]
            for k in range(1, lines):
                norm_line(k).start()

    def make(t):
        @pl.when(t < 4 * RATIO)
        def _():
            p = t // 2

            @pl.when(t % 2 == 0)
            def _():
                pl.when(p + 1 < 2 * RATIO)(lambda: left_start(p + 1))
                left_load(p, z_hbm).wait()
                pl.when(p == 0)(lambda: early_load(0).wait())
                pl.when(p == RATIO)(lambda: early_load(1).wait())
                turn(opnd.at[token_rows(2 + p % 2), :], 0)

            produce(t, (0, opnd.at[token_rows(p // RATIO), :]))
            pl.when(t == 4 * RATIO - 1)(lambda: late_load(0).start())

        base = 4 * RATIO
        pl.when(t == base)(lambda: turn(o, 0))
        pl.when(t // 2 == base // 2)(lambda: produce(t, (0, dhb)))

        @pl.when(t == base + 2)
        def _():
            late_load(0).wait()
            early_load(6).wait()
            early_load(7).wait()
            turn(opnd.at[token_rows(raw_devs - 1), :], raw - tok_dev)

        pl.when(t // 2 == base // 2 + 1)(lambda: produce(t, (raw - tok_dev, q)))

        @pl.when(t == base + 3)
        def _():
            for i in range(raw_devs - 1):
                turn(opnd.at[token_rows(i), :], i * tok_dev)
            for i in range(comp // tok_dev):
                turn(c_win.at[token_rows(i), :], raw + i * tok_dev)

        pl.when(t // 2 == base // 2 + 2)(lambda: produce(t, (0, dkr), (raw, dkc)))
        pl.when(t // 2 == base // 2 + 3)(lambda: produce(t, (0, dvr), (raw, dvc)))
        for k in range(3):
            pl.when(t == base + 8 + 2 * k)(lambda k=k: turn(a3.at[k], 0))
        pl.when((t >= base + 8) & (t < base + 14))(lambda: produce(t, (0, dc)))

    at.announce()
    for i in range(len(early)):
        early_load(i).start()
    left_load(0, z_hbm).start()
    for panel, slot in ((6, 0), (4, 1), (5, 2)):
        weight_load(panel, slot).start()
    for copy in head_loads(0):
        copy.start()
    at.enter()

    def step(t, carry):
        pl.when((t >= 1) & (t < chunks + 1))(lambda: start_first(t - 1))
        pl.when((t >= 2) & (t < chunks + 2))(lambda: start_second(t - 2))
        pl.when((t >= 3) & (t < chunks + 3))(lambda: start_lines(t - 3))
        pl.when(t >= BACK_LAG)(lambda: finish(t - BACK_LAG))
        pl.when(t < chunks)(lambda: make(t))
        work(t)
        return carry

    lax.fori_loop(0, chunks + BACK_LAG, step, 0)
    count = slot_out.shape[0]
    for j in range(4 * count):
        slots[j] = (out[place_ref[j]].astype(F32) * slot_scale_ref[j]).astype(BF16)
    handed = at.exchange(slots, slots_in, es, er)
    for copy in handed:
        copy.start()
    slots_in[pl.ds(at.grp * count, count)] = slots[pl.ds(at.grp * count, count)]
    for i in range(3):
        norm_copy(i).wait_send()
    for k in range(1, lines):
        norm_line_arrival(k).wait_recv()
        norm_line(k).wait_send()
    total = n_line[0]
    for i in range(1, lines):
        total = total + n_line[i]
    norm_out[...] = total
    late_load(2).wait()
    for copy in handed:
        copy.wait_send()
        copy.wait_recv()
    for g in range(4):
        for j in range(count):
            slot_out[j, :, pl.ds(g * wide, wide)] = slots_in[g * count + j]


def backward(place, slot_scale, weights, arrays, lse, norm_params, lines):
    panels, rows = weights.shape[0], weights.shape[4]
    wide, pairs, half_rows = D // 4, lines // 2, weights.shape[4] // 2
    a_win, c_win = arrays[0], arrays[1]
    tok_dev = arrays[3].shape[0]
    raw, comp, comp_dev = a_win.shape[0], c_win.shape[0], tok_dev // 3
    raw_devs, all_slots = raw // tok_dev, place.shape[0]
    reach = min(2 * lines - 1, (2 * S + 3 * CM + tok_dev - 1) // tok_dev)
    dma = pltpu.SemaphoreType.DMA
    regular = pltpu.SemaphoreType.REGULAR
    any_spec, vmem = pl.BlockSpec(memory_space=pl.ANY), pl.BlockSpec(memory_space=pltpu.VMEM)
    smem = pl.BlockSpec(memory_space=pltpu.SMEM)

    def buffer(kind, *shape):
        return pltpu.VMEM(shape, kind)

    return pl.pallas_call(
        functools.partial(backward_kernel, panels, lines),
        out_shape=[
            jax.ShapeDtypeStruct((all_slots // 4, rows, D), BF16),
            jax.ShapeDtypeStruct((tok_dev, D), F32),
            jax.ShapeDtypeStruct((4, D), F32),
        ],
        in_specs=[smem] * 2 + [any_spec] * (1 + len(arrays)) + [vmem] * 2,
        out_specs=[vmem, any_spec, vmem],
        scratch_shapes=[
            buffer(BF16, HELD, pairs, 2, 2, 2, 2, half_rows, wide),
            buffer(BF16, RING, pairs, 2, 2, 2, half_rows, wide),
            buffer(BF16, RING, 2, pairs, 2, half_rows, wide),
            buffer(BF16, RING, 2, pairs, half_rows, wide),
            buffer(BF16, 2 * panels, lines, half_rows, wide),
            buffer(BF16, panels, rows, wide),
            buffer(BF16, all_slots, rows, wide),
            buffer(BF16, all_slots, rows, wide),
            buffer(BF16, raw, D),
            buffer(BF16, 2 * pairs, 2, 2, half_rows, raw + comp),
            buffer(BF16, comp, D),
            buffer(BF16, 3, comp_dev, D),
            buffer(F32, tok_dev, D),
            buffer(F32, tok_dev, D),
            buffer(F32, tok_dev, D),
            buffer(BF16, max(comp, 2 * tok_dev), D),
            buffer(BF16, tok_dev, D),
            buffer(BF16, raw, HEAD_DIM),
            buffer(BF16, raw, HEAD_DIM),
            buffer(BF16, comp, HEAD_DIM),
            buffer(BF16, comp, HEAD_DIM),
            buffer(F32, raw, HEAD_DIM),
            buffer(F32, raw, HEAD_DIM),
            buffer(F32, comp, HEAD_DIM),
            buffer(F32, comp, HEAD_DIM),
            buffer(BF16, raw, D),
            buffer(BF16, raw, D),
            buffer(BF16, comp, D),
            buffer(BF16, comp, D),
            buffer(BF16, 3, pairs, 2, 2, rows, D),
            buffer(BF16, comp_dev, D),
            buffer(BF16, reach // 2 + 2, comp_dev, D),
            buffer(BF16, reach // 2 + 1, comp_dev, D),
            buffer(BF16, 3, tok_dev, D),
            buffer(F32, 4, 4, D),
            buffer(F32, 3, 4, D),
            buffer(F32, lines, 4, D),
            dma((RING,)), dma((RING,)),
            dma((RING, 2)), dma((RING, 2)),
            dma((RING, 2)), dma((RING, 2)),
            dma((2 * panels, lines)), dma((2 * panels, lines)),
            regular, regular((2,)), regular((2,)),
            dma((2,)), dma((11,)), dma((4,)), dma((3,)),
            dma((reach // 2 + 2,)), dma((reach // 2 + 2,)),
            dma((reach // 2 + 1,)), dma((reach // 2 + 1,)),
            dma((3,)), dma((3,)),
            dma((3,)), dma((3,)),
            dma((lines,)), dma((lines,)),
            dma((3,)), dma((3,)),
        ],
        compiler_params=pltpu.CompilerParams(
            collective_id=1, has_side_effects=True, vmem_limit_bytes=62 * MIB
        ),
        name="backward",
    )(place, slot_scale, weights, *arrays, lse, norm_params)


def local(
    tokens, cotangent, master, first_moment, second_moment, norm_params, norm_first, norm_second,
    seg_valid, book_of_group, panel_slot,
):
    seq_count = lax.axis_size("seq")
    group_count = lax.axis_size("grp")
    seq_index = lax.axis_index("seq")
    group_index = lax.axis_index("grp")
    lines = seq_count // 2
    tok_dev = tokens.shape[0]
    slot_count, slot_rows = master.shape[0], master.shape[1]
    all_slots = slot_count * group_count
    comp_dev = tok_dev // 3
    wide = D // group_count

    slot_ids = jnp.arange(all_slots, dtype=jnp.int32)
    is_panel = panel_slot[None, :] == slot_ids[:, None]
    slot_used = jnp.any(is_panel, 1)
    slot_panel = jnp.argmax(is_panel, 1).astype(jnp.int32)
    scale_all = jnp.sum(jnp.where(is_panel, panel_deviations()[None, :], 0.0), 1)
    slot_scale = lax.dynamic_slice_in_dim(scale_all, group_index * slot_count, slot_count, 0)
    order = panel_slot[jnp.array(ARRIVAL)]

    positions = seq_index * tok_dev + jnp.arange(tok_dev, dtype=jnp.int32)
    book_id = jnp.sum(jnp.where(jnp.arange(group_count) == group_index, book_of_group, 0))
    book_counts = jnp.sum(jnp.where((jnp.arange(group_count) == book_id)[:, None], seg_valid, 0), 0)
    segments = seg_valid.shape[1]
    row_counts = jnp.sum(
        jnp.where((positions // S)[:, None] == jnp.arange(segments)[None, :], book_counts[None, :], 0), 1
    )
    row_valid = (positions % S < row_counts).astype(F32)

    tokens3 = tokens.reshape(comp_dev, 3, D).transpose(1, 0, 2)
    grad_out = (cotangent.astype(F32) * row_valid[:, None]).astype(BF16)
    results = forward(
        slot_scale, order, master, tokens, tokens3, grad_out, row_valid[:, None], norm_params, lines
    )
    weights, saved, log_total, mixed = results[0], results[1:-2], results[-2], results[-1]
    a_win, c_win, q, kr, vr, kc, vc, o, z, df, b, h, db, a3 = saved
    arrays = (a_win, c_win, a3, q, kr, vr, kc, vc, o, z, df, b, h, db, grad_out, tokens)
    place = jnp.argsort(jnp.array(RETURN, jnp.int32))[slot_panel]
    slot_scales = jnp.where(slot_used, scale_all, 0.0)
    slot_sums, input_grad, norm_grad = backward(
        place.astype(jnp.int32), slot_scales, weights, arrays, log_total, norm_params, lines
    )
    slot_grad = slot_sums.astype(F32)
    slot_first, slot_second, slot_weight = adam_update(
        slot_grad, first_moment, second_moment, master, SLOT_RATE
    )
    norm_first_new, norm_second_all, norm_weight = adam_update(
        norm_grad, norm_first, norm_second, norm_params, NORM_RATE
    )
    return (
        mixed, input_grad, slot_grad, slot_first, slot_second, slot_weight, norm_grad,
        norm_first_new, norm_second_all[:2], norm_second_all[2:], norm_weight,
    )


def solution(mesh):
    rows, slots, whole = P(("grp", "seq"), None), P("grp", "seq", None), P()
    return jax.shard_map(
        local,
        mesh=mesh,
        in_specs=(rows, rows, slots, slots, slots) + (whole,) * 6,
        out_specs=(rows, rows, slots, slots, slots, slots) + (whole,) * 5,
        check_vma=False,
    )
```

time: 566 us -> 449 us (0.79); the launches traced: 561 us -> 451 us
  Pallas kernels: 489 us -> 421 us
  waiting for transfers between devices: 29.8 us -> 0 us
  local copies, waits for them, and re-layouts: 20.1 us -> 9.4 us
  starting transfers between devices: 8.86 us -> 0 us
  other arithmetic: 11.7 us -> 19.1 us
    pallas_call x1, Pallas kernels: 272 us -> 230 us  [backward(): pl.pallas_call(functools.partial(backward_kernel, panels, lines), out_sha...]
    all_to_all x2 -> x0, waiting for transfers between devices: 29.8 us -> none  [the longest x1 17.4 us: local(): slot_parts = lax.all_to_all(slotted, 'grp', 0, 0, tiled=True)]
    pallas_call x1, Pallas kernels: 218 us -> 191 us  [forward(): pl.pallas_call(functools.partial(forward_kernel, panels, lines), out_shap...]
    all_to_all x2 -> x0, starting transfers between devices: 8.86 us -> none  [the longest x1 5.29 us: local(): slots_in = lax.all_to_all(scaled, 'grp', 0, 0, tiled=True)]
    unnamed x40 -> x17, local copies, waits for them, and re-layouts: 9.28 us -> 2.67 us
  transfers between devices with their start and end apart: 2 -> 0, of which waited for: 2 -> 0; matrix products, arithmetic and copies ran while one was open for 2% -> 0% of each run, Pallas kernels for 0% -> 0%
where the time goes in v4:
time: 449 us; the launch traced here: 451 us
  Pallas kernels  421 us (94%)
  other arithmetic  19.1 us (4%)
  local copies, waits for them, and re-layouts  9.4 us (2%)
    pallas_call x1, Pallas kernels, backward(): pl.pallas_call(functools.partial(backward_kernel, panels, lines), out_sha...  230 us
    pallas_call x1, Pallas kernels, forward(): pl.pallas_call(functools.partial(forward_kernel, panels, lines), out_shap...  191 us
    sub x2, other arithmetic, adam_update(): weight_old - step_rate * (movement + WEIGHT_DECAY * weight_old)  9.34 us

profile of v4, /device:TPU:0, one launch (start us, length us, event | category | flops | bytes accessed | tf_op | source)
XLA Modules:
  0.0 450.6 jit_solution(10527005265016671634)
XLA Ops:
  0.7 1.4 fusion.10
  2.0 0.6 iota_compare_fusion.2
  2.7 0.8 select_reduce_fusion.2
  3.5 0.8 select_reduce_fusion.1
  4.2 0.6 dynamic_slice.3.scale_ref
  4.8 0.7 fusion.2
  5.5 0.5 broadcast_select_fusion.slot_scale_ref
  6.1 1.3 iota_reduce_fusion
  7.5 1.9 gather_fusion.1
  9.3 0.7 pad_clamp_fusion.1
  10.0 1.8 gather_fusion
  11.8 0.2 copy.30
  12.0 0.7 convert_element_type.25.valid_ref
  12.7 2.2 multiply_convert_fusion.dy_ref.dy_hbm
  14.9 0.5 reshape.100
  15.4 1.2 copy.32
  16.6 190.9 %forward.1 = (bf16[15,2,2,2,128,1024]{5,4,3,2,1,0:T(8,128)(2,1)}, bf16[1536,1024]{1,0:T(8,128)(2,1)}, bf16[768,1024]{1,0:T(8,128)(2,1)}, bf16[384,1024]{1,0:T(8,...) custom-call(f32[6]{0:T(128)} %dynamic_slice.3.scale_ref, ...), custom_call_target="tpu_custom_call" | custom-call | tf_op jit(solution)/shard_map/forward/pallas_call | solution.py:671
  207.5 230.2 %backward.1 = (bf16[6,128,1024]{2,1,0:T(8,128)(2,1)}, f32[384,1024]{1,0:T(8,128)}, f32[4,1024]{1,0:T(4,128)}) custom-call(s32[24]{0:T(128)} %gather_fusion.1, f32[24]{0:T(128)} %broadcast_select_fusion.slot_scale_ref, bf16[15,2,2,2,128,1024]{5,4,3,2,1,0:T(8,128)(2,1)} %get-tuple-element.36.full_ref, bf16[1536,1024]{1,0:T(8,128)(2,1)} %get-tuple-element.37.a_hbm, ...), custom_call_target="tpu_custom_call" | custom-call | tf_op jit(solution)/shard_map/backward/pallas_call | solution.py:1293
  437.8 1.4 add_subtract_fusion
  439.2 0.6 fusion.13
  439.8 8.0 %multiply_subtract_fusion = (f32[6,128,1024]{2,1,0:T(8,128)}, f32[6,128,1024]{2,1,0:T(8,128)}, f32[6,128,1024]{2,1,0:T(8,128)}, f32[6,128,1024]{2,1,0:T(8,128)}) fusion(f32[6,128,1024]{2,1,0:T(8,128)} %master_ref.1, f32[6,128,1024]{2,1,0:T(8,128)} %param.18, f32[6,128,1024]{2,1,0:T(8,128)} %param.17, bf16[6,128,1024]{2,1,0:T(8,128)(2,1)} %get-tuple-element.53), kind=kLoop, calls=%fused_computation.4 | loop fusion | flops 12582912 | bytes 23592960 | tf_op jit(solution)/shard_map/sub | solution.py:57
  447.8 0.9 copy.36
  448.6 1.1 copy.37
  449.8 0.6 copy.38
  (20 shorter events, 0.2 us)
Async XLA Ops:
  0.6 14.3 %copy-start = (bf16[384,1024]{1,0:T(8,128)(2,1)S(1)}, bf16[384,1024]{1,0:T(8,128)(2,1)}, u32[]{:S(2)}) copy-start(bf16[384,1024]{1,0:T(8,128)(2,1)} %tok_hbm.1) | copy-start | bytes 2359300
  207.5 230.3 %copy-start.3 = (f32[4,1024]{1,0:T(4,128)S(1)}, f32[4,1024]{1,0:T(4,128)}, u32[]{:S(2)}) copy-start(f32[4,1024]{1,0:T(4,128)} %norm_ref.3) | copy-start | bytes 49156
  207.5 230.3 %copy-start.5 = (f32[4,1024]{1,0:T(4,128)S(1)}, f32[4,1024]{1,0:T(4,128)}, u32[]{:S(2)}) copy-start(f32[4,1024]{1,0:T(4,128)} %param.21) | copy-start | bytes 49156
  207.5 230.3 %copy-start.6 = (f32[4,1024]{1,0:T(4,128)S(1)}, f32[4,1024]{1,0:T(4,128)}, u32[]{:S(2)}) copy-start(f32[4,1024]{1,0:T(4,128)} %param.20) | copy-start | bytes 49156
  439.8 8.0 %copy-start.2 = (bf16[384,1024]{1,0:T(8,128)(2,1)S(1)}, bf16[384,1024]{1,0:T(8,128)(2,1)}, u32[]{:S(2)}) copy-start(bf16[384,1024]{1,0:T(8,128)(2,1)} %get-tuple-element.75) | copy-start | bytes 2359300
  439.8 8.9 %copy-start.1 = (f32[384,1024]{1,0:T(8,128)S(1)}, f32[384,1024]{1,0:T(8,128)}, u32[]{:S(2)}) copy-start(f32[384,1024]{1,0:T(8,128)} %get-tuple-element.76) | copy-start | bytes 4718596
  447.7 2.0 copy-start.4
